TPU v7x, 32 devices: a whole 2x2x4 slice. The times are simulated.
32 devices in a mesh: dp: 8 (over z, core), fsdp: 4 (over y, x).
Axes of the slice: x: 2, y: 2, z: 4, core: 2. Of those that a mesh axis runs over, the one named last changes fastest.
Arguments:
- inputs: bfloat16 [8, 2, 1024, 2048], P('dp', None, 'fsdp'), may hold values from -6 to 6
- cotangent: bfloat16 [8, 2, 1024, 2048], P('dp', None, 'fsdp'), may hold values from -6 to 6
- lengths: int32 [8, 2], replicated, may hold values from 512 to 1024, as said below
- dealing: int32 [2, 8], replicated, may hold values from 0 to 7, as said below
- query_weight: bfloat16 [2048, 2048], P('dp', 'fsdp'), may hold values from -0.125 to 0.125
- key_weight: bfloat16 [2048, 512], P('dp', 'fsdp'), may hold values from -0.125 to 0.125
- value_weight: bfloat16 [2048, 512], P('dp', 'fsdp'), may hold values from -0.125 to 0.125
- output_weight: bfloat16 [2048, 2048], P('fsdp', 'dp'), may hold values from -0.375 to 0.375
- gate_weight: bfloat16 [2048, 8192], P('dp', 'fsdp'), may hold values from -0.125 to 0.125
- up_weight: bfloat16 [2048, 8192], P('dp', 'fsdp'), may hold values from -0.125 to 0.125
- down_weight: bfloat16 [8192, 2048], P('fsdp', 'dp'), may hold values from -0.0625 to 0.0625
- adapter_down_weights: bfloat16 [2048, 32], P(('dp', 'fsdp')), may hold values from -0.125 to 0.125
- adapter_up_query_output: bfloat16 [2048, 16], P(('dp', 'fsdp')), may hold values from -2 to 2
- adapter_up_key_value: bfloat16 [512, 16], P(('dp', 'fsdp')), may hold values from -2 to 2
- query_feature_weights: bfloat16 [2048, 64], P(('dp', 'fsdp')), may hold values from -0.75 to 0.75
- key_feature_weights: bfloat16 [512, 64], P(('dp', 'fsdp')), may hold values from -0.75 to 0.75
- norm_gain_weights: bfloat16 [2048, 2], P(('dp', 'fsdp')), may hold values from 0.5 to 1.5
Outputs:
- output: bfloat16 [8, 2, 1024, 2048], P('dp', None, 'fsdp')
- input_grad: bfloat16 [8, 2, 1024, 2048], P('dp', None, 'fsdp')
- lora_in_grad: float32 [2048, 32], P(('dp', 'fsdp'))
- lora_up_d_grad: float32 [2048, 16], P(('dp', 'fsdp'))
- lora_up_kv_grad: float32 [512, 16], P(('dp', 'fsdp'))
- fmap_q_grad: float32 [2048, 64], P(('dp', 'fsdp'))
- fmap_k_grad: float32 [512, 64], P(('dp', 'fsdp'))
- norm_gains_grad: float32 [2048, 2], P(('dp', 'fsdp'))
Inputs may be any that keep to these rules, and one draw needn't show every extreme that they name: Each row of dealing is a permutation of the groups. A sequence fills the first lengths[i, m] positions of its block; the rest is padding.
All inputs are finite; a program needn't handle non-finite values.
Results may differ from a plain program's by a relative error of at most 0.018.
Values may be sent and summed in bfloat16 or wider, within the bound.
No kernel may reach another device: no remote copies, remote signals or barrier semaphores. Data moves between devices by JAX's collectives and lax.ppermute only.
A program may use at most 896 MiB of HBM per device.

v0:
```python
import math

import jax
import jax.numpy as jnp
from jax import lax
from jax.sharding import PartitionSpec as P

H = 32
KEY_VALUE_HEADS = 8
HEAD_SIZE = 64
ADAPTER_RANK = 8
WIN = 64


EPSILON = 1e-05
ROPE_BASE = 500000.0
EXACT_PRECISION = lax.Precision.HIGHEST


def add_tuple(first_set, second_set):
    return tuple(
        (first_item + second_item for first_item, second_item in zip(first_set, second_set))
    )


def rope_tables(positions):
    half_size = HEAD_SIZE // 2
    frequencies = jnp.exp(
        -(2.0 * jnp.arange(half_size, dtype=jnp.float32) / HEAD_SIZE) * math.log(ROPE_BASE)
    )
    angles = positions.astype(jnp.float32)[:, None] * frequencies[None, :]
    return (jnp.cos(angles), jnp.sin(angles))


def rotate(heads, cosine, sine_part):
    half_size = heads.shape[-1] // 2
    front_half = heads[..., :half_size]
    back_half = heads[..., half_size:]
    cos_rows = cosine[:, None, :]
    sin_rows = sine_part[:, None, :]
    return jnp.concatenate(
        [
            front_half * cos_rows - back_half * sin_rows,
            back_half * cos_rows + front_half * sin_rows,
        ],
        axis=-1,
    )


def rotate_back(grads, cosine, sine_part):
    half_size = grads.shape[-1] // 2
    front_half = grads[..., :half_size]
    back_half = grads[..., half_size:]
    cos_rows = cosine[:, None, :]
    sin_rows = sine_part[:, None, :]
    return jnp.concatenate(
        [
            front_half * cos_rows + back_half * sin_rows,
            back_half * cos_rows - front_half * sin_rows,
        ],
        axis=-1,
    )


def rms_scale(value_rows):
    return lax.rsqrt(jnp.mean(value_rows * value_rows, axis=-1, keepdims=True) + EPSILON)


def attention_masks(query_pos, key_pos):
    distance = query_pos[:, None] - key_pos[None, :]
    key_valid = (key_pos >= 0)[None, :]
    window_mask = (distance >= 0) & (distance < WIN) & key_valid
    band_mask = (
        (key_pos[None, :] // WIN == query_pos[:, None] // WIN - 1) & (distance >= WIN) & key_valid
    )
    return (window_mask, band_mask)


def feature_map(rotated, weights):
    mapped = jnp.einsum("thd,hde->the", rotated, weights, preferred_element_type=jnp.float32)
    return (jax.nn.softmax(mapped, axis=-1), jax.nn.softmax(-mapped, axis=-1))


def feature_back(grad_feat, positive, negative):
    half_size = positive.shape[-1]
    grad_pos = grad_feat[..., :half_size]
    grad_neg = grad_feat[..., half_size:]
    return positive * (
        grad_pos - jnp.sum(positive * grad_pos, axis=-1, keepdims=True)
    ) - negative * (grad_neg - jnp.sum(negative * grad_neg, axis=-1, keepdims=True))


def fetch_small(local_adapter_weights):
    return (
        lax.all_gather(local_adapter_weights[0], ("dp", "fsdp"), axis=0, tiled=True),
        lax.all_gather(local_adapter_weights[1], ("dp", "fsdp"), axis=0, tiled=True),
        lax.all_gather(local_adapter_weights[2], ("dp", "fsdp"), axis=0, tiled=True),
        lax.all_gather(local_adapter_weights[3], ("dp", "fsdp"), axis=0, tiled=True),
        lax.all_gather(local_adapter_weights[4], ("dp", "fsdp"), axis=0, tiled=True),
        lax.all_gather(local_adapter_weights[5], ("dp", "fsdp"), axis=0, tiled=True),
    )


def fetch_rows(local_frozen):
    return (
        lax.all_gather(local_frozen[0], "dp", axis=0, tiled=True),
        lax.all_gather(local_frozen[1], "dp", axis=0, tiled=True),
        lax.all_gather(local_frozen[2], "dp", axis=0, tiled=True),
        lax.all_gather(local_frozen[3], "dp", axis=1, tiled=True),
        lax.all_gather(local_frozen[4], "dp", axis=0, tiled=True),
        lax.all_gather(local_frozen[5], "dp", axis=0, tiled=True),
        lax.all_gather(local_frozen[6], "dp", axis=1, tiled=True),
    )


def rows_in(local_rows):
    return lax.all_gather(local_rows, "fsdp", axis=0, tiled=True)


def rows_out_pair(wide_part, narrow_part):
    return (
        lax.psum_scatter(wide_part, "fsdp", scatter_dimension=0, tiled=True),
        lax.psum_scatter(narrow_part, "fsdp", scatter_dimension=0, tiled=True),
    )


def rows_out_one(wide_part):
    return lax.psum_scatter(
        wide_part.astype(jnp.bfloat16), "fsdp", scatter_dimension=0, tiled=True
    ).astype(jnp.float32)


def deal(block_rows, deal_table):
    groups = deal_table.shape[0]
    row_count = block_rows.shape[0]
    width = block_rows.shape[1]
    pieces = block_rows.reshape(groups, row_count // groups, width)
    spread = lax.all_to_all(pieces, "dp", split_axis=0, concat_axis=0, tiled=True)
    ordered = jnp.einsum(
        "ji,isw->jsw", deal_table, spread, preferred_element_type=jnp.float32
    ).astype(jnp.bfloat16)
    settled = lax.all_to_all(ordered, "dp", split_axis=0, concat_axis=0, tiled=True)
    return settled.reshape(row_count, width)


def attend(
    q_rot,
    key_extended,
    value_extended,
    q_feat,
    key_feature_extended,
    states,
    norm_states,
    query_pos,
    key_pos,
):
    row_count = q_rot.shape[0]
    kv_count = key_extended.shape[1]
    head_count = q_feat.shape[1]
    repeat = head_count // kv_count
    span_count = row_count // WIN
    window_mask, band_mask = attention_masks(query_pos, key_pos)
    grouped_heads = q_rot.reshape(row_count, kv_count, repeat, HEAD_SIZE)
    grouped_features = q_feat.reshape(row_count, kv_count, repeat, 2 * HEAD_SIZE)
    score_matrix = jnp.einsum(
        "yzpo,nzo->zpyn", grouped_heads, key_extended, preferred_element_type=jnp.float32
    ) / math.sqrt(HEAD_SIZE)
    linear_attention = jnp.einsum(
        "zbpj,qbj->bpzq", grouped_features, key_feature_extended, preferred_element_type=jnp.float32
    )
    weight_matrix = jnp.where(window_mask, jnp.exp(score_matrix), 0.0) + jnp.where(
        band_mask, linear_attention, 0.0
    )
    feat_spans = grouped_features.astype(jnp.float32).reshape(
        span_count, WIN, kv_count, repeat, 2 * HEAD_SIZE
    )
    state_numerator = jnp.einsum(
        "cwgrf,cgfd->cwgrd", feat_spans, states, precision=EXACT_PRECISION
    ).reshape(row_count, kv_count, repeat, HEAD_SIZE)
    state_den = jnp.einsum(
        "cwgrf,cgf->grcw", feat_spans, norm_states, precision=EXACT_PRECISION
    ).reshape(kv_count, repeat, row_count)
    softmax_divisor = jnp.sum(weight_matrix, axis=-1) + state_den
    rank_weights = (weight_matrix / softmax_divisor[..., None]).astype(jnp.bfloat16)
    state_output = state_numerator / jnp.transpose(softmax_divisor, (2, 0, 1))[..., None]
    combined_heads = (
        jnp.einsum(
            "qxlm,mqo->lqxo", rank_weights, value_extended, preferred_element_type=jnp.float32
        )
        + state_output
    )
    return (
        combined_heads.reshape(row_count, head_count * HEAD_SIZE),
        softmax_divisor,
        state_output,
    )


def attend_back(
    grad_out,
    q_rot,
    key_extended,
    value_extended,
    q_feat,
    key_feature_extended,
    states,
    norm_states,
    softmax_divisor,
    state_output,
    query_pos,
    key_pos,
):
    row_count = q_rot.shape[0]
    kv_count = key_extended.shape[1]
    head_count = q_feat.shape[1]
    repeat = head_count // kv_count
    span_count = row_count // WIN
    window_mask, band_mask = attention_masks(query_pos, key_pos)
    grouped_heads = q_rot.reshape(row_count, kv_count, repeat, HEAD_SIZE)
    grouped_features = q_feat.reshape(row_count, kv_count, repeat, 2 * HEAD_SIZE)
    score_matrix = jnp.einsum(
        "yzpo,nzo->zpyn", grouped_heads, key_extended, preferred_element_type=jnp.float32
    ) / math.sqrt(HEAD_SIZE)
    linear_attention = jnp.einsum(
        "zbpj,qbj->bpzq", grouped_features, key_feature_extended, preferred_element_type=jnp.float32
    )
    exp_scores = jnp.where(window_mask, jnp.exp(score_matrix), 0.0)
    weight_matrix = exp_scores + jnp.where(band_mask, linear_attention, 0.0)
    ratio_full = weight_matrix / softmax_divisor[..., None]
    rank_weights = ratio_full.astype(jnp.bfloat16)
    gradient_grouped_heads = grad_out.reshape(row_count, kv_count, repeat, HEAD_SIZE)
    grad_weights = jnp.einsum(
        "yzpo,nzo->zpyn", gradient_grouped_heads, value_extended, preferred_element_type=jnp.float32
    )
    delta_rows = jnp.sum(ratio_full * grad_weights, axis=-1) + jnp.einsum(
        "jwsc,jwsc->wsj", gradient_grouped_heads.astype(jnp.float32), state_output
    )
    grad_weight = (grad_weights - delta_rows[..., None]) / softmax_divisor[..., None]
    gradient_score_matrix = jnp.where(window_mask, grad_weight * exp_scores, 0.0).astype(
        jnp.bfloat16
    )
    gradient_linear_branch = jnp.where(band_mask, grad_weight, 0.0).astype(jnp.bfloat16)
    inverse_scale = 1.0 / math.sqrt(HEAD_SIZE)
    grad_q = (
        jnp.einsum(
            "qxlm,mqo->lqxo",
            gradient_score_matrix,
            key_extended,
            preferred_element_type=jnp.float32,
        )
        * inverse_scale
    )
    grad_k = (
        jnp.einsum(
            "nzmy,mnzu->ynu",
            gradient_score_matrix,
            grouped_heads,
            preferred_element_type=jnp.float32,
        )
        * inverse_scale
    )
    gradient_query_features = jnp.einsum(
        "bauh,hbm->ubam",
        gradient_linear_branch,
        key_feature_extended,
        preferred_element_type=jnp.float32,
    )
    grad_kf = jnp.einsum(
        "zxql,qzxw->lzw",
        gradient_linear_branch,
        grouped_features,
        preferred_element_type=jnp.float32,
    )
    grad_v = jnp.einsum(
        "nzmy,mnzu->ynu", rank_weights, gradient_grouped_heads, preferred_element_type=jnp.float32
    )
    inverse_den = jnp.transpose(1.0 / softmax_divisor, (2, 0, 1))
    scaled_spans = (gradient_grouped_heads.astype(jnp.float32) * inverse_den[..., None]).reshape(
        span_count, WIN, kv_count, repeat, HEAD_SIZE
    )
    grad_den = (-jnp.transpose(delta_rows, (2, 0, 1)) * inverse_den).reshape(
        span_count, WIN, kv_count, repeat
    )
    feat_spans = grouped_features.astype(jnp.float32).reshape(
        span_count, WIN, kv_count, repeat, 2 * HEAD_SIZE
    )
    gradient_query_features = gradient_query_features + (
        jnp.einsum("cwgrd,cgfd->cwgrf", scaled_spans, states, precision=EXACT_PRECISION)
        + jnp.einsum("cwgr,cgf->cwgrf", grad_den, norm_states, precision=EXACT_PRECISION)
    ).reshape(row_count, kv_count, repeat, 2 * HEAD_SIZE)
    grad_states = jnp.einsum(
        "cwgrf,cwgrd->cgfd", feat_spans, scaled_spans, precision=EXACT_PRECISION
    )
    grad_norms = jnp.einsum("cwgrf,cwgr->cgf", feat_spans, grad_den, precision=EXACT_PRECISION)
    return (grad_q, grad_k, gradient_query_features, grad_kf, grad_v, grad_states, grad_norms)


def span_states(k_feat, value_rows):
    span_count = k_feat.shape[0] // WIN
    kv_count = k_feat.shape[1]
    key_spans = k_feat.astype(jnp.float32).reshape(span_count, WIN, kv_count, 2 * HEAD_SIZE)
    contrib = jnp.einsum(
        "cwgf,cwgd->cgfd",
        key_spans,
        value_rows.astype(jnp.float32).reshape(span_count, WIN, kv_count, HEAD_SIZE),
        precision=EXACT_PRECISION,
    )
    running = jnp.cumsum(contrib, axis=0)
    norm_running = jnp.cumsum(jnp.sum(key_spans, axis=1), axis=0)
    states = jnp.concatenate(
        [
            jnp.zeros((2, kv_count, 2 * HEAD_SIZE, HEAD_SIZE), jnp.float32),
            running[: span_count - 2],
        ],
        axis=0,
    )
    norm_states = jnp.concatenate(
        [jnp.zeros((2, kv_count, 2 * HEAD_SIZE), jnp.float32), norm_running[: span_count - 2]],
        axis=0,
    )
    return (states, norm_states)


def padded_keys(k_rot, value_rows, k_feat):
    return tuple(
        (
            jnp.concatenate([jnp.zeros((WIN,) + array.shape[1:], array.dtype), array], axis=0)
            for array in (k_rot, value_rows, k_feat)
        )
    )


def local_attend(q_rot, k_rot, value_rows, q_feat, k_feat):
    row_count = q_rot.shape[0]
    states, norm_states = span_states(k_feat, value_rows)
    key_pad, value_pad, feat_pad = padded_keys(k_rot, value_rows, k_feat)
    block_rows = math.gcd(row_count, 512)
    mixed_parts = []
    den_parts = []
    state_parts = []
    for block_index in range(row_count // block_rows):
        row_start = block_index * block_rows
        span_start = row_start // WIN
        span_stop = span_start + block_rows // WIN
        query_pos = row_start + jnp.arange(block_rows, dtype=jnp.int32)
        key_pos = row_start - WIN + jnp.arange(block_rows + WIN, dtype=jnp.int32)
        mixed_block, den_block, state_block = attend(
            q_rot[row_start : row_start + block_rows],
            key_pad[row_start : row_start + block_rows + WIN],
            value_pad[row_start : row_start + block_rows + WIN],
            q_feat[row_start : row_start + block_rows],
            feat_pad[row_start : row_start + block_rows + WIN],
            states[span_start:span_stop],
            norm_states[span_start:span_stop],
            query_pos,
            key_pos,
        )
        mixed_parts.append(mixed_block)
        den_parts.append(den_block)
        state_parts.append(state_block)
    return (
        jnp.concatenate(mixed_parts, axis=0),
        jnp.concatenate(den_parts, axis=2),
        jnp.concatenate(state_parts, axis=0),
        states,
        norm_states,
    )


def local_attend_back(
    grad_mixed,
    q_rot,
    k_rot,
    value_rows,
    q_feat,
    k_feat,
    states,
    norm_states,
    softmax_divisor,
    state_output,
):
    row_count = q_rot.shape[0]
    kv_count = k_rot.shape[1]
    span_count = row_count // WIN
    key_pad, value_pad, feat_pad = padded_keys(k_rot, value_rows, k_feat)
    block_rows = math.gcd(row_count, 512)
    grad_k_pad = jnp.zeros((row_count + WIN, kv_count, HEAD_SIZE), jnp.float32)
    grad_f_pad = jnp.zeros((row_count + WIN, kv_count, 2 * HEAD_SIZE), jnp.float32)
    grad_v_pad = jnp.zeros((row_count + WIN, kv_count, HEAD_SIZE), jnp.float32)
    grad_q_parts = []
    grad_qf_parts = []
    state_grad_parts = []
    norm_grad_parts = []
    for block_index in range(row_count // block_rows):
        row_start = block_index * block_rows
        span_start = row_start // WIN
        span_stop = span_start + block_rows // WIN
        query_pos = row_start + jnp.arange(block_rows, dtype=jnp.int32)
        key_pos = row_start - WIN + jnp.arange(block_rows + WIN, dtype=jnp.int32)
        grad_q, grad_k, gradient_query_features, grad_kf, grad_v, grad_states, grad_norms = (
            attend_back(
                grad_mixed[row_start : row_start + block_rows],
                q_rot[row_start : row_start + block_rows],
                key_pad[row_start : row_start + block_rows + WIN],
                value_pad[row_start : row_start + block_rows + WIN],
                q_feat[row_start : row_start + block_rows],
                feat_pad[row_start : row_start + block_rows + WIN],
                states[span_start:span_stop],
                norm_states[span_start:span_stop],
                softmax_divisor[:, :, row_start : row_start + block_rows],
                state_output[row_start : row_start + block_rows],
                query_pos,
                key_pos,
            )
        )
        pad_rows = ((row_start, row_count - row_start - block_rows), (0, 0), (0, 0))
        grad_k_pad = grad_k_pad + jnp.pad(grad_k, pad_rows)
        grad_f_pad = grad_f_pad + jnp.pad(grad_kf, pad_rows)
        grad_v_pad = grad_v_pad + jnp.pad(grad_v, pad_rows)
        grad_q_parts.append(grad_q)
        grad_qf_parts.append(gradient_query_features)
        state_grad_parts.append(grad_states)
        norm_grad_parts.append(grad_norms)
    grad_states = jnp.concatenate(state_grad_parts, axis=0)
    grad_norms = jnp.concatenate(norm_grad_parts, axis=0)
    suffix = jnp.flip(jnp.cumsum(jnp.flip(grad_states, 0), axis=0), 0)
    norm_suffix = jnp.flip(jnp.cumsum(jnp.flip(grad_norms, 0), axis=0), 0)
    span_grad = jnp.concatenate(
        [suffix[2:], jnp.zeros((2,) + suffix.shape[1:], jnp.float32)], axis=0
    )
    span_norm_grad = jnp.concatenate(
        [norm_suffix[2:], jnp.zeros((2,) + norm_suffix.shape[1:], jnp.float32)], axis=0
    )
    key_spans = k_feat.astype(jnp.float32).reshape(span_count, WIN, kv_count, 2 * HEAD_SIZE)
    value_spans = value_rows.astype(jnp.float32).reshape(span_count, WIN, kv_count, HEAD_SIZE)
    grad_kf = grad_f_pad[WIN:] + (
        jnp.einsum("cwgd,cgfd->cwgf", value_spans, span_grad, precision=EXACT_PRECISION)
        + span_norm_grad[:, None]
    ).reshape(row_count, kv_count, 2 * HEAD_SIZE)
    grad_v = grad_v_pad[WIN:] + jnp.einsum(
        "cwgf,cgfd->cwgd", key_spans, span_grad, precision=EXACT_PRECISION
    ).reshape(row_count, kv_count, HEAD_SIZE)
    return (
        jnp.concatenate(grad_q_parts, axis=0),
        grad_k_pad[WIN:],
        jnp.concatenate(grad_qf_parts, axis=0),
        grad_kf,
        grad_v,
    )


def local_forward(
    tokens, frozen_part, adapter_weight_list, seq_len, geometry, full_tables, shard_index
):
    query_weight, key_weight, value_weight, output_weight, gate_weight, up_weight, down_weight = (
        frozen_part
    )
    (
        adapter_down_weights,
        adapter_up_query_output,
        adapter_up_key_value,
        query_feature_weights,
        key_feature_weights,
        norm_gain_weights,
    ) = adapter_weight_list
    query_pos = geometry[0]
    full_cos, full_sin = full_tables
    query_width = query_weight.shape[1]
    key_value_width = key_weight.shape[1]
    head_count = query_width // HEAD_SIZE
    kv_count = key_value_width // HEAD_SIZE
    query_start = shard_index * query_width
    key_value_start = shard_index * key_value_width
    tok_f = tokens.astype(jnp.float32)
    scale_one = rms_scale(tok_f)
    normalized_attention_input = (
        tok_f * scale_one * norm_gain_weights[:, 0].astype(jnp.float32)
    ).astype(jnp.bfloat16)
    normalized_inputs = rows_in(normalized_attention_input)
    block_len = normalized_inputs.shape[0]
    adapter_rank_inputs = jnp.dot(
        normalized_inputs,
        adapter_down_weights[:, : 3 * ADAPTER_RANK],
        preferred_element_type=jnp.float32,
    ).astype(jnp.bfloat16)
    up_query_weight = lax.dynamic_slice_in_dim(adapter_up_query_output, query_start, query_width, 0)
    up_key_value = lax.dynamic_slice_in_dim(
        adapter_up_key_value, key_value_start, key_value_width, 0
    )
    query_rows = jnp.dot(
        normalized_inputs, query_weight, preferred_element_type=jnp.float32
    ) + jnp.einsum(
        "jo,so->js",
        adapter_rank_inputs[:, :ADAPTER_RANK],
        up_query_weight[:, :ADAPTER_RANK],
        preferred_element_type=jnp.float32,
    )
    key_projected = jnp.dot(
        normalized_inputs, key_weight, preferred_element_type=jnp.float32
    ) + jnp.einsum(
        "jo,so->js",
        adapter_rank_inputs[:, ADAPTER_RANK : 2 * ADAPTER_RANK],
        up_key_value[:, :ADAPTER_RANK],
        preferred_element_type=jnp.float32,
    )
    value_rows = (
        (
            jnp.dot(normalized_inputs, value_weight, preferred_element_type=jnp.float32)
            + jnp.einsum(
                "jo,so->js",
                adapter_rank_inputs[:, 2 * ADAPTER_RANK : 3 * ADAPTER_RANK],
                up_key_value[:, ADAPTER_RANK:],
                preferred_element_type=jnp.float32,
            )
        )
        .astype(jnp.bfloat16)
        .reshape(block_len, kv_count, HEAD_SIZE)
    )
    q_rot = rotate(query_rows.reshape(block_len, head_count, HEAD_SIZE), full_cos, full_sin).astype(
        jnp.bfloat16
    )
    k_rot = rotate(
        key_projected.reshape(block_len, kv_count, HEAD_SIZE), full_cos, full_sin
    ).astype(jnp.bfloat16)
    fmap_q3 = lax.dynamic_slice_in_dim(query_feature_weights, query_start, query_width, 0).reshape(
        head_count, HEAD_SIZE, HEAD_SIZE
    )
    fmap_k3 = lax.dynamic_slice_in_dim(
        key_feature_weights, key_value_start, key_value_width, 0
    ).reshape(kv_count, HEAD_SIZE, HEAD_SIZE)
    q_pos, q_neg = feature_map(q_rot, fmap_q3)
    q_feat = jnp.concatenate([q_pos, q_neg], axis=-1).astype(jnp.bfloat16)
    k_pos, k_neg = feature_map(k_rot, fmap_k3)
    k_feat = jnp.concatenate([k_pos, k_neg], axis=-1).astype(jnp.bfloat16)
    combined_heads, softmax_divisor, state_output, states, norm_states = local_attend(
        q_rot, k_rot, value_rows, q_feat, k_feat
    )
    combined_rank_rows = combined_heads.astype(jnp.bfloat16)
    adapter_output_rows = lax.dynamic_slice_in_dim(
        adapter_down_weights, query_start, query_width, 0
    )[:, 3 * ADAPTER_RANK :]
    branch_rows, out_rows = rows_out_pair(
        jnp.dot(combined_rank_rows, output_weight, preferred_element_type=jnp.float32),
        jnp.dot(combined_rank_rows, adapter_output_rows, preferred_element_type=jnp.float32),
    )
    output_rank_rows = out_rows.astype(jnp.bfloat16)
    middle_sum = tok_f + (
        branch_rows
        + jnp.einsum(
            "jo,so->js",
            output_rank_rows,
            adapter_up_query_output[:, ADAPTER_RANK:],
            preferred_element_type=jnp.float32,
        )
    )
    scale_two = rms_scale(middle_sum)
    normed_two = (middle_sum * scale_two * norm_gain_weights[:, 1].astype(jnp.float32)).astype(
        jnp.bfloat16
    )
    normed_wide = rows_in(normed_two)
    gate_proj = jnp.dot(normed_wide, gate_weight, preferred_element_type=jnp.float32)
    up_proj = jnp.dot(normed_wide, up_weight, preferred_element_type=jnp.float32)
    hidden = (jax.nn.silu(gate_proj) * up_proj).astype(jnp.bfloat16)
    result = middle_sum + rows_out_one(
        jnp.dot(hidden, down_weight, preferred_element_type=jnp.float32)
    )
    valid_rows = (query_pos < seq_len)[:, None]
    out_block = jnp.where(valid_rows, result, 0.0).astype(jnp.bfloat16)
    saved = (
        scale_one,
        normalized_attention_input,
        adapter_rank_inputs,
        q_rot,
        k_rot,
        value_rows,
        q_feat,
        k_feat,
        q_pos,
        q_neg,
        k_pos,
        k_neg,
        states,
        norm_states,
        softmax_divisor,
        state_output,
        combined_rank_rows,
        output_rank_rows,
        middle_sum,
        scale_two,
        gate_proj,
        up_proj,
    )
    return (out_block, saved)


def local_backward(
    tokens,
    cot_block,
    frozen_part,
    adapter_weight_list,
    seq_len,
    geometry,
    full_tables,
    shard_index,
    saved,
):
    query_weight, key_weight, value_weight, output_weight, gate_weight, up_weight, down_weight = (
        frozen_part
    )
    (
        adapter_down_weights,
        adapter_up_query_output,
        adapter_up_key_value,
        query_feature_weights,
        key_feature_weights,
        norm_gain_weights,
    ) = adapter_weight_list
    query_pos = geometry[0]
    full_cos, full_sin = full_tables
    (
        scale_one,
        normalized_attention_input,
        adapter_rank_inputs,
        q_rot,
        k_rot,
        value_rows,
        q_feat,
        k_feat,
        q_pos,
        q_neg,
        k_pos,
        k_neg,
        states,
        norm_states,
        softmax_divisor,
        state_output,
        combined_rank_rows,
        output_rank_rows,
        middle_sum,
        scale_two,
        gate_proj,
        up_proj,
    ) = saved
    query_width = query_weight.shape[1]
    key_value_width = key_weight.shape[1]
    head_count = query_width // HEAD_SIZE
    kv_count = key_value_width // HEAD_SIZE
    query_start = shard_index * query_width
    key_value_start = shard_index * key_value_width
    block_len = q_rot.shape[0]
    tok_f = tokens.astype(jnp.float32)
    gain_one = norm_gain_weights[:, 0].astype(jnp.float32)
    gain_two = norm_gain_weights[:, 1].astype(jnp.float32)
    up_query_weight = lax.dynamic_slice_in_dim(adapter_up_query_output, query_start, query_width, 0)
    up_key_value = lax.dynamic_slice_in_dim(
        adapter_up_key_value, key_value_start, key_value_width, 0
    )
    adapter_output_rows = lax.dynamic_slice_in_dim(
        adapter_down_weights, query_start, query_width, 0
    )[:, 3 * ADAPTER_RANK :]
    fmap_q3 = lax.dynamic_slice_in_dim(query_feature_weights, query_start, query_width, 0).reshape(
        head_count, HEAD_SIZE, HEAD_SIZE
    )
    fmap_k3 = lax.dynamic_slice_in_dim(
        key_feature_weights, key_value_start, key_value_width, 0
    ).reshape(kv_count, HEAD_SIZE, HEAD_SIZE)
    grad_y = jnp.where((query_pos < seq_len)[:, None], cot_block, jnp.zeros_like(cot_block))
    grad_y_all = rows_in(grad_y)
    grad_hidden = jnp.einsum(
        "td,fd->tf", grad_y_all, down_weight, preferred_element_type=jnp.float32
    )
    sigmoid_gate = jax.nn.sigmoid(gate_proj)
    grad_gate = (
        grad_hidden * up_proj * sigmoid_gate * (1.0 + gate_proj * (1.0 - sigmoid_gate))
    ).astype(jnp.bfloat16)
    grad_up = (grad_hidden * gate_proj * sigmoid_gate).astype(jnp.bfloat16)
    grad_norm2 = rows_out_one(
        jnp.einsum("tf,df->td", grad_gate, gate_weight, preferred_element_type=jnp.float32)
        + jnp.einsum("tf,df->td", grad_up, up_weight, preferred_element_type=jnp.float32)
    )
    grad_g2 = jnp.sum(grad_norm2 * middle_sum * scale_two, axis=0)
    grad_mid = (
        grad_y.astype(jnp.float32)
        + scale_two * gain_two * grad_norm2
        - middle_sum
        * scale_two**3
        * jnp.mean(gain_two * grad_norm2 * middle_sum, axis=-1, keepdims=True)
    )
    grad_branch = grad_mid.astype(jnp.bfloat16)
    grad_up_o = jnp.einsum(
        "jq,je->qe", grad_branch, output_rank_rows, preferred_element_type=jnp.float32
    )
    branch_outputs = rows_in(grad_branch)
    gradient_output_adapter = jnp.einsum(
        "gw,wh->gh",
        branch_outputs,
        adapter_up_query_output[:, ADAPTER_RANK:],
        preferred_element_type=jnp.float32,
    ).astype(jnp.bfloat16)
    grad_mixed = (
        jnp.einsum("td,ed->te", branch_outputs, output_weight, preferred_element_type=jnp.float32)
        + jnp.einsum(
            "ih,fh->if",
            gradient_output_adapter,
            adapter_output_rows,
            preferred_element_type=jnp.float32,
        )
    ).astype(jnp.bfloat16)
    grad_down_o = lax.dynamic_update_slice_in_dim(
        jnp.zeros((H * HEAD_SIZE, ADAPTER_RANK), jnp.float32),
        jnp.einsum(
            "te,tr->er",
            combined_rank_rows,
            gradient_output_adapter,
            preferred_element_type=jnp.float32,
        ),
        query_start,
        0,
    )
    grad_q, grad_k_rot, gradient_query_features, grad_k_feat, grad_v = local_attend_back(
        grad_mixed,
        q_rot,
        k_rot,
        value_rows,
        q_feat,
        k_feat,
        states,
        norm_states,
        softmax_divisor,
        state_output,
    )
    gradient_value_rows = grad_v.reshape(block_len, key_value_width).astype(jnp.bfloat16)
    grad_k_map = feature_back(grad_k_feat, k_pos, k_neg).astype(jnp.bfloat16)
    fmap_k_rows = jnp.einsum(
        "tgd,tge->gde", k_rot, grad_k_map, preferred_element_type=jnp.float32
    ).reshape(key_value_width, HEAD_SIZE)
    grad_fmap_k = lax.dynamic_update_slice_in_dim(
        jnp.zeros((KEY_VALUE_HEADS * HEAD_SIZE, HEAD_SIZE), jnp.float32),
        fmap_k_rows,
        key_value_start,
        0,
    )
    grad_k_rot = grad_k_rot + jnp.einsum(
        "tge,gde->tgd", grad_k_map, fmap_k3, preferred_element_type=jnp.float32
    )
    grad_q_map = feature_back(
        gradient_query_features.reshape(block_len, head_count, 2 * HEAD_SIZE), q_pos, q_neg
    ).astype(jnp.bfloat16)
    fmap_q_rows = jnp.einsum(
        "thd,the->hde", q_rot, grad_q_map, preferred_element_type=jnp.float32
    ).reshape(query_width, HEAD_SIZE)
    grad_fmap_q = lax.dynamic_update_slice_in_dim(
        jnp.zeros((H * HEAD_SIZE, HEAD_SIZE), jnp.float32), fmap_q_rows, query_start, 0
    )
    grad_q_rot = grad_q.reshape(block_len, head_count, HEAD_SIZE) + jnp.einsum(
        "the,hde->thd", grad_q_map, fmap_q3, preferred_element_type=jnp.float32
    )
    gradient_query_rows = (
        rotate_back(grad_q_rot, full_cos, full_sin)
        .reshape(block_len, query_width)
        .astype(jnp.bfloat16)
    )
    gradient_key_rows = (
        rotate_back(grad_k_rot, full_cos, full_sin)
        .reshape(block_len, key_value_width)
        .astype(jnp.bfloat16)
    )
    grad_up_q = lax.dynamic_update_slice_in_dim(
        jnp.zeros((H * HEAD_SIZE, ADAPTER_RANK), jnp.float32),
        jnp.einsum(
            "jq,je->qe",
            gradient_query_rows,
            adapter_rank_inputs[:, :ADAPTER_RANK],
            preferred_element_type=jnp.float32,
        ),
        query_start,
        0,
    )
    grad_up_k = lax.dynamic_update_slice_in_dim(
        jnp.zeros((KEY_VALUE_HEADS * HEAD_SIZE, ADAPTER_RANK), jnp.float32),
        jnp.einsum(
            "jq,je->qe",
            gradient_key_rows,
            adapter_rank_inputs[:, ADAPTER_RANK : 2 * ADAPTER_RANK],
            preferred_element_type=jnp.float32,
        ),
        key_value_start,
        0,
    )
    grad_up_v = lax.dynamic_update_slice_in_dim(
        jnp.zeros((KEY_VALUE_HEADS * HEAD_SIZE, ADAPTER_RANK), jnp.float32),
        jnp.einsum(
            "jq,je->qe",
            gradient_value_rows,
            adapter_rank_inputs[:, 2 * ADAPTER_RANK : 3 * ADAPTER_RANK],
            preferred_element_type=jnp.float32,
        ),
        key_value_start,
        0,
    )
    low_part = jnp.concatenate(
        [
            jnp.einsum(
                "gw,wh->gh",
                gradient_query_rows,
                up_query_weight[:, :ADAPTER_RANK],
                preferred_element_type=jnp.float32,
            ),
            jnp.einsum(
                "gw,wh->gh",
                gradient_key_rows,
                up_key_value[:, :ADAPTER_RANK],
                preferred_element_type=jnp.float32,
            ),
            jnp.einsum(
                "gw,wh->gh",
                gradient_value_rows,
                up_key_value[:, ADAPTER_RANK:],
                preferred_element_type=jnp.float32,
            ),
        ],
        axis=1,
    )
    norm_part = (
        jnp.einsum(
            "te,de->td", gradient_query_rows, query_weight, preferred_element_type=jnp.float32
        )
        + jnp.einsum("te,de->td", gradient_key_rows, key_weight, preferred_element_type=jnp.float32)
        + jnp.einsum(
            "te,de->td", gradient_value_rows, value_weight, preferred_element_type=jnp.float32
        )
    )
    norm_rows, low_rows = rows_out_pair(norm_part, low_part)
    gradient_adapter_rank = low_rows.astype(jnp.bfloat16)
    grad_down_qkv = jnp.einsum(
        "jq,je->qe",
        normalized_attention_input,
        gradient_adapter_rank,
        preferred_element_type=jnp.float32,
    )
    grad_norm1 = norm_rows + jnp.einsum(
        "jo,so->js",
        gradient_adapter_rank,
        adapter_down_weights[:, : 3 * ADAPTER_RANK],
        preferred_element_type=jnp.float32,
    )
    grad_g1 = jnp.sum(grad_norm1 * tok_f * scale_one, axis=0)
    grad_tokens = (
        grad_mid
        + scale_one * gain_one * grad_norm1
        - tok_f * scale_one**3 * jnp.mean(gain_one * grad_norm1 * tok_f, axis=-1, keepdims=True)
    )
    grads = (
        jnp.concatenate([grad_down_qkv, grad_down_o], axis=1),
        jnp.concatenate([grad_up_q, grad_up_o], axis=1),
        jnp.concatenate([grad_up_k, grad_up_v], axis=1),
        grad_fmap_q,
        grad_fmap_k,
        jnp.stack([grad_g1, grad_g2], axis=1),
    )
    return (grad_tokens.astype(jnp.bfloat16), grads)


def shards(
    inputs,
    cotangent,
    lengths,
    dealing,
    query_weight,
    key_weight,
    value_weight,
    output_weight,
    gate_weight,
    up_weight,
    down_weight,
    adapter_down_weights,
    adapter_up_query_output,
    adapter_up_key_value,
    query_feature_weights,
    key_feature_weights,
    norm_gain_weights,
):
    groups = lax.axis_size("dp")
    group_index = lax.axis_index("dp")
    shard_index = lax.axis_index("fsdp")
    micro_count = inputs.shape[1]
    slot_rows = inputs.shape[2]
    block_len = slot_rows * lax.axis_size("fsdp")
    query_pos = shard_index * slot_rows + jnp.arange(slot_rows, dtype=jnp.int32)
    key_pos = shard_index * slot_rows - WIN + jnp.arange(slot_rows + WIN, dtype=jnp.int32)
    cosine, sine_part = rope_tables(query_pos)
    geometry = (query_pos, key_pos, cosine, sine_part)
    full_tables = rope_tables(jnp.arange(block_len, dtype=jnp.int32))
    local_adapter_weights = (
        adapter_down_weights,
        adapter_up_query_output,
        adapter_up_key_value,
        query_feature_weights,
        key_feature_weights,
        norm_gain_weights,
    )
    local_frozen = (
        query_weight,
        key_weight,
        value_weight,
        output_weight,
        gate_weight,
        up_weight,
        down_weight,
    )
    outputs = []
    input_grads = []
    summed = None
    shares = None
    for micro_index in range(micro_count):
        targets = dealing[micro_index]
        deal_table = (jnp.arange(groups, dtype=jnp.int32)[:, None] == targets[None, :]).astype(
            jnp.bfloat16
        )
        seq_len = jnp.sum(jnp.where(targets == group_index, lengths[:, micro_index], 0))
        dealt_rows = deal(inputs[0, micro_index], deal_table)
        adapter_weight_list = fetch_small(local_adapter_weights)
        frozen_part = fetch_rows(local_frozen)
        out_block, saved = local_forward(
            dealt_rows,
            frozen_part,
            adapter_weight_list,
            seq_len,
            geometry,
            full_tables,
            shard_index,
        )
        fresh_small, fresh_frozen, out_block = lax.optimization_barrier(
            (local_adapter_weights, local_frozen, out_block)
        )
        adapter_weight_list = fetch_small(fresh_small)
        frozen_part = fetch_rows(fresh_frozen)
        grad_tokens, grads = local_backward(
            dealt_rows,
            cotangent[0, micro_index],
            frozen_part,
            adapter_weight_list,
            seq_len,
            geometry,
            full_tables,
            shard_index,
            saved,
        )
        input_grads.append(deal(grad_tokens, jnp.transpose(deal_table)))
        outputs.append(out_block)
        summed = grads if summed is None else add_tuple(summed, grads)
    shares = (
        lax.psum_scatter(summed[0], ("dp", "fsdp"), scatter_dimension=0, tiled=True),
        lax.psum_scatter(summed[1], ("dp", "fsdp"), scatter_dimension=0, tiled=True),
        lax.psum_scatter(summed[2], ("dp", "fsdp"), scatter_dimension=0, tiled=True),
        lax.psum_scatter(summed[3], ("dp", "fsdp"), scatter_dimension=0, tiled=True),
        lax.psum_scatter(summed[4], ("dp", "fsdp"), scatter_dimension=0, tiled=True),
        lax.psum_scatter(summed[5], ("dp", "fsdp"), scatter_dimension=0, tiled=True),
    )
    return (
        jnp.stack(outputs)[None],
        jnp.stack(input_grads)[None],
        shares[0],
        shares[1],
        shares[2],
        shares[3],
        shares[4],
        shares[5],
    )


def solution(mesh):
    in_specs = (
        P("dp", None, "fsdp", None),
        P("dp", None, "fsdp", None),
        P(),
        P(),
        P("dp", "fsdp"),
        P("dp", "fsdp"),
        P("dp", "fsdp"),
        P("fsdp", "dp"),
        P("dp", "fsdp"),
        P("dp", "fsdp"),
        P("fsdp", "dp"),
        P(("dp", "fsdp"), None),
        P(("dp", "fsdp"), None),
        P(("dp", "fsdp"), None),
        P(("dp", "fsdp"), None),
        P(("dp", "fsdp"), None),
        P(("dp", "fsdp"), None),
    )
    out_specs = (
        P("dp", None, "fsdp", None),
        P("dp", None, "fsdp", None),
        P(("dp", "fsdp"), None),
        P(("dp", "fsdp"), None),
        P(("dp", "fsdp"), None),
        P(("dp", "fsdp"), None),
        P(("dp", "fsdp"), None),
        P(("dp", "fsdp"), None),
    )
    return jax.shard_map(shards, mesh=mesh, in_specs=in_specs, out_specs=out_specs, check_vma=False)
```

profile of v0, /device:TPU:0, one launch (start us, length us, event | category | flops | bytes accessed | tf_op | source)
XLA Modules:
  0.0 4147.8 jit_solution(14382630525624979559)
XLA Ops:
  106.5 79.1 %all-gather = bf16[32,64,2]{1,2,0:T(2,128)(2,1)S(1)} all-gather(bf16[1,64,2]{1,2,0:T(2,128)(2,1)S(1)} %bitcast.1071), channel_id=1, replica_groups=mesh['dp'=8,'fsdp'=4] {'dp','fsdp'}, dimensions={0}, use_global_device_ids=true | all-gather | bytes 8448 | tf_op jit(solution)/shard_map/all_gather | solution.py:100
  191.3 67.3 %all_gather.158 = bf16[512,16]{1,0:T(8,128)(2,1)S(1)} all-gather(bf16[16,16]{1,0:T(8,128)(2,1)S(1)} %copy-done.286), channel_id=1, replica_groups=mesh['dp'=8,'fsdp'=4] {'dp','fsdp'}, dimensions={0}, use_global_device_ids=true | all-gather | bytes 16896 | tf_op jit(solution)/shard_map/all_gather | solution.py:97
  258.7 66.3 %all-gather.1 = bf16[32,64,32]{1,2,0:T(8,128)(2,1)S(1)} all-gather(bf16[1,64,32]{1,2,0:T(8,128)(2,1)S(1)} %bitcast.1044), channel_id=1, replica_groups=mesh['dp'=8,'fsdp'=4] {'dp','fsdp'}, dimensions={0}, use_global_device_ids=true | all-gather | bytes 135168 | tf_op jit(solution)/shard_map/all_gather | solution.py:95
  341.1 69.0 %all_gather.163 = bf16[2048,64]{1,0:T(8,128)(2,1)S(1)} all-gather(bf16[64,64]{1,0:T(8,128)(2,1)S(1)} %copy-done.249), channel_id=1, replica_groups=mesh['dp'=8,'fsdp'=4] {'dp','fsdp'}, dimensions={0}, use_global_device_ids=true | all-gather | bytes 270336 | tf_op jit(solution)/shard_map/all_gather | solution.py:98
  474.6 66.4 %all_gather.162 = bf16[512,64]{1,0:T(8,128)(2,1)S(1)} all-gather(bf16[16,64]{1,0:T(8,128)(2,1)S(1)} %copy-done.284), channel_id=1, replica_groups=mesh['dp'=8,'fsdp'=4] {'dp','fsdp'}, dimensions={0}, use_global_device_ids=true | all-gather | bytes 67584 | tf_op jit(solution)/shard_map/all_gather | solution.py:99
  828.1 89.8 %reduce-scatter.33.cloned.1.call-done = f32[256,2048]{1,0:T(8,128)} async-done(((f32[1024,2048]{1,0:T(8,128)}), f32[256,2048]{1,0:T(8,128)}) %reduce-scatter.33.cloned.1.call-update) | async-done | bytes 2097168 | tf_op jit(solution)/shard_map/reduce_scatter | solution.py:122
  925.0 76.6 %all-gather.43.cloned.1.call-done = bf16[2048,2048]{1,0:T(8,128)(2,1)} async-done(((bf16[256,2048]{1,0:T(8,128)(2,1)}), bf16[2048,2048]{1,0:T(8,128)(2,1)}) %all-gather.43.cloned.1.call-update) | async-done | bytes 8388624 | tf_op jit(solution)/shard_map/all_gather | solution.py:111
  1069.3 69.0 %all-gather.41.cloned.1.call-done = bf16[2048,2048]{1,0:T(8,128)(2,1)} async-done(((bf16[256,2048]{1,0:T(8,128)(2,1)}), bf16[2048,2048]{1,0:T(8,128)(2,1)}) %all-gather.41.cloned.1.call-update) | async-done | bytes 8388624 | tf_op jit(solution)/shard_map/all_gather | solution.py:110
  1152.8 67.9 %all-gather.45.cloned.1.call-done = bf16[2048,2048]{1,0:T(8,128)(2,1)} async-done(((bf16[2048,256]{1,0:T(8,128)(2,1)}), bf16[2048,2048]{1,0:T(8,128)(2,1)}) %all-gather.45.cloned.1.call-update) | async-done | bytes 8388624 | tf_op jit(solution)/shard_map/all_gather | solution.py:112
  1439.3 84.0 %all-gather.67.cloned.1.call-done = bf16[2048,2048]{1,0:T(8,128)(2,1)} async-done(((bf16[2048,256]{1,0:T(8,128)(2,1)}), bf16[2048,2048]{1,0:T(8,128)(2,1)}) %all-gather.67.cloned.1.call-update) | async-done | bytes 8388624 | tf_op jit(solution)/shard_map/all_gather | solution.py:112
  1538.2 66.8 %all-gather.69.cloned.1.call-done = bf16[2048,2048]{1,0:T(8,128)(2,1)} async-done(((bf16[256,2048]{1,0:T(8,128)(2,1)}), bf16[2048,2048]{1,0:T(8,128)(2,1)}) %all-gather.69.cloned.1.call-update) | async-done | bytes 8388624 | tf_op jit(solution)/shard_map/all_gather | solution.py:110
  1740.2 84.1 %all-gather.53.cloned.1.call-done = bf16[2048,2048]{1,0:T(8,128)(2,1)} async-done(((bf16[2048,256]{1,0:T(8,128)(2,1)}), bf16[2048,2048]{1,0:T(8,128)(2,1)}) %all-gather.53.cloned.1.call-update) | async-done | bytes 8388624 | tf_op jit(solution)/shard_map/all_gather | solution.py:112
  1839.2 67.0 %all-gather.55.cloned.1.call-done = bf16[2048,2048]{1,0:T(8,128)(2,1)} async-done(((bf16[256,2048]{1,0:T(8,128)(2,1)}), bf16[2048,2048]{1,0:T(8,128)(2,1)}) %all-gather.55.cloned.1.call-update) | async-done | bytes 8388624 | tf_op jit(solution)/shard_map/all_gather | solution.py:110
  2154.0 67.3 %all-gather.7 = bf16[32,64,16]{1,2,0:T(8,128)(2,1)S(1)} all-gather(bf16[1,64,16]{1,2,0:T(8,128)(2,1)S(1)} %bitcast.1053), channel_id=1, replica_groups=mesh['dp'=8,'fsdp'=4] {'dp','fsdp'}, dimensions={0}, use_global_device_ids=true | all-gather | bytes 67584 | tf_op jit(solution)/shard_map/all_gather | solution.py:96
  2287.6 66.8 %all-gather.4 = bf16[32,64,16]{1,2,0:T(8,128)(2,1)S(1)} all-gather(bf16[1,64,16]{1,2,0:T(8,128)(2,1)S(1)} %bitcast.1054), channel_id=1, replica_groups=mesh['dp'=8,'fsdp'=4] {'dp','fsdp'}, dimensions={0}, use_global_device_ids=true | all-gather | bytes 67584 | tf_op jit(solution)/shard_map/all_gather | solution.py:96
  2419.9 71.0 %all_gather.200 = bf16[512,16]{1,0:T(8,128)(2,1)} all-gather(bf16[16,16]{1,0:T(8,128)(2,1)S(1)} %copy-done.287), channel_id=1, replica_groups=mesh['dp'=8,'fsdp'=4] {'dp','fsdp'}, dimensions={0}, use_global_device_ids=true | all-gather | bytes 16896 | tf_op jit(solution)/shard_map/all_gather | solution.py:97
  2555.0 66.4 %all_gather.197 = bf16[512,64]{1,0:T(8,128)(2,1)S(1)} all-gather(bf16[16,64]{1,0:T(8,128)(2,1)S(1)} %copy-done.285), channel_id=1, replica_groups=mesh['dp'=8,'fsdp'=4] {'dp','fsdp'}, dimensions={0}, use_global_device_ids=true | all-gather | bytes 67584 | tf_op jit(solution)/shard_map/all_gather | solution.py:99
  2689.4 68.7 %all_gather.195 = bf16[2048,64]{1,0:T(8,128)(2,1)S(1)} all-gather(bf16[64,64]{1,0:T(8,128)(2,1)S(1)} %copy-done.250), channel_id=1, replica_groups=mesh['dp'=8,'fsdp'=4] {'dp','fsdp'}, dimensions={0}, use_global_device_ids=true | all-gather | bytes 270336 | tf_op jit(solution)/shard_map/all_gather | solution.py:98
  3238.6 85.6 %reduce-scatter.41.cloned.1.call-done = f32[256,2048]{1,0:T(8,128)} async-done(((f32[1024,2048]{1,0:T(8,128)}), f32[256,2048]{1,0:T(8,128)}) %reduce-scatter.41.cloned.1.call-update) | async-done | bytes 2097168 | tf_op jit(solution)/shard_map/reduce_scatter | solution.py:122
  3476.5 131.6 %reduce-scatter.55.cloned.1.call-done = f32[64,32]{1,0:T(8,128)} async-done(((f32[2048,32]{1,0:T(8,128)}), f32[64,32]{1,0:T(8,128)}) %reduce-scatter.55.cloned.1.call-update) | async-done | bytes 8208
  3609.6 132.0 %reduce-scatter.61.cloned.1.call-done = f32[64,2]{1,0:T(8,128)} async-done(((f32[2048,2]{1,0:T(8,128)}), f32[64,2]{1,0:T(8,128)}) %reduce-scatter.61.cloned.1.call-update) | async-done | bytes 528
  3746.0 128.3 %reduce-scatter.59.cloned.1.call-done = f32[16,16]{1,0:T(8,128)} async-done(((f32[512,16]{1,0:T(8,128)}), f32[16,16]{1,0:T(8,128)}) %reduce-scatter.59.cloned.1.call-update) | async-done | bytes 1040
  3874.2 132.8 %reduce-scatter.53.cloned.1.call-done = f32[16,64]{1,0:T(8,128)} async-done(((f32[512,64]{1,0:T(8,128)}), f32[16,64]{1,0:T(8,128)}) %reduce-scatter.53.cloned.1.call-update) | async-done | bytes 4112 | tf_op jit(solution)/shard_map/reduce_scatter | solution.py:957
  4007.0 133.8 %reduce-scatter.51.cloned.1.call-done = f32[64,64]{1,0:T(8,128)} async-done(((f32[2048,64]{1,0:T(8,128)}), f32[64,64]{1,0:T(8,128)}) %reduce-scatter.51.cloned.1.call-update) | async-done | bytes 16400 | tf_op jit(solution)/shard_map/reduce_scatter | solution.py:956
  (1333 shorter events, 2090.7 us)
Async XLA Ops:
  106.4 454.7 %all-gather.33.cloned.1.call-start = ((), (), s32[]{:S(2)}) async-start(), calls=%async_computation.26 | async-start | bytes 5242880 | tf_op jit(solution)/shard_map/all_gather | solution.py:117
  189.1 376.5 %all-gather.47.cloned.1.call-start = ((), (), s32[]{:S(2)}) async-start(), calls=%async_computation.36 | async-start | bytes 5242880 | tf_op jit(solution)/shard_map/all_gather | solution.py:117
  189.9 380.1 %all-gather.35.cloned.1.call-start = ((), (), s32[]{:S(2)}) async-start(), calls=%async_computation.27 | async-start | bytes 2359296 | tf_op jit(solution)/shard_map/all_gather | solution.py:106
  190.6 500.9 %all-gather.37.cloned.1.call-start = ((), (), s32[]{:S(2)}) async-start(), calls=%async_computation.28 | async-start | bytes 2359296 | tf_op jit(solution)/shard_map/all_gather | solution.py:109
  191.2 600.8 %reduce-scatter.29.cloned.1.call-start = ((), (), s32[]{:S(2)}) async-start(), calls=%async_computation.30 | async-start | bytes 40960 | tf_op jit(solution)/shard_map/reduce_scatter | solution.py:123
  924.9 404.2 %reduce-scatter.37.cloned.1.call-start = ((), (), s32[]{:S(2)}) async-start(), calls=%async_computation.40 | async-start | bytes 5242880 | tf_op jit(solution)/shard_map/reduce_scatter | solution.py:128
  1332.8 354.4 %all-gather.71.cloned.1.call-start = ((), (), s32[]{:S(2)}) async-start(), calls=%async_computation.54 | async-start | bytes 9437184 | tf_op jit(solution)/shard_map/all_gather | solution.py:111
  1333.6 406.6 %all-gather.51.cloned.1.call-start = ((), (), s32[]{:S(2)}) async-start(), calls=%async_computation.41 | async-start | bytes 5242880 | tf_op jit(solution)/shard_map/all_gather | solution.py:117
  1334.2 490.2 %all-gather.53.cloned.1.call-start = ((), (), s32[]{:S(2)}) async-start(), calls=%async_computation.42 | async-start | bytes 9437184 | tf_op jit(solution)/shard_map/all_gather | solution.py:112
  1387.4 518.8 %all-gather.55.cloned.1.call-start = ((), (), s32[]{:S(2)}) async-start(), calls=%async_computation.43 | async-start | bytes 9437184 | tf_op jit(solution)/shard_map/all_gather | solution.py:110
  1388.1 600.3 %all-gather.57.cloned.1.call-start = ((), (), s32[]{:S(2)}) async-start(), calls=%async_computation.44 | async-start | bytes 9437184 | tf_op jit(solution)/shard_map/all_gather | solution.py:111
  1388.9 685.6 %reduce-scatter.45.cloned.1.call-start = ((), (), s32[]{:S(2)}) async-start(), calls=%async_computation.55 | async-start | bytes 5242880 | tf_op jit(solution)/shard_map/reduce_scatter | solution.py:128
  1706.7 438.8 %reduce-scatter.39.cloned.1.call-start = ((), (), s32[]{:S(2)}) async-start(), calls=%async_computation.45 | async-start | bytes 5242880 | tf_op jit(solution)/shard_map/reduce_scatter | solution.py:128
  2007.6 783.0 %all-gather.75.cloned.1.call-start = ((), (), s32[]{:S(2)}) async-start(), calls=%async_computation.57 | async-start | bytes 2359296 | tf_op jit(solution)/shard_map/all_gather | solution.py:109
  2008.2 782.5 %all-gather.73.cloned.1.call-start = ((), (), s32[]{:S(2)}) async-start(), calls=%async_computation.56 | async-start | bytes 5242880 | tf_op jit(solution)/shard_map/all_gather | solution.py:117
  2080.9 721.0 %all-gather.61.cloned.1.call-start = ((), (), s32[]{:S(2)}) async-start(), calls=%async_computation.47 | async-start | bytes 2359296 | tf_op jit(solution)/shard_map/all_gather | solution.py:109
  2081.6 720.3 %all-gather.59.cloned.1.call-start = ((), (), s32[]{:S(2)}) async-start(), calls=%async_computation.46 | async-start | bytes 5242880 | tf_op jit(solution)/shard_map/all_gather | solution.py:117
  2150.5 938.1 %all-gather.77.cloned.1.call-start = ((), (), s32[]{:S(2)}) async-start(), calls=%async_computation.58 | async-start | bytes 2359296 | tf_op jit(solution)/shard_map/all_gather | solution.py:106
  2151.1 1061.5 %all-gather.63.cloned.1.call-start = ((), (), s32[]{:S(2)}) async-start(), calls=%async_computation.48 | async-start | bytes 2359296 | tf_op jit(solution)/shard_map/all_gather | solution.py:106
  2790.4 432.8 %reduce-scatter.49.cloned.1.call-start = ((), (), s32[]{:S(2)}) async-start(), calls=%async_computation.60 | async-start | bytes 122880 | tf_op jit(solution)/shard_map/reduce_scatter | solution.py:123
  3367.5 374.0 %reduce-scatter.61.cloned.1.call-start = ((), (), s32[]{:S(2)}) async-start(), calls=%async_computation.66 | async-start | bytes 1081344
  3369.4 504.8 %reduce-scatter.59.cloned.1.call-start = ((), (), s32[]{:S(2)}) async-start(), calls=%async_computation.65 | async-start | bytes 270336
  3397.5 609.5 %reduce-scatter.53.cloned.1.call-start = ((), (), s32[]{:S(2)}) async-start(), calls=%async_computation.62 | async-start | bytes 270336 | tf_op jit(solution)/shard_map/reduce_scatter | solution.py:957
  3398.4 742.4 %reduce-scatter.51.cloned.1.call-start = ((), (), s32[]{:S(2)}) async-start(), calls=%async_computation.61 | async-start | bytes 1081344 | tf_op jit(solution)/shard_map/reduce_scatter | solution.py:956
  (414 other events, 14607.1 us)
Sparse Core Ops, SparseCore 0:
  243.0 54.7 all-gather.46
  714.8 86.4 reduce-scatter.26
  831.4 86.4 reduce-scatter.32
  919.5 82.0 all-gather.42
  1056.2 82.0 all-gather.40
  1139.7 81.0 all-gather.44
  1276.3 52.6 reduce-scatter.36
  1440.8 82.4 all-gather.66
  1524.8 80.2 all-gather.68
  1606.6 80.5 all-gather.70
  1741.8 82.4 all-gather.52
  1826.0 80.2 all-gather.54
  1907.8 80.5 all-gather.56
  2045.9 52.7 reduce-scatter.38
  2132.7 52.8 all-gather.72
  2220.1 54.4 all-gather.58
  3112.3 87.8 reduce-scatter.46
  3237.8 86.4 reduce-scatter.40
  3337.0 138.0 reduce-scatter.56
  3477.3 130.7 reduce-scatter.54
  3610.4 131.1 reduce-scatter.60
  3744.3 129.9 reduce-scatter.58
  3877.0 129.9 reduce-scatter.52
  4009.9 130.8 reduce-scatter.50
  (17 shorter events, 625.4 us)
where the time goes:
time: 4160 us; the launch traced here: 4150 us
  waiting for transfers between devices  1880 us (45%)
  blocking collectives  1330 us (32%)
  matrix products  587 us (14%)
  other arithmetic  156 us (4%)
  local copies, waits for them, and re-layouts  140 us (3%)
    unnamed x45, waiting for transfers between devices  461 us
    all_gather x3, waiting for transfers between devices, fetch_rows(): lax.all_gather(local_frozen[6], 'dp', axis=1, tiled=True)  236 us
    all_gather x3, blocking collectives, fetch_small(): lax.all_gather(local_adapter_weights[5], ('dp', 'fsdp'), axis=0, tiled=True)  208 us
    all_gather x3, blocking collectives, fetch_small(): lax.all_gather(local_adapter_weights[3], ('dp', 'fsdp'), axis=0, tiled=True)  204 us
    all_gather x3, blocking collectives, fetch_small(): lax.all_gather(local_adapter_weights[2], ('dp', 'fsdp'), axis=0, tiled=True)  204 us
    all_gather x3, waiting for transfers between devices, fetch_rows(): lax.all_gather(local_frozen[4], 'dp', axis=0, tiled=True)  203 us
    all_gather x3, blocking collectives, fetch_small(): lax.all_gather(local_adapter_weights[1], ('dp', 'fsdp'), axis=0, tiled=True)  198 us
    all_gather x3, blocking collectives, fetch_small(): lax.all_gather(local_adapter_weights[4], ('dp', 'fsdp'), axis=0, tiled=True)  197 us
  transfers between devices with their start and end apart: 48, of which 29 were waited for; matrix products, arithmetic and copies ran while one was open for 20% of the time, Pallas kernels for 0%

commit v1 on v0

v1 whole, which is shorter than its diff:
```python
import functools
import math

import jax
import jax.numpy as jnp
from jax import lax
from jax.experimental import pallas as pl
from jax.experimental.pallas import tpu as pltpu
from jax.sharding import PartitionSpec as P

H = 32
KEY_VALUE_HEADS = 8
REPEAT = H // KEY_VALUE_HEADS
HEAD_SIZE = 64
ADAPTER_RANK = 8
WIN = 64
AUG = 80
RANK_LANES = 128

EPSILON = 1e-05
ROPE_BASE = 500000.0
F32 = jnp.float32
BF16 = jnp.bfloat16
MIB = 1024 * 1024


def dot(a, b):
    return lax.dot_general(a, b, (((1,), (0,)), ((), ())), preferred_element_type=F32)


def dot_nt(a, b):
    return lax.dot_general(a, b, (((1,), (1,)), ((), ())), preferred_element_type=F32)


def params(mib, semantics=("arbitrary",)):
    return pltpu.CompilerParams(vmem_limit_bytes=mib * MIB, dimension_semantics=semantics)


def cost(flops, bytes_accessed, transcendentals=0):
    return pl.CostEstimate(
        flops=int(flops), bytes_accessed=int(bytes_accessed), transcendentals=int(transcendentals)
    )


def whole(shape):
    return pl.BlockSpec(shape, lambda *_: (0,) * len(shape))


def rope_tables_t(positions):
    half_size = HEAD_SIZE // 2
    frequencies = jnp.exp(
        -(2.0 * jnp.arange(half_size, dtype=F32) / HEAD_SIZE) * math.log(ROPE_BASE)
    )
    angles = frequencies[:, None] * positions.astype(F32)[None, :]
    return jnp.cos(angles), jnp.sin(angles)


def rotate_t(head, cos_t, sin_t):
    a, b = head[:32], head[32:]
    return jnp.concatenate([a * cos_t - b * sin_t, b * cos_t + a * sin_t], axis=0)


def rotate_back_t(head, cos_t, sin_t):
    a, b = head[:32], head[32:]
    return jnp.concatenate([a * cos_t + b * sin_t, b * cos_t - a * sin_t], axis=0)


def half_softmax_t(scores):
    e = jnp.exp(scores - jnp.max(scores, axis=0, keepdims=True))
    return e * (1.0 / jnp.sum(e, axis=0, keepdims=True))


def features_t(mapped):
    return jnp.concatenate([half_softmax_t(mapped[:64]), half_softmax_t(mapped[64:])], axis=0)


def features_back_t(e, f):
    ef = e * f
    t1 = jnp.sum(ef[:64], axis=0, keepdims=True)
    t2 = jnp.sum(ef[64:], axis=0, keepdims=True)
    return (ef[:64] - e[:64] * t1) - (ef[64:] - e[64:] * t2)


def project(h1_ref, u_ref, w_ref, b_ref, depth):
    total = dot(u_ref[...], b_ref[0])
    for j in range(w_ref.shape[0]):
        total += dot(h1_ref[:, j * depth : (j + 1) * depth], w_ref[j, 0])
    return total


def kv_kernel(kv_heads, micro, depth, h1_ref, u_ref, w_ref, b_ref, cos_ref, sin_ref, f_ref,
              n_ref, tot_ref):
    rows = h1_ref.shape[0] // micro
    kv_t = project(h1_ref, u_ref, w_ref, b_ref, depth).T
    cos_t, sin_t = cos_ref[...], sin_ref[...]
    width = kv_heads * HEAD_SIZE
    for g in range(kv_heads):
        kr = rotate_t(kv_t[g * 64 : (g + 1) * 64], cos_t, sin_t).astype(BF16)
        v = kv_t[width + g * 64 : width + (g + 1) * 64].astype(BF16)
        pk = features_t(dot(f_ref[g], kr)).astype(BF16)
        natural = (
            jnp.concatenate([pk.astype(F32), kr.astype(F32), v.astype(F32)], axis=0).T
        ).astype(BF16)
        v_aug = jnp.concatenate([v, jnp.ones((AUG - 64, v.shape[1]), BF16)], axis=0)
        for m in range(micro):
            part = natural[m * rows : (m + 1) * rows]
            n_ref[g, m] = part
            tot_ref[g, m] = dot(v_aug[:, m * rows : (m + 1) * rows], part[:, :128]).astype(BF16)


def q_kernel(heads, depth, h1_ref, u_ref, w_ref, b_ref, cos_ref, sin_ref, f_ref, qr_ref, pq_ref):
    q_t = project(h1_ref, u_ref, w_ref, b_ref, depth).T
    cos_t, sin_t = cos_ref[...], sin_ref[...]
    for h in range(heads):
        qr = rotate_t(q_t[h * 64 : (h + 1) * 64], cos_t, sin_t).astype(BF16)
        qr_ref[h * 64 : (h + 1) * 64] = qr
        pq_ref[h * 128 : (h + 1) * 128] = features_t(dot(f_ref[h], qr)).astype(BF16)


def pair_masks(has_prev):
    lane = lax.broadcasted_iota(jnp.int32, (64, REPEAT * 128), 1)
    row = lax.broadcasted_iota(jnp.int32, (64, REPEAT * 128), 0)
    low = (lane % 128) < 64
    ahead = row - lane % 64
    value = jnp.where(low, ahead - 1, -ahead)
    hidden = jnp.where(low, (1 - has_prev) * 1024, 0)
    return low, value >= 0, value - hidden >= 0


def heads_side(ref, size, start):
    return jnp.concatenate(
        [ref[h * size : (h + 1) * size, start : start + 128] for h in range(REPEAT)], axis=1
    )


def attend_kernel(micro, prev_ref, n_ref, halo_ref, base_ref, qr_ref, pq_ref,
                  o_ref, ot_ref, den_ref, s_ref):
    rows = n_ref.shape[2]
    low, mask_a, mask_first = pair_masks(prev_ref[0])
    low_row = (lax.broadcasted_iota(jnp.int32, (1, REPEAT * 128), 1) % 128) < 64
    key_lane = lax.broadcasted_iota(jnp.int32, (AUG, 128), 1) < 64
    for m in range(micro):
        ext = jnp.concatenate([halo_ref[0, m], n_ref[0, m]], axis=0)
        ext_t = ext.astype(F32).T.astype(BF16)
        v_aug_all = jnp.concatenate([ext_t[192:256], jnp.ones((AUG - 64, rows + WIN), BF16)], axis=0)
        running = base_ref[0, m]
        for p in range(rows // 128):
            start = m * rows + p * 128
            r0 = p * 128
            qr4 = heads_side(qr_ref, 64, start)
            pq4 = heads_side(pq_ref, 128, start)
            pk = ext[r0 : r0 + 128, :128]
            kr = ext[r0 : r0 + 192, 128:192]
            v_aug = v_aug_all[:, r0 : r0 + 128]
            zero = jnp.zeros_like(v_aug)
            spans = dot(
                jnp.concatenate(
                    [jnp.where(key_lane, v_aug, zero), jnp.where(key_lane, zero, v_aug)], axis=0
                ),
                pk,
            )
            if p == 0:
                running = running - spans[:AUG]
            state = jnp.concatenate([running, running + spans[:AUG]], axis=0).astype(BF16)
            running = running + spans[:AUG] + spans[AUG:]
            s_ref[0, m, p] = state
            from_state = dot(state, pq4)
            scores = dot(kr, qr4) * (1.0 / math.sqrt(HEAD_SIZE))
            linear = dot(pk, pq4)
            exp_a = jnp.exp(jnp.where(low, scores[:64], scores[128:]))
            exp_b = jnp.exp(scores[64:128])
            mask = mask_first if p == 0 else mask_a
            w_a = jnp.where(mask, exp_a, jnp.where(low, linear[:64], 0.0))
            w_b = jnp.where(mask_a, jnp.where(low, 0.0, linear[64:]), exp_b)
            den = (
                jnp.sum(w_a, axis=0, keepdims=True)
                + jnp.sum(w_b, axis=0, keepdims=True)
                + jnp.where(low_row, from_state[64:65], from_state[AUG + 64 : AUG + 65])
            )
            inv = 1.0 / den
            p_a = w_a * inv
            weights = jnp.concatenate(
                [jnp.where(low, p_a, 0.0), w_b * inv, jnp.where(low, 0.0, p_a)], axis=0
            ).astype(BF16)
            out = (
                dot(ext_t[192:256, r0 : r0 + 192], weights)
                + jnp.where(low, from_state[:64], from_state[AUG : AUG + 64]) * inv
            )
            for h in range(REPEAT):
                den_ref[0, h : h + 1, start : start + 128] = den[:, h * 128 : (h + 1) * 128]
            out_t = jnp.concatenate(
                [out[:, h * 128 : (h + 1) * 128] for h in range(REPEAT)], axis=0
            )
            ot_ref[:, start : start + 128] = out_t.astype(BF16)
            o_ref[start : start + 128, :] = out_t.T.astype(BF16)


def attend_back_kernel(micro, prev_ref, n_ref, halo_ref, s_ref, qr_ref, pq_ref, go_ref, ot_ref,
                       den_ref, f_ref, cos_ref, sin_ref,
                       gq_ref, df_ref, gn_ref, gs_ref, gqr_ref, gmq_ref):
    rows = n_ref.shape[2]
    low, mask_a, mask_first = pair_masks(prev_ref[0])
    low_aug = (lax.broadcasted_iota(jnp.int32, (AUG, REPEAT * 128), 1) % 128) < 64
    low_feat = (lax.broadcasted_iota(jnp.int32, (128, REPEAT * 128), 1) % 128) < 64
    scale = 1.0 / math.sqrt(HEAD_SIZE)
    for m in range(micro):
        ext = jnp.concatenate([halo_ref[0, m], n_ref[0, m]], axis=0)
        ext_t = ext.astype(F32).T.astype(BF16)
        tail = None
        for p in range(rows // 128):
            start = m * rows + p * 128
            r0 = p * 128
            qr4 = heads_side(qr_ref, 64, start)
            pq4 = heads_side(pq_ref, 128, start)
            go4 = heads_side(go_ref, 64, start)
            o4 = heads_side(ot_ref, 64, start)
            den = jnp.concatenate(
                [den_ref[0, h : h + 1, start : start + 128] for h in range(REPEAT)], axis=1
            )
            inv = 1.0 / den
            pk = ext[r0 : r0 + 128, :128]
            kr = ext[r0 : r0 + 192, 128:192]
            v = ext[r0 : r0 + 192, 192:256]
            go_f = go4.astype(F32)
            delta = jnp.sum(go_f * o4.astype(F32), axis=0, keepdims=True)
            scores = dot(kr, qr4) * scale
            linear = dot(pk, pq4)
            g_p = dot(v, go4)
            mask = mask_first if p == 0 else mask_a
            exp_a = jnp.exp(jnp.where(low, scores[:64], scores[128:]))
            exp_b = jnp.exp(scores[64:128])
            p_a = jnp.where(mask, exp_a, jnp.where(low, linear[:64], 0.0)) * inv
            p_b = jnp.where(mask_a, jnp.where(low, 0.0, linear[64:]), exp_b) * inv
            weights = jnp.concatenate(
                [jnp.where(low, p_a, 0.0), p_b, jnp.where(low, 0.0, p_a)], axis=0
            ).astype(BF16)
            gw_a = (jnp.where(low, g_p[:64], g_p[128:]) - delta) * inv
            gw_b = (g_p[64:128] - delta) * inv
            gs_a = jnp.where(mask, gw_a * exp_a, 0.0)
            gs_b = jnp.where(mask_a, 0.0, gw_b * exp_b)
            g_scores = jnp.concatenate(
                [jnp.where(low, gs_a, 0.0), gs_b, jnp.where(low, 0.0, gs_a)], axis=0
            ).astype(BF16)
            g_linear = jnp.concatenate(
                [
                    jnp.where(mask_a, 0.0, jnp.where(low, gw_a, 0.0)),
                    jnp.where(mask_a, jnp.where(low, 0.0, gw_b), 0.0),
                ],
                axis=0,
            ).astype(BF16)
            go_aug = jnp.concatenate(
                [go_f * inv, -delta * inv, jnp.zeros((AUG - 65, REPEAT * 128), F32)], axis=0
            )
            go_aug_b = go_aug.astype(BF16)
            gqr = dot(ext_t[128:192, r0 : r0 + 192], g_scores) * scale
            state_t = s_ref[0, m, p].astype(F32).T.astype(BF16)
            gpq = dot(ext_t[:128, r0 : r0 + 128], g_linear) + jnp.where(
                low_feat, dot(state_t[:, :AUG], go_aug_b), dot(state_t[:, AUG:], go_aug_b)
            )
            zero = jnp.zeros_like(go_aug_b)
            gs_ref[0, m, p] = dot_nt(
                jnp.concatenate(
                    [jnp.where(low_aug, go_aug_b, zero), jnp.where(low_aug, zero, go_aug_b)], axis=0
                ),
                pq4,
            )
            g_pk = dot_nt(g_linear, pq4)
            g_kr = dot_nt(g_scores, qr4) * scale
            g_v = dot_nt(weights, go4)
            g_keys = jnp.concatenate(
                [
                    jnp.concatenate([g_pk, jnp.zeros((64, 128), F32)], axis=0),
                    g_kr,
                    g_v,
                ],
                axis=1,
            )
            if tail is None:
                gn_ref[0, m, 0:64] = g_keys[:64]
            else:
                gn_ref[0, m, r0 : r0 + 64] = g_keys[:64] + tail
            gn_ref[0, m, r0 + 64 : r0 + 128] = g_keys[64:128]
            tail = g_keys[128:]
            if p == rows // 128 - 1:
                gn_ref[0, m, rows : rows + 64] = tail
            pq_f = pq4.astype(F32)
            gmq = features_back_t(pq_f, gpq).astype(BF16)
            for h in range(REPEAT):
                gqr_ref[h * 64 : (h + 1) * 64, start : start + 128] = gqr[:, h * 128 : (h + 1) * 128]
                gmq_ref[h * 64 : (h + 1) * 64, start : start + 128] = gmq[:, h * 128 : (h + 1) * 128]
    cos_t, sin_t = cos_ref[...], sin_ref[...]
    grads = []
    for h in range(REPEAT):
        sl = slice(h * 64, (h + 1) * 64)
        gmq = gmq_ref[sl]
        df_ref[0, sl] = dot_nt(qr_ref[sl], gmq)
        grads.append(rotate_back_t(gqr_ref[sl] + dot(f_ref[h], gmq), cos_t, sin_t))
    gq_ref[0] = jnp.concatenate(grads, axis=0).T.astype(BF16)


def kv_back_kernel(kv_heads, micro, gn_ref, ghalo_ref, n_ref, gs_ref, next_ref, f_ref, cos_ref,
                   sin_ref, gkv_ref, df_ref):
    rows = n_ref.shape[2]
    spans = rows // WIN
    cos_t, sin_t = cos_ref[...], sin_ref[...]
    keys, values = [], []
    unit = (lax.broadcasted_iota(jnp.int32, (64, AUG - 64), 1) == 0).astype(BF16)
    for g in range(kv_heads):
        parts = []
        for m in range(micro):
            natural = n_ref[g, m]
            later = [None] * spans
            later[spans - 1] = next_ref[g, m, 1]
            later[spans - 2] = next_ref[g, m, 0]
            for c in range(spans - 3, -1, -1):
                later[c] = later[c + 1] + gs_ref[g, m, (c + 2) // 2, ((c + 2) % 2) * AUG : ((c + 2) % 2 + 1) * AUG]
            for c in range(spans):
                part = natural[c * 64 : (c + 1) * 64]
                grad = gn_ref[g, m, 64 + c * 64 : 128 + c * 64]
                if c == spans - 1:
                    grad = grad + ghalo_ref[g, m].astype(F32)
                big = later[c].astype(BF16)
                g_pk = dot(jnp.concatenate([part[:, 192:256], unit], axis=1), big)
                g_v = dot_nt(part[:, :128], big[:64])
                parts.append(
                    grad + jnp.concatenate([g_pk, jnp.zeros((64, 64), F32), g_v], axis=1)
                )
        grad_t = jnp.concatenate(parts, axis=0).T
        nat_t = jnp.concatenate([n_ref[g, m, :, :192] for m in range(micro)], axis=0).astype(F32).T
        gmk = features_back_t(nat_t[:128], grad_t[:128]).astype(BF16)
        df_ref[0, g * 64 : (g + 1) * 64] = dot_nt(nat_t[128:].astype(BF16), gmk)
        keys.append(rotate_back_t(grad_t[128:192] + dot(f_ref[g], gmk), cos_t, sin_t))
        values.append(grad_t[192:256])
    gkv_ref[0] = jnp.concatenate(keys + values, axis=0).T.astype(BF16)


def out_kernel(shards, depth, o_ref, w_ref, ao_ref, bo_ref, x_ref, gain_ref,
               x2_ref, h2_ref, uo_ref, r2_ref, x2_all, sq_ref):
    j = pl.program_id(0)
    last = pl.num_programs(0) - 1

    @pl.when(j == 0)
    def _():
        uo_ref[...] = dot(o_ref[...], ao_ref[...]).astype(BF16)
        sq_ref[...] = jnp.zeros_like(sq_ref)

    total = dot_nt(uo_ref[...], bo_ref[...])
    halves = w_ref.shape[3] // depth
    for f in range(shards):
        for a in range(halves):
            e0 = (f * halves + a) * depth
            total += dot(o_ref[:, e0 : e0 + depth], w_ref[0, f, :, a * depth : (a + 1) * depth])
    x2 = x_ref[...].astype(F32) + total
    x2_ref[...] = x2
    x2_all[j] = x2
    sq_ref[...] += jnp.sum(x2 * x2, axis=1, keepdims=True)

    @pl.when(j == last)
    def _():
        width = depth * x2_all.shape[0]
        r2 = lax.rsqrt(sq_ref[...] * (1.0 / width) + EPSILON)
        r2_ref[...] = r2
        for i in range(x2_all.shape[0]):
            cols = slice(i * depth, (i + 1) * depth)
            h2_ref[:, cols] = (x2_all[i] * r2 * gain_ref[:, cols]).astype(BF16)


def go_kernel(depth, gb_ref, w_ref, ao_ref, guo_ref, go_ref):
    groups = w_ref.shape[0]
    halves = w_ref.shape[3] // depth
    low_rank = dot_nt(ao_ref[...], guo_ref[...])
    for a in range(halves):
        total = low_rank[a * depth : (a + 1) * depth]
        for j in range(groups):
            total += dot_nt(
                w_ref[j, 0, :, a * depth : (a + 1) * depth], gb_ref[:, j * depth : (j + 1) * depth]
            )
        go_ref[a * depth : (a + 1) * depth] = total.astype(BF16)


def gx_kernel(shards, depth, gq_ref, gkv_ref, wq_ref, wkv_ref, gu_ref, a_ref, x_ref, x_all_ref,
              gx2_ref, r1_ref, gain_ref, gx_ref, dg_ref, gh_all, dot_ref):
    j = pl.program_id(0)
    last = pl.num_programs(0) - 1

    @pl.when(j == 0)
    def _():
        dot_ref[...] = jnp.zeros_like(dot_ref)

    total = dot_nt(gu_ref[...], a_ref[...])
    for f in range(shards):
        total += dot_nt(gq_ref[f], wq_ref[0, f])
        total += dot_nt(gkv_ref[f], wkv_ref[0, f])
    gh_all[j] = total
    hx = total * x_ref[...].astype(F32)
    dg_ref[...] = jnp.sum(hx * r1_ref[...], axis=0, keepdims=True)
    dot_ref[...] += jnp.sum(hx * gain_ref[0], axis=1, keepdims=True)

    @pl.when(j == last)
    def _():
        count = gh_all.shape[0]
        r1 = r1_ref[...]
        back = r1 * r1 * r1 * dot_ref[...] * (1.0 / (count * depth))
        for i in range(count):
            cols = slice(i * depth, (i + 1) * depth)
            gx_ref[:, cols] = (
                gx2_ref[:, cols]
                + r1 * gain_ref[i] * gh_all[i]
                - x_all_ref[:, cols].astype(F32) * back
            ).astype(BF16)


def ffn_kernel(depth, h2_ref, gy_ref, wg_ref, wu_ref, wd_ref, out_ref, gh_ref, out_acc, gh_acc):
    j = pl.program_id(1)
    last = pl.num_programs(1) - 1
    groups = wd_ref.shape[0]
    gate = dot(h2_ref[...], wg_ref[...])
    up = dot(h2_ref[...], wu_ref[...])
    g_hid = dot_nt(gy_ref[:, :depth], wd_ref[0])
    for i in range(1, groups):
        g_hid += dot_nt(gy_ref[:, i * depth : (i + 1) * depth], wd_ref[i])
    sig = 1.0 / (1.0 + jnp.exp(-gate))
    silu = gate * sig
    hid = (silu * up).astype(BF16)
    g_gate = (g_hid * up * sig * (1.0 + gate * (1.0 - sig))).astype(BF16)
    g_up = (g_hid * silu).astype(BF16)
    g_h2 = dot_nt(g_gate, wg_ref[...]) + dot_nt(g_up, wu_ref[...])

    @pl.when(j == 0)
    def _():
        gh_acc[...] = g_h2
        for i in range(groups):
            out_acc[:, i * depth : (i + 1) * depth] = dot(hid, wd_ref[i])

    @pl.when(j > 0)
    def _():
        gh_acc[...] += g_h2
        for i in range(groups):
            out_acc[:, i * depth : (i + 1) * depth] += dot(hid, wd_ref[i])

    @pl.when(j == last)
    def _():
        gh_ref[...] = gh_acc[...].astype(BF16)
        out_ref[...] = out_acc[...].astype(BF16)


def ffn(h2, gy, wg, wu, wd):
    total, width = h2.shape
    hidden = wg.shape[1]
    groups, _, depth = wd.shape
    row_tile = min(512, total)
    hid_tile = min(512, hidden)
    grid = (total // row_tile, hidden // hid_tile)
    return pl.pallas_call(
        functools.partial(ffn_kernel, depth),
        grid=grid,
        in_specs=[
            pl.BlockSpec((row_tile, width), lambda r, j: (r, 0)),
            pl.BlockSpec((row_tile, width), lambda r, j: (r, 0)),
            pl.BlockSpec((width, hid_tile), lambda r, j: (0, j)),
            pl.BlockSpec((width, hid_tile), lambda r, j: (0, j)),
            pl.BlockSpec((groups, hid_tile, depth), lambda r, j: (0, j, 0)),
        ],
        out_specs=[
            pl.BlockSpec((row_tile, width), lambda r, j: (r, 0)),
            pl.BlockSpec((row_tile, width), lambda r, j: (r, 0)),
        ],
        out_shape=[jax.ShapeDtypeStruct((total, width), BF16)] * 2,
        scratch_shapes=[pltpu.VMEM((row_tile, width), F32)] * 2,
        compiler_params=params(58, ("arbitrary", "arbitrary")),
        cost_estimate=cost(12 * total * width * hidden, 2 * (4 * total * width + 3 * grid[0] * width * hidden)),
        name="feed_forward",
    )(h2, gy, wg, wu, wd)


def shift_sum(array, axis_name, size, direction):
    total = None
    for step in range(1, size):
        if direction > 0:
            perm = [(i, i + step) for i in range(size - step)]
        else:
            perm = [(i + step, i) for i in range(size - step)]
        moved = lax.ppermute(array, axis_name, perm).astype(F32)
        total = moved if total is None else total + moved
    return total


def deal(rows, order):
    micro, count, width = rows.shape
    groups = order.shape[1]
    pieces = rows.reshape(micro, groups, count // groups, width).transpose(1, 0, 2, 3)
    spread = lax.all_to_all(pieces, "dp", split_axis=0, concat_axis=0, tiled=True)
    ordered = jnp.stack(
        [
            jnp.stack([lax.dynamic_index_in_dim(spread, order[m, j], 0, keepdims=False)[m] for m in range(micro)])
            for j in range(groups)
        ]
    )
    settled = lax.all_to_all(ordered, "dp", split_axis=0, concat_axis=0, tiled=True)
    return settled.transpose(1, 0, 2, 3).reshape(micro, count, width)


def shards(
    inputs, cotangent, lengths, dealing, wq, wk, wv, wo, wg, wu, wd,
    down_ad, up_qo, up_kv, fmap_q, fmap_k, gains,
):
    n_dp = lax.axis_size("dp")
    n_f = lax.axis_size("fsdp")
    group = lax.axis_index("dp")
    quarter = lax.axis_index("fsdp")
    micro, rows, width = inputs.shape[1:]
    total = micro * rows
    depth = wq.shape[0]
    q_cols, k_cols = wq.shape[1], wk.shape[1]
    kv_heads = k_cols // HEAD_SIZE
    heads = q_cols // HEAD_SIZE
    halves = wo.shape[0] // depth
    n_all = n_dp * n_f
    x = inputs[0].reshape(total, width)

    small_parts = [down_ad, up_qo, up_kv, fmap_q, fmap_k, gains]
    flat = jnp.concatenate([part.reshape(-1) for part in small_parts])
    pack_cols = 2 * q_cols + 2 * k_cols
    small_rows = -(-flat.shape[0] // pack_cols)
    small_rows = -(-small_rows // 16) * 16
    flat = jnp.pad(flat, (0, small_rows * pack_cols - flat.shape[0])).reshape(small_rows, pack_cols)
    wo_side = jnp.concatenate([wo[a * depth : (a + 1) * depth] for a in range(halves)], axis=1)
    packed = jnp.concatenate([jnp.concatenate([wq, wo_side, wk, wv], axis=1), flat], axis=0)
    gathered = lax.all_gather(packed, ("dp", "fsdp"), axis=0, tiled=False)
    gathered = gathered.reshape(n_dp, n_f, depth + small_rows, pack_cols)
    small = gathered[:, :, depth:].reshape(n_all, small_rows * pack_cols)
    at = 0
    fetched = []
    for part in small_parts:
        fetched.append(
            small[:, at : at + part.size].reshape((n_all * part.shape[0],) + part.shape[1:])
        )
        at += part.size
    down_ad, up_qo, up_kv, fmap_q, fmap_k, gains = fetched
    gain_one = gains[:, 0].astype(F32)
    gain_two = gains[:, 1].astype(F32)

    wg_all = lax.all_gather(wg, "dp", axis=0, tiled=True)
    wu_all = lax.all_gather(wu, "dp", axis=0, tiled=True)
    wd_all = lax.all_gather(wd, "dp", axis=0, tiled=False)

    cot = deal(cotangent[0], dealing)
    positions = quarter * rows + jnp.arange(rows, dtype=jnp.int32)
    seq_len = lax.dynamic_index_in_dim(lengths, group, 0, keepdims=False)
    valid = positions[None, :] < seq_len[:, None]
    gy = jnp.where(valid[:, :, None], cot, jnp.zeros_like(cot)).reshape(total, width)
    gy_all = lax.all_gather(gy, "fsdp", axis=0, tiled=True)

    xf = x.astype(F32)
    r1 = lax.rsqrt(jnp.mean(xf * xf, axis=-1, keepdims=True) + EPSILON)
    h1 = (xf * r1 * gain_one).astype(BF16)
    rank = ADAPTER_RANK
    lanes = RANK_LANES
    a_qkv = jnp.pad(down_ad[:, : 3 * rank], ((0, 0), (0, lanes - 3 * rank)))
    a_o = jnp.pad(down_ad[:, 3 * rank :], ((0, 0), (0, lanes - rank)))
    u = dot(h1, a_qkv).astype(BF16)
    b_q = up_qo[:, :rank].reshape(n_f, q_cols, rank)
    b_k = up_kv[:, :rank].reshape(n_f, k_cols, rank)
    b_v = up_kv[:, rank:].reshape(n_f, k_cols, rank)
    b_o = jnp.pad(up_qo[:, rank:], ((0, 0), (0, lanes - rank)))

    def placed(block, at):
        return jnp.pad(block.transpose(0, 2, 1), ((0, 0), (at, lanes - at - rank), (0, 0)))

    b_q_t = placed(b_q, 0)
    b_kv_t = jnp.concatenate([placed(b_k, rank), placed(b_v, 2 * rank)], axis=2)
    fq = fmap_q.reshape(H, HEAD_SIZE, HEAD_SIZE)
    fk = fmap_k.reshape(KEY_VALUE_HEADS, HEAD_SIZE, HEAD_SIZE)
    fq_t = jnp.concatenate([fq.transpose(0, 2, 1), -fq.transpose(0, 2, 1)], axis=1)
    fk_t = jnp.concatenate([fk.transpose(0, 2, 1), -fk.transpose(0, 2, 1)], axis=1)
    cos_t, sin_t = rope_tables_t(jnp.tile(positions, micro))
    spans = rows // WIN
    pairs = rows // 128
    w_rows = depth + small_rows

    kv_natural, totals = pl.pallas_call(
        functools.partial(kv_kernel, kv_heads, micro, depth),
        grid=(n_f,),
        in_specs=[
            whole((total, width)),
            whole((total, lanes)),
            pl.BlockSpec((n_dp, 1, depth, 2 * k_cols), lambda f: (0, f, 0, q_cols // k_cols)),
            pl.BlockSpec((1, lanes, 2 * k_cols), lambda f: (f, 0, 0)),
            whole((32, total)),
            whole((32, total)),
            pl.BlockSpec((kv_heads, 128, 64), lambda f: (f, 0, 0)),
        ],
        out_specs=[
            pl.BlockSpec((kv_heads, micro, rows, 256), lambda f: (f, 0, 0, 0)),
            pl.BlockSpec((kv_heads, micro, AUG, 128), lambda f: (f, 0, 0, 0)),
        ],
        out_shape=[
            jax.ShapeDtypeStruct((KEY_VALUE_HEADS, micro, rows, 256), BF16),
            jax.ShapeDtypeStruct((KEY_VALUE_HEADS, micro, AUG, 128), BF16),
        ],
        compiler_params=params(40),
        cost_estimate=cost(4 * total * width * k_cols * n_f, 2 * (total * width + 2 * width * k_cols * n_f), 128 * 8 * total),
        name="key_value",
    )(h1, u, gathered, b_kv_t, cos_t, sin_t, fk_t)

    forward_one = [(i, i + 1) for i in range(n_f - 1)]
    backward_one = [(i + 1, i) for i in range(n_f - 1)]
    halo = lax.ppermute(kv_natural[:, :, rows - WIN :], "fsdp", forward_one)
    base = shift_sum(totals, "fsdp", n_f, 1)

    q_rot, q_feat = pl.pallas_call(
        functools.partial(q_kernel, heads, depth),
        grid=(n_f,),
        in_specs=[
            whole((total, width)),
            whole((total, lanes)),
            pl.BlockSpec((n_dp, 1, depth, q_cols), lambda f: (0, f, 0, 0)),
            pl.BlockSpec((1, lanes, q_cols), lambda f: (f, 0, 0)),
            whole((32, total)),
            whole((32, total)),
            pl.BlockSpec((heads, 128, 64), lambda f: (f, 0, 0)),
        ],
        out_specs=[
            pl.BlockSpec((q_cols, total), lambda f: (f, 0)),
            pl.BlockSpec((2 * q_cols, total), lambda f: (f, 0)),
        ],
        out_shape=[
            jax.ShapeDtypeStruct((H * 64, total), BF16),
            jax.ShapeDtypeStruct((H * 128, total), BF16),
        ],
        compiler_params=params(40),
        cost_estimate=cost(2 * total * width * q_cols * n_f, 2 * (total * width + width * q_cols * n_f + 3 * total * 2048), 128 * 32 * total),
        name="query",
    )(h1, u, gathered, b_q_t, cos_t, sin_t, fq_t)

    has_prev = (quarter > 0).astype(jnp.int32).reshape(1)
    g4 = REPEAT * 64
    prev_spec = pl.BlockSpec(memory_space=pltpu.SMEM)
    n_spec = pl.BlockSpec((1, micro, rows, 256), lambda g: (g, 0, 0, 0))
    halo_spec = pl.BlockSpec((1, micro, WIN, 256), lambda g: (g, 0, 0, 0))
    state_spec = pl.BlockSpec((1, micro, pairs, 2 * AUG, 128), lambda g: (g, 0, 0, 0, 0))
    head_spec = pl.BlockSpec((g4, total), lambda g: (g, 0))
    feat_spec = pl.BlockSpec((2 * g4, total), lambda g: (g, 0))
    den_spec = pl.BlockSpec((1, 8, total), lambda g: (g, 0, 0))
    attend_flops = H * total * 2 * (192 * 64 + 128 * 128 + 160 * 128 + 192 * 64)
    o, o_t, den, states = pl.pallas_call(
        functools.partial(attend_kernel, micro),
        grid=(KEY_VALUE_HEADS,),
        in_specs=[
            prev_spec,
            n_spec,
            halo_spec,
            pl.BlockSpec((1, micro, AUG, 128), lambda g: (g, 0, 0, 0)),
            head_spec,
            feat_spec,
        ],
        out_specs=[pl.BlockSpec((total, g4), lambda g: (0, g)), head_spec, den_spec, state_spec],
        out_shape=[
            jax.ShapeDtypeStruct((total, H * 64), BF16),
            jax.ShapeDtypeStruct((H * 64, total), BF16),
            jax.ShapeDtypeStruct((KEY_VALUE_HEADS, 8, total), F32),
            jax.ShapeDtypeStruct((KEY_VALUE_HEADS, micro, pairs, 2 * AUG, 128), BF16),
        ],
        compiler_params=params(40),
        cost_estimate=cost(attend_flops, 14 * MIB, 128 * H * total),
        name="attend",
    )(has_prev, kv_natural, halo, base, q_rot, q_feat)

    x2, h2, uo, r2 = pl.pallas_call(
        functools.partial(out_kernel, n_f, depth),
        grid=(n_dp,),
        in_specs=[
            whole((total, H * 64)),
            pl.BlockSpec((1, n_f, depth, q_cols), lambda j: (j, 0, 0, 1)),
            whole((H * 64, lanes)),
            pl.BlockSpec((depth, lanes), lambda j: (j, 0)),
            pl.BlockSpec((total, depth), lambda j: (0, j)),
            whole((1, width)),
        ],
        out_specs=[
            pl.BlockSpec((total, depth), lambda j: (0, j)),
            whole((total, width)),
            whole((total, lanes)),
            whole((total, 1)),
        ],
        out_shape=[
            jax.ShapeDtypeStruct((total, width), F32),
            jax.ShapeDtypeStruct((total, width), BF16),
            jax.ShapeDtypeStruct((total, lanes), BF16),
            jax.ShapeDtypeStruct((total, 1), F32),
        ],
        scratch_shapes=[pltpu.VMEM((n_dp, total, depth), F32), pltpu.VMEM((total, 1), F32)],
        compiler_params=params(40),
        cost_estimate=cost(2 * total * width * H * 64, 20 * MIB),
        name="output_projection",
    )(o, gathered, a_o, b_o, x, gain_two.reshape(1, width))

    h2_all = lax.all_gather(h2, "fsdp", axis=0, tiled=True)
    down_part, gh2_part = ffn(h2_all, gy_all, wg_all, wu_all, wd_all)

    def scatter(part):
        moved = lax.all_to_all(
            part.reshape(n_f, total, width), "fsdp", split_axis=0, concat_axis=0, tiled=True
        )
        return jnp.sum(moved.astype(F32), axis=0)

    gh2 = scatter(gh2_part)
    result = x2 + scatter(down_part)
    result = jnp.where(valid.reshape(total, 1), result, 0.0).astype(BF16)
    inverse = jnp.argsort(dealing, axis=1).astype(jnp.int32)
    output = deal(result.reshape(micro, rows, width), inverse)

    dg2 = jnp.sum(gh2 * x2 * r2, axis=0)
    gx2 = (
        gy.astype(F32)
        + r2 * gain_two * gh2
        - x2 * r2**3 * jnp.mean(gain_two * gh2 * x2, axis=-1, keepdims=True)
    )
    gb = gx2.astype(BF16)
    guo = dot(gb, b_o).astype(BF16)
    d_bo = lax.dot_general(gb, uo[:, :rank], (((0,), (0,)), ((), ())), preferred_element_type=F32)

    go_t = pl.pallas_call(
        functools.partial(go_kernel, depth),
        grid=(n_f,),
        in_specs=[
            whole((total, width)),
            pl.BlockSpec((n_dp, 1, depth, q_cols), lambda f: (0, f, 0, 1)),
            pl.BlockSpec((q_cols, lanes), lambda f: (f, 0)),
            whole((total, lanes)),
        ],
        out_specs=pl.BlockSpec((q_cols, total), lambda f: (f, 0)),
        out_shape=jax.ShapeDtypeStruct((H * 64, total), BF16),
        compiler_params=params(40),
        cost_estimate=cost(2 * total * width * H * 64, 12 * MIB),
        name="output_projection_back",
    )(gb, gathered, a_o, guo)
    d_ao = dot(o_t, guo[:, :rank])

    gq, d_fq, g_keys, g_states = pl.pallas_call(
        functools.partial(attend_back_kernel, micro),
        grid=(KEY_VALUE_HEADS,),
        in_specs=[
            prev_spec,
            n_spec,
            halo_spec,
            state_spec,
            head_spec,
            feat_spec,
            head_spec,
            head_spec,
            den_spec,
            pl.BlockSpec((REPEAT, 64, 64), lambda g: (g, 0, 0)),
            whole((32, total)),
            whole((32, total)),
        ],
        out_specs=[
            pl.BlockSpec((1, total, g4), lambda g: (g * g4 // q_cols, 0, g % (q_cols // g4))),
            pl.BlockSpec((1, g4, 64), lambda g: (g, 0, 0)),
            pl.BlockSpec((1, micro, rows + WIN, 256), lambda g: (g, 0, 0, 0)),
            state_spec,
        ],
        out_shape=[
            jax.ShapeDtypeStruct((n_f, total, q_cols), BF16),
            jax.ShapeDtypeStruct((KEY_VALUE_HEADS, g4, 64), F32),
            jax.ShapeDtypeStruct((KEY_VALUE_HEADS, micro, rows + WIN, 256), F32),
            jax.ShapeDtypeStruct((KEY_VALUE_HEADS, micro, pairs, 2 * AUG, 128), F32),
        ],
        scratch_shapes=[pltpu.VMEM((g4, total), F32), pltpu.VMEM((g4, total), BF16)],
        compiler_params=params(50),
        cost_estimate=cost(3 * attend_flops, 24 * MIB, 128 * H * total),
        name="attend_back",
    )(has_prev, kv_natural, halo, states, q_rot, q_feat, go_t, o_t, den, fq, cos_t, sin_t)

    g_halo = lax.ppermute(g_keys[:, :, :WIN].astype(BF16), "fsdp", backward_one)
    g_total = jnp.sum(g_states[:, :, :, :AUG] + g_states[:, :, :, AUG:], axis=2)
    g_first = g_states[:, :, 0, :AUG]
    g_next = shift_sum(g_total.astype(BF16), "fsdp", n_f, -1)
    g_first_next = lax.ppermute(g_first.astype(BF16), "fsdp", backward_one).astype(F32)
    g_later = jnp.stack([g_next, g_next - g_first_next], axis=2)

    gkv, d_fk = pl.pallas_call(
        functools.partial(kv_back_kernel, kv_heads, micro),
        grid=(n_f,),
        in_specs=[
            pl.BlockSpec((kv_heads, micro, rows + WIN, 256), lambda f: (f, 0, 0, 0)),
            pl.BlockSpec((kv_heads, micro, WIN, 256), lambda f: (f, 0, 0, 0)),
            pl.BlockSpec((kv_heads, micro, rows, 256), lambda f: (f, 0, 0, 0)),
            pl.BlockSpec((kv_heads, micro, pairs, 2 * AUG, 128), lambda f: (f, 0, 0, 0, 0)),
            pl.BlockSpec((kv_heads, micro, 2, AUG, 128), lambda f: (f, 0, 0, 0, 0)),
            pl.BlockSpec((kv_heads, 64, 64), lambda f: (f, 0, 0)),
            whole((32, total)),
            whole((32, total)),
        ],
        out_specs=[
            pl.BlockSpec((1, total, 2 * k_cols), lambda f: (f, 0, 0)),
            pl.BlockSpec((1, k_cols, 64), lambda f: (f, 0, 0)),
        ],
        out_shape=[
            jax.ShapeDtypeStruct((n_f, total, 2 * k_cols), BF16),
            jax.ShapeDtypeStruct((n_f, k_cols, 64), F32),
        ],
        compiler_params=params(40),
        cost_estimate=cost(8 * total * 128 * 128, 8 * MIB),
        name="key_value_back",
    )(g_keys, g_halo, kv_natural, g_states, g_later, fk, cos_t, sin_t)

    gk, gv = gkv[:, :, :k_cols], gkv[:, :, k_cols:]

    def ranks(grad, up):
        return jnp.einsum("fte,fer->tr", grad, up, preferred_element_type=F32)

    def outer(grad, at):
        out = jnp.einsum("fte,tr->fer", grad, u[:, at : at + rank], preferred_element_type=F32)
        return out.reshape(-1, rank)

    gu = jnp.concatenate([ranks(gq, b_q), ranks(gk, b_k), ranks(gv, b_v)], axis=1).astype(BF16)
    d_bq, d_bk, d_bv = outer(gq, 0), outer(gk, rank), outer(gv, 2 * rank)
    d_qkv = lax.dot_general(h1, gu, (((0,), (0,)), ((), ())), preferred_element_type=F32)
    gu = jnp.pad(gu, ((0, 0), (0, lanes - 3 * rank)))

    gx, dg1 = pl.pallas_call(
        functools.partial(gx_kernel, n_f, depth),
        grid=(n_dp,),
        in_specs=[
            whole((n_f, total, q_cols)),
            whole((n_f, total, 2 * k_cols)),
            pl.BlockSpec((1, n_f, depth, q_cols), lambda j: (j, 0, 0, 0)),
            pl.BlockSpec((1, n_f, depth, 2 * k_cols), lambda j: (j, 0, 0, q_cols // k_cols)),
            whole((total, lanes)),
            pl.BlockSpec((depth, lanes), lambda j: (j, 0)),
            pl.BlockSpec((total, depth), lambda j: (0, j)),
            whole((total, width)),
            whole((total, width)),
            whole((total, 1)),
            whole((n_dp, 1, depth)),
        ],
        out_specs=[whole((total, width)), pl.BlockSpec((1, depth), lambda j: (0, j))],
        out_shape=[
            jax.ShapeDtypeStruct((total, width), BF16),
            jax.ShapeDtypeStruct((1, width), F32),
        ],
        scratch_shapes=[pltpu.VMEM((n_dp, total, depth), F32), pltpu.VMEM((total, 1), F32)],
        compiler_params=params(56),
        cost_estimate=cost(2 * total * width * 3072, 30 * MIB),
        name="input_gradient",
    )(gq, gkv, gathered, gathered, gu, a_qkv, x, x, gx2, r1, gain_one.reshape(n_dp, 1, depth))

    grads = [
        jnp.concatenate([d_qkv, d_ao], axis=1),
        jnp.concatenate([d_bq, d_bo], axis=1),
        jnp.concatenate([d_bk, d_bv], axis=1),
        d_fq.reshape(H * 64, 64),
        d_fk.reshape(KEY_VALUE_HEADS * 64, 64),
        jnp.stack([dg1[0], dg2], axis=1),
    ]
    flat = jnp.concatenate([grad.reshape(n_all, -1) for grad in grads], axis=1)
    columns = flat.shape[1]
    padded = -(-columns // 1024) * 1024
    flat = jnp.pad(flat, ((0, 0), (0, padded - columns))).reshape(n_all, padded // 128, 128)
    moved = lax.all_to_all(flat, ("dp", "fsdp"), split_axis=0, concat_axis=0, tiled=True)
    mine = jnp.sum(moved, axis=0).reshape(-1)
    shares = []
    at = 0
    for grad in grads:
        size = grad.size // n_all
        shares.append(mine[at : at + size].reshape(grad.shape[0] // n_all, grad.shape[1]))
        at += size
    return (output[None], gx.reshape(1, micro, rows, width), *shares)


def solution(mesh):
    every = ("dp", "fsdp")
    blocks = P("dp", None, "fsdp", None)
    in_specs = (
        blocks,
        blocks,
        P(),
        P(),
        P("dp", "fsdp"),
        P("dp", "fsdp"),
        P("dp", "fsdp"),
        P("fsdp", "dp"),
        P("dp", "fsdp"),
        P("dp", "fsdp"),
        P("fsdp", "dp"),
    ) + (P(every, None),) * 6
    out_specs = (blocks, blocks) + (P(every, None),) * 6
    return jax.shard_map(shards, mesh=mesh, in_specs=in_specs, out_specs=out_specs, check_vma=False)
```

time: 4160 us -> 1230 us (0.30)
  waiting for transfers between devices: 1880 us -> 626 us
  blocking collectives: 1330 us -> 101 us
  matrix products: 587 us -> 6.24 us
  Pallas kernels: 0 us -> 234 us
  other arithmetic: 156 us -> 46.7 us
  local copies, waits for them, and re-layouts: 140 us -> 79.1 us
  between operations: 19.5 us -> 76.5 us
    all_gather x24 -> x0, blocking collectives: 1300 us -> none  [the longest x3 208 us: fetch_small(): lax.all_gather(local_adapter_weights[5], ('dp', 'fsdp'), axis=0, tiled=True)]
    dot_general x140 -> x11, matrix products: 573 us -> 6.24 us  [the longest x3 2.71 us: dot(): lax.dot_general(a, b, (((1,), (0,)), ((), ())), preferred_element_type=F32)]
    reduce_scatter x14 -> x0, waiting for transfers between devices: 532 us -> none  [the longest x4 185 us: rows_out_pair(): lax.psum_scatter(wide_part, 'fsdp', scatter_dimension=0, tiled=True)]
    all_gather x23 -> x6, waiting for transfers between devices: 805 us -> 336 us  [the longest x1 89.9 us: shards(): h2_all = lax.all_gather(h2, 'fsdp', axis=0, tiled=True)]
    unnamed x45 -> x6, waiting for transfers between devices: 461 us -> 1.95 us
    pallas_call x0 -> x9, Pallas kernels: none -> 234 us  [the longest x1 125 us: ffn(): pl.pallas_call(functools.partial(ffn_kernel, depth), grid=grid, in_specs=...]
    all_to_all x4 -> x2, waiting for transfers between devices: 40.7 us -> 144 us  [deal(): lax.all_to_all(ordered, 'dp', split_axis=0, concat_axis=0, tiled=True)]
    all_to_all x0 -> x2, waiting for transfers between devices: none -> 78.6 us  [the longest x1 78.6 us: scatter(): lax.all_to_all(part.reshape(n_f, total, width), 'fsdp', split_axis=0, con...]
  transfers between devices with their start and end apart: 48 -> 21, of which waited for: 29 -> 11; matrix products, arithmetic and copies ran while one was open for 20% -> 7% of each run, Pallas kernels for 0% -> 6%
where the time goes in v1:
time: 1230 us; the launch traced here: 1220 us
  waiting for transfers between devices  626 us (51%)
  Pallas kernels  234 us (19%)
  blocking collectives  101 us (8%)
  local copies, waits for them, and re-layouts  79.1 us (6%)
  between operations  76.5 us (6%)
  starting transfers between devices  53.1 us (4%)
  other arithmetic  46.7 us (4%)
    all_to_all x2, waiting for transfers between devices, deal(): lax.all_to_all(ordered, 'dp', split_axis=0, concat_axis=0, tiled=True)  144 us
    pallas_call x1, Pallas kernels, ffn(): pl.pallas_call(functools.partial(ffn_kernel, depth), grid=grid, in_specs=...  125 us
    all_to_all x1, blocking collectives, scatter(): lax.all_to_all(part.reshape(n_f, total, width), 'fsdp', split_axis=0, con...  101 us
    all_gather x1, waiting for transfers between devices, shards(): h2_all = lax.all_gather(h2, 'fsdp', axis=0, tiled=True)  89.9 us
    all_gather x1, waiting for transfers between devices, shards(): gy_all = lax.all_gather(gy, 'fsdp', axis=0, tiled=True)  87.9 us
    all_gather x1, waiting for transfers between devices, shards(): wd_all = lax.all_gather(wd, 'dp', axis=0, tiled=False)  82.1 us
    all_to_all x1, waiting for transfers between devices, scatter(): lax.all_to_all(part.reshape(n_f, total, width), 'fsdp', split_axis=0, con...  78.6 us
    all_gather x1, waiting for transfers between devices, shards(): wu_all = lax.all_gather(wu, 'dp', axis=0, tiled=True)  72.8 us
  transfers between devices with their start and end apart: 21, of which 11 were waited for; matrix products, arithmetic and copies ran while one was open for 7% of the time, Pallas kernels for 6%

profile of v1, /device:TPU:0, one launch (start us, length us, event | category | flops | bytes accessed | tf_op | source)
XLA Modules:
  0.0 1221.9 jit_solution(9679861989087577261)
XLA Ops:
  22.3 6.5 all-to-all-start
  59.6 58.7 %all-to-all-done = bf16[8,2,32,2048]{3,2,1,0:T(8,128)(2,1)S(1)} async-done(((bf16[8,2,32,2048]{3,2,1,0:T(8,128)(2,1)}), bf16[8,2,32,2048]{3,2,1,0:T(8,128)(2,1)S(1)}, u32[]{:S(2)}, u32[]{:S(2)}) %all-to-all-start) | async-done | bytes 2097184 | tf_op jit(solution)/shard_map/all_to_all | solution.py:492
  128.8 99.8 %all-to-all-done.1 = bf16[8,2,32,2048]{3,2,1,0:T(8,128)(2,1)S(1)} async-done(((bf16[8,2,32,2048]{3,2,1,0:T(8,128)(2,1)}), bf16[8,2,32,2048]{3,2,1,0:T(8,128)(2,1)S(1)}, u32[]{:S(2)}, u32[]{:S(2)}) %all-to-all-start.1) | async-done | bytes 2097184 | tf_op jit(solution)/shard_map/all_to_all | solution.py:499
  246.0 9.0 key_value.1
  279.6 11.3 query.1
  295.1 18.3 %attend.1 = (bf16[512,2048]{1,0:T(8,128)(2,1)S(1)}, bf16[2048,512]{1,0:T(8,128)(2,1)S(1)}, f32[8,8,512]{2,1,0:T(8,128)S(1)}, bf16[8,2,2,160,128]{4,3,2,1,0:T(8,128)(2,1)S(1)}) custom-call(s32[1]{0:T(128)} %bitcast.prev_ref, bf16[8,2,256,256]{3,2,1,0:T(8,128)(2,1)S(1)} %copy-done.9, bf16[8,2,64,256]{3,2,1,0:T(8,128)(2,1)} %collective-permute-done.halo_ref, ...), custom_call_target="tpu_custom_call" | custom-call | flops 2013265920 | bytes 14680064 | tf_op jit(solution)/shard_map/attend/pallas_call | solution.py:646
  314.7 11.4 output_projection.1
  330.4 72.8 %all-gather.15.cloned.1.call-done.wu_ref = bf16[2048,2048]{1,0:T(8,128)(2,1)} async-done(((bf16[256,2048]{1,0:T(8,128)(2,1)}), bf16[2048,2048]{1,0:T(8,128)(2,1)}) %all-gather.15.cloned.1.call-update) | async-done | bytes 8388624 | tf_op jit(solution)/shard_map/all_gather | solution.py:544
  403.1 82.1 %all-gather.19.cloned.1.call-done = bf16[16384,256]{1,0:T(8,128)(2,1)} async-done(((bf16[2048,256]{1,0:T(8,128)(2,1)}), bf16[16384,256]{1,0:T(8,128)(2,1)}) %all-gather.19.cloned.1.call-update) | async-done | bytes 8388624 | tf_op jit(solution)/shard_map/all_gather | solution.py:545
  485.2 87.9 %all-gather.11.cloned.1.call-done.gy_ref = bf16[2048,2048]{1,0:T(8,128)(2,1)} async-done(((bf16[512,2048]{1,0:T(8,128)(2,1)}), bf16[2048,2048]{1,0:T(8,128)(2,1)}) %all-gather.11.cloned.1.call-update) | async-done | bytes 8388624 | tf_op jit(solution)/shard_map/all_gather | solution.py:552
  573.1 89.9 %all-gather.9.cloned.1.call-done.h2_ref = bf16[2048,2048]{1,0:T(8,128)(2,1)} async-done(((bf16[512,2048]{1,0:T(8,128)(2,1)}), bf16[2048,2048]{1,0:T(8,128)(2,1)}) %all-gather.9.cloned.1.call-update) | async-done | bytes 8388624 | tf_op jit(solution)/shard_map/all_gather | solution.py:698
  663.0 125.0 %feed_forward.1 = (bf16[2048,2048]{1,0:T(8,128)(2,1)}, bf16[2048,2048]{1,0:T(8,128)(2,1)}) custom-call(bf16[2048,2048]{1,0:T(8,128)(2,1)} %all-gather.9.cloned.1.call-done.h2_ref, bf16[2048,2048]{1,0:T(8,128)(2,1)} %all-gather.11.cloned.1.call-done.gy_ref, bf16[2048,2048]{1,0:T(8,128)(2,1)} %all-gather.13.cloned.1.call-done.wg_ref, ...), custom_call_target="tpu_custom_call" | custom-call | flops 103079215104 | bytes 134217728 | tf_op jit(solution)/shard_map/feed_forward/pallas_call | solution.py:454
  788.0 100.5 %all_to_all.35 = bf16[4,512,2048]{2,1,0:T(8,128)(2,1)} all-to-all(bf16[4,512,2048]{2,1,0:T(8,128)(2,1)} %bitcast.284), channel_id=1, replica_groups=mesh['dp'=8,'fsdp'=4] {'fsdp'}, dimensions={0} | all-to-all | bytes 16777216 | tf_op jit(solution)/shard_map/all_to_all | solution.py:702
  888.5 6.0 all-to-all-start.2
  898.5 6.0 convert_reduce_fusion
  907.1 78.6 %all-to-all-done.2 = bf16[4,512,2048]{2,1,0:T(8,128)(2,1)} async-done(((bf16[4,512,2048]{2,1,0:T(8,128)(2,1)}), bf16[4,512,2048]{2,1,0:T(8,128)(2,1)}, u32[]{:S(2)}, u32[]{:S(2)}) %all-to-all-start.2) | async-done | bytes 8388640 | tf_op jit(solution)/shard_map/all_to_all | solution.py:702
  985.7 7.9 convert_reduce_fusion.1
  993.7 5.7 fusion.41
  1000.1 7.6 output_projection_back.1.go_ref
  1009.2 26.2 %attend_back.1 = (bf16[4,512,512]{2,1,0:T(8,128)(2,1)}, f32[8,256,64]{2,1,0:T(8,128)S(1)}, f32[8,2,320,256]{3,2,1,0:T(8,128)}, f32[8,2,2,160,128]{4,3,2,1,0:T(8,128)}) custom-call(s32[1]{0:T(128)} %bitcast.prev_ref, bf16[8,2,256,256]{3,2,1,0:T(8,128)(2,1)} %copy-done.8, bf16[8,2,64,256]{3,2,1,0:T(8,128)(2,1)} %collective-permute-done.halo_ref, ...), custom_call_target="tpu_custom_call" | custom-call | flops 6039797760 | bytes 25165824 | tf_op jit(solution)/shard_map/attend_back/pallas_call | solution.py:740
  1073.7 7.4 key_value_back.1
  1085.5 17.2 %input_gradient.1 = (bf16[512,2048]{1,0:T(8,128)(2,1)}, f32[1,2048]{1,0:T(1,128)}) custom-call(bf16[4,512,512]{2,1,0:T(8,128)(2,1)} %get-tuple-element.45.gq_ref, bf16[4,512,256]{2,1,0:T(8,128)(2,1)} %copy-done.14, bf16[8,4,272,1280]{3,2,1,0:T(8,128)(2,1)} %bitcast.280, bf16[8,4,272,1280]{3,2,1,0:T(8,128)(2,1)} %bitcast.281, bf16[512,128]{1,0:T(8,128)(2,1)} %pad.42.gu_ref, ...), custom_call_target="tpu_custom_call" | custom-call | flops 6442450944 | bytes 31457280 | tf_op jit(solution)/shard_map/input_gradient/pallas_call | solution.py:822
  1114.8 9.0 all-to-all-start.6
  1168.6 44.6 %all-to-all-done.4 = bf16[8,2,32,2048]{3,2,1,0:T(8,128)(2,1)S(1)} async-done(((bf16[8,2,32,2048]{3,2,1,0:T(8,128)(2,1)}), bf16[8,2,32,2048]{3,2,1,0:T(8,128)(2,1)S(1)}, u32[]{:S(2)}, u32[]{:S(2)}) %all-to-all-start.4) | async-done | bytes 2097184 | tf_op jit(solution)/shard_map/all_to_all | solution.py:499
  (323 shorter events, 155.9 us)
Async XLA Ops:
  7.2 120.8 %copy-start = (s32[8,2]{0,1:T(2,128)S(1)}, s32[8,2]{0,1:T(2,128)}, u32[]{:S(2)}) copy-start(s32[8,2]{0,1:T(2,128)} %param.19) | copy-start | bytes 196
  7.2 231.0 %all-gather.17.cloned.1.call-start = ((), (), s32[]{:S(2)}) async-start(), calls=%async_computation.11 | async-start | bytes 22978560 | tf_op jit(solution)/shard_map/all_gather | solution.py:529
  18.8 311.6 %all-gather.13.cloned.1.call-start = ((), (), s32[]{:S(2)}) async-start(), calls=%async_computation.9 | async-start | bytes 9437184 | tf_op jit(solution)/shard_map/all_gather | solution.py:543
  19.5 383.6 %all-gather.15.cloned.1.call-start = ((), (), s32[]{:S(2)}) async-start(), calls=%async_computation.10 | async-start | bytes 9437184 | tf_op jit(solution)/shard_map/all_gather | solution.py:544
  20.2 465.0 %all-gather.19.cloned.1.call-start = ((), (), s32[]{:S(2)}) async-start(), calls=%async_computation.12 | async-start | bytes 9437184 | tf_op jit(solution)/shard_map/all_gather | solution.py:545
  22.3 96.1 %all-to-all-start = ((bf16[8,2,32,2048]{3,2,1,0:T(8,128)(2,1)}), bf16[8,2,32,2048]{3,2,1,0:T(8,128)(2,1)S(1)}, u32[]{:S(2)}, u32[]{:S(2)}) async-start(bf16[8,2,32,2048]{3,2,1,0:T(8,128)(2,1)} %copy.247), calls=%async_computation | async-start | bytes 4194304 | tf_op jit(solution)/shard_map/all_to_all | solution.py:492
  124.3 104.3 %all-to-all-start.1 = ((bf16[8,2,32,2048]{3,2,1,0:T(8,128)(2,1)}), bf16[8,2,32,2048]{3,2,1,0:T(8,128)(2,1)S(1)}, u32[]{:S(2)}, u32[]{:S(2)}) async-start(bf16[8,2,32,2048]{3,2,1,0:T(8,128)(2,1)} %fusion.20), calls=%async_computation.1 | async-start | bytes 4194304 | tf_op jit(solution)/shard_map/all_to_all | solution.py:499
  128.0 445.1 %all-gather.11.cloned.1.call-start = ((), (), s32[]{:S(2)}) async-start(), calls=%async_computation.8 | async-start | bytes 10485760 | tf_op jit(solution)/shard_map/all_gather | solution.py:552
  128.8 100.1 %copy-start.60 = (pred[512]{0:T(512)(128)(4,1)}, pred[512]{0:T(512)(128)(4,1)S(1)}, u32[]{:S(2)}) copy-start(pred[512]{0:T(512)(128)(4,1)S(1)} %get-tuple-element.174) | copy-start | bytes 1540
  232.0 431.0 %all-gather.9.cloned.1.call-start = ((), (), s32[]{:S(2)}) async-start(), calls=%async_computation.7 | async-start | bytes 10485760 | tf_op jit(solution)/shard_map/all_gather | solution.py:698
  255.0 38.0 %collective-permute-start.1 = (bf16[8,2,80,128]{3,2,1,0:T(8,128)(2,1)}, bf16[8,2,80,128]{3,2,1,0:T(8,128)(2,1)}, u32[]{:S(2)}, u32[]{:S(2)}) collective-permute-start(bf16[8,2,80,128]{3,2,1,0:T(8,128)(2,1)} %get-tuple-element.32), channel_id=1, source_target_pairs={{0,1},{1,2},{2,3},{4,5},{5,6},{6,7},{8,9},{9,10},{10,11},{12,13},{... | collective-permute-start | bytes 983048 | tf_op jit(solution)/shard_map/ppermute | solution.py:483
  259.0 33.9 %collective-permute-start.2 = (bf16[8,2,80,128]{3,2,1,0:T(8,128)(2,1)}, bf16[8,2,80,128]{3,2,1,0:T(8,128)(2,1)}, u32[]{:S(2)}, u32[]{:S(2)}) collective-permute-start(bf16[8,2,80,128]{3,2,1,0:T(8,128)(2,1)} %get-tuple-element.32), channel_id=1, source_target_pairs={{0,2},{1,3},{4,6},{5,7},{8,10},{9,11},{12,14},{13,15},{16,18},{17,... | collective-permute-start | bytes 983048 | tf_op jit(solution)/shard_map/ppermute | solution.py:483
  262.4 30.6 %collective-permute-start.3 = (bf16[8,2,80,128]{3,2,1,0:T(8,128)(2,1)}, bf16[8,2,80,128]{3,2,1,0:T(8,128)(2,1)}, u32[]{:S(2)}, u32[]{:S(2)}) collective-permute-start(bf16[8,2,80,128]{3,2,1,0:T(8,128)(2,1)} %get-tuple-element.32), channel_id=1, source_target_pairs={{0,3},{4,7},{8,11},{12,15},{16,19},{20,23},{24,27},{28,31}} | collective-permute-start | bytes 983048 | tf_op jit(solution)/shard_map/ppermute | solution.py:483
  268.7 26.4 %collective-permute-start = (bf16[8,2,64,256]{3,2,1,0:T(8,128)(2,1)}, bf16[8,2,64,256]{3,2,1,0:T(8,128)(2,1)}, u32[]{:S(2)}, u32[]{:S(2)}) collective-permute-start(bf16[8,2,64,256]{3,2,1,0:T(8,128)(2,1)} %slice.412), channel_id=1, source_target_pairs={{0,1},{1,2},{2,3},{4,5},{5,6},{6,7},{8,9},{9,10},{10,11},{12,13},{... | collective-permute-start | bytes 1572872 | tf_op jit(solution)/shard_map/ppermute | solution.py:608
  888.5 97.2 %all-to-all-start.2 = ((bf16[4,512,2048]{2,1,0:T(8,128)(2,1)}), bf16[4,512,2048]{2,1,0:T(8,128)(2,1)}, u32[]{:S(2)}, u32[]{:S(2)}) async-start(bf16[4,512,2048]{2,1,0:T(8,128)(2,1)} %bitcast.283), calls=%async_computation.2 | async-start | bytes 16777216 | tf_op jit(solution)/shard_map/all_to_all | solution.py:702
  1039.3 26.4 %collective-permute-start.5 = (bf16[8,2,80,128]{3,2,1,0:T(8,128)(2,1)}, bf16[8,2,80,128]{3,2,1,0:T(8,128)(2,1)}, u32[]{:S(2)}, u32[]{:S(2)}) collective-permute-start(bf16[8,2,80,128]{3,2,1,0:T(8,128)(2,1)} %add_reduce_fusion), channel_id=1, source_target_pairs={{1,0},{2,1},{3,2},{5,4},{6,5},{7,6},{9,8},{10,9},{11,10},{13,12},{... | collective-permute-start | bytes 983048 | tf_op jit(solution)/shard_map/ppermute | solution.py:483
  1040.9 24.8 %collective-permute-start.6 = (bf16[8,2,80,128]{3,2,1,0:T(8,128)(2,1)}, bf16[8,2,80,128]{3,2,1,0:T(8,128)(2,1)}, u32[]{:S(2)}, u32[]{:S(2)}) collective-permute-start(bf16[8,2,80,128]{3,2,1,0:T(8,128)(2,1)} %add_reduce_fusion), channel_id=1, source_target_pairs={{2,0},{3,1},{6,4},{7,5},{10,8},{11,9},{14,12},{15,13},{18,16},{19,... | collective-permute-start | bytes 983048 | tf_op jit(solution)/shard_map/ppermute | solution.py:483
  1042.2 23.5 %collective-permute-start.7 = (bf16[8,2,80,128]{3,2,1,0:T(8,128)(2,1)}, bf16[8,2,80,128]{3,2,1,0:T(8,128)(2,1)}, u32[]{:S(2)}, u32[]{:S(2)}) collective-permute-start(bf16[8,2,80,128]{3,2,1,0:T(8,128)(2,1)} %add_reduce_fusion), channel_id=1, source_target_pairs={{3,0},{7,4},{11,8},{15,12},{19,16},{23,20},{27,24},{31,28}} | collective-permute-start | bytes 983048 | tf_op jit(solution)/shard_map/ppermute | solution.py:483
  1048.4 17.3 %collective-permute-start.8 = (bf16[8,2,80,128]{3,2,1,0:T(8,128)(2,1)}, bf16[8,2,80,128]{3,2,1,0:T(8,128)(2,1)}, u32[]{:S(2)}, u32[]{:S(2)}) collective-permute-start(bf16[8,2,80,128]{3,2,1,0:T(8,128)(2,1)} %fusion.10), channel_id=1, source_target_pairs={{1,0},{2,1},{3,2},{5,4},{6,5},{7,6},{9,8},{10,9},{11,10},{13,12},{... | collective-permute-start | bytes 983048 | tf_op jit(solution)/shard_map/ppermute | solution.py:779
  1051.8 19.3 %collective-permute-start.4 = (bf16[8,2,64,256]{3,2,1,0:T(8,128)(2,1)}, bf16[8,2,64,256]{3,2,1,0:T(8,128)(2,1)}, u32[]{:S(2)}, u32[]{:S(2)}) collective-permute-start(bf16[8,2,64,256]{3,2,1,0:T(8,128)(2,1)} %slice.588), channel_id=1, source_target_pairs={{1,0},{2,1},{3,2},{5,4},{6,5},{7,6},{9,8},{10,9},{11,10},{13,12},{... | collective-permute-start | bytes 1572872 | tf_op jit(solution)/shard_map/ppermute | solution.py:775
  1061.1 53.7 %all-to-all-start.3 = ((bf16[8,2,32,2048]{3,2,1,0:T(8,128)(2,1)}), bf16[8,2,32,2048]{3,2,1,0:T(8,128)(2,1)}, u32[]{:S(2)}, u32[]{:S(2)}) async-start(bf16[8,2,32,2048]{3,2,1,0:T(8,128)(2,1)} %bitcast.285), calls=%async_computation.3 | async-start | bytes 4194304 | tf_op jit(solution)/shard_map/all_to_all | solution.py:492
  1114.8 44.5 %all-to-all-start.6 = ((f32[32,72,128]{2,1,0:T(8,128)}), f32[32,72,128]{2,1,0:T(8,128)S(1)}, u32[]{:S(2)}, u32[]{:S(2)}) async-start(f32[32,72,128]{2,1,0:T(8,128)} %bitcast.144), calls=%async_computation.6 | async-start | bytes 2359296 | tf_op jit(solution)/shard_map/all_to_all | solution.py:861
  1159.3 54.0 %all-to-all-start.4 = ((bf16[8,2,32,2048]{3,2,1,0:T(8,128)(2,1)}), bf16[8,2,32,2048]{3,2,1,0:T(8,128)(2,1)S(1)}, u32[]{:S(2)}, u32[]{:S(2)}) async-start(bf16[8,2,32,2048]{3,2,1,0:T(8,128)(2,1)} %copy-done.40), calls=%async_computation.4 | async-start | bytes 4194304 | tf_op jit(solution)/shard_map/all_to_all | solution.py:499
  1168.0 46.8 %copy-start.1 = (s32[8,2]{0,1:T(2,128)S(1)}, s32[8,2]{0,1:T(2,128)}, u32[]{:S(2)}) copy-start(s32[8,2]{0,1:T(2,128)} %param.19) | copy-start | bytes 196
  (60 other events, 341.0 us)
Sparse Core Ops, SparseCore 0:
  18.9 219.2 all-gather.16
  239.8 81.0 all-gather.12
  322.5 80.5 all-gather.14
  404.6 80.5 all-gather.18
  486.9 86.1 all-gather.10
  575.3 87.5 all-gather.8

commit v2 on v1

v2 whole, which is shorter than its diff:
```python
import functools
import math

import jax
import jax.numpy as jnp
from jax import lax
from jax.experimental import pallas as pl
from jax.experimental.pallas import tpu as pltpu
from jax.sharding import PartitionSpec as P

H = 32
KEY_VALUE_HEADS = 8
REPEAT = H // KEY_VALUE_HEADS
HEAD_SIZE = 64
ADAPTER_RANK = 8
WIN = 64
AUG = 80
RANK_LANES = 128

EPSILON = 1e-05
ROPE_BASE = 500000.0
F32 = jnp.float32
BF16 = jnp.bfloat16
MIB = 1024 * 1024
X_PAIRS = [(i, i ^ 1) for i in range(4)]
Y_PAIRS = [(i, i ^ 2) for i in range(4)]


def dot(a, b):
    return lax.dot_general(a, b, (((1,), (0,)), ((), ())), preferred_element_type=F32)


def dot_nt(a, b):
    return lax.dot_general(a, b, (((1,), (1,)), ((), ())), preferred_element_type=F32)


def params(mib, semantics=("arbitrary",)):
    return pltpu.CompilerParams(vmem_limit_bytes=mib * MIB, dimension_semantics=semantics)


def cost(flops, bytes_accessed, transcendentals=0):
    return pl.CostEstimate(
        flops=int(flops), bytes_accessed=int(bytes_accessed), transcendentals=int(transcendentals)
    )


def whole(shape):
    return pl.BlockSpec(shape, lambda *_: (0,) * len(shape))


def after(value, *others):
    return lax.optimization_barrier((value, *others))[0]


def together(*jobs):
    arguments = lax.optimization_barrier([job[1:] for job in jobs])
    return lax.optimization_barrier([job[0](*args) for job, args in zip(jobs, arguments)])


def by_x(rows):
    return lax.ppermute(rows, "fsdp", X_PAIRS)


def by_y(rows):
    return lax.ppermute(rows, "fsdp", Y_PAIRS)


def rope_tables_t(positions):
    half_size = HEAD_SIZE // 2
    frequencies = jnp.exp(
        -(2.0 * jnp.arange(half_size, dtype=F32) / HEAD_SIZE) * math.log(ROPE_BASE)
    )
    angles = frequencies[:, None] * positions.astype(F32)[None, :]
    return jnp.cos(angles), jnp.sin(angles)


def rotate_t(head, cos_t, sin_t):
    a, b = head[:32], head[32:]
    return jnp.concatenate([a * cos_t - b * sin_t, b * cos_t + a * sin_t], axis=0)


def rotate_back_t(head, cos_t, sin_t):
    a, b = head[:32], head[32:]
    return jnp.concatenate([a * cos_t + b * sin_t, b * cos_t - a * sin_t], axis=0)


def half_softmax_t(scores):
    e = jnp.exp(scores - jnp.max(scores, axis=0, keepdims=True))
    return e * (1.0 / jnp.sum(e, axis=0, keepdims=True))


def features_t(mapped):
    return jnp.concatenate([half_softmax_t(mapped[:64]), half_softmax_t(mapped[64:])], axis=0)


def features_back_t(e, f):
    ef = e * f
    t1 = jnp.sum(ef[:64], axis=0, keepdims=True)
    t2 = jnp.sum(ef[64:], axis=0, keepdims=True)
    return (ef[:64] - e[:64] * t1) - (ef[64:] - e[64:] * t2)


def block_pieces(refs, place_ref, n_dp):
    if len(refs) == 9:
        own, x_mine, y_mine, dx_mine, dy_mine, x_other, y_other, dx_other, dy_other = refs
        shard, core = place_ref[0], place_ref[1]
        half = n_dp // 2
        mine, other = core * half, (1 - core) * half
        quarter = half // 2
        return [
            (shard, [(own, 0)]),
            (shard ^ 1, [(x_mine, mine), (x_other, other)]),
            (shard ^ 2, [(y_mine, mine), (y_other, other)]),
            (
                shard ^ 3,
                [
                    (dx_mine, mine),
                    (dy_mine, mine + quarter),
                    (dx_other, other),
                    (dy_other, other + quarter),
                ],
            ),
        ]
    return [(f, [(ref, 0)]) for f, ref in enumerate(refs)]


def project(h1_ref, u_ref, pieces, low_rank, depth):
    total = dot(u_ref[...], low_rank)
    for ref, start in pieces:
        count = ref.shape[0] * depth
        if isinstance(start, int):
            columns = h1_ref[:, start * depth : start * depth + count]
        else:
            columns = h1_ref[:, pl.ds(pl.multiple_of(start * depth, depth), count)]
        total += dot(columns, ref[...].reshape(count, ref.shape[2]))
    return total


def kv_kernel(kv_heads, micro, depth, n_dp, place_ref, h1_ref, u_ref, b_ref, cos_ref, sin_ref,
              f_ref, *refs):
    *w_refs, n_ref, tot_ref, msg_ref = refs
    rows = h1_ref.shape[0] // micro
    cos_t, sin_t = cos_ref[...], sin_ref[...]
    width = kv_heads * HEAD_SIZE
    for f, pieces in block_pieces(w_refs, place_ref, n_dp):
        kv_t = project(h1_ref, u_ref, pieces, b_ref[f], depth).T
        for g in range(kv_heads):
            head = f * kv_heads + g
            kr = rotate_t(kv_t[g * 64 : (g + 1) * 64], cos_t, sin_t).astype(BF16)
            v = kv_t[width + g * 64 : width + (g + 1) * 64].astype(BF16)
            pk = features_t(dot(f_ref[head], kr)).astype(BF16)
            natural = (
                jnp.concatenate([pk.astype(F32), kr.astype(F32), v.astype(F32)], axis=0).T
            ).astype(BF16)
            v_aug = jnp.concatenate([v, jnp.ones((AUG - 64, v.shape[1]), BF16)], axis=0)
            for m in range(micro):
                part = natural[m * rows : (m + 1) * rows]
                n_ref[head, m] = part
                sums = dot(v_aug[:, m * rows : (m + 1) * rows], part[:, :128])
                tot_ref[head, m] = sums.astype(BF16)
                msg_ref[head, m, :64] = part[rows - 64 :]
                tail = jnp.concatenate([sums[48:], jnp.zeros((16, 128), F32)], axis=0)
                msg_ref[head, m, 64:] = jnp.concatenate([sums[:48], tail], axis=1).astype(BF16)


def q_kernel(heads, depth, n_dp, place_ref, h1_ref, u_ref, b_ref, cos_ref, sin_ref, f_ref, *refs):
    *w_refs, qr_ref, pq_ref = refs
    cos_t, sin_t = cos_ref[...], sin_ref[...]
    for f, pieces in block_pieces(w_refs, place_ref, n_dp):
        q_t = project(h1_ref, u_ref, pieces, b_ref[f], depth).T
        for h in range(heads):
            head = f * heads + h
            qr = rotate_t(q_t[h * 64 : (h + 1) * 64], cos_t, sin_t).astype(BF16)
            pq = features_t(dot(f_ref[head], qr)).astype(BF16)
            if isinstance(head, int):
                qr_ref[head * 64 : (head + 1) * 64] = qr
                pq_ref[head * 128 : (head + 1) * 128] = pq
            else:
                qr_ref[pl.ds(pl.multiple_of(head * 64, 64), 64)] = qr
                pq_ref[pl.ds(pl.multiple_of(head * 128, 128), 128)] = pq


def pair_masks(has_prev):
    lane = lax.broadcasted_iota(jnp.int32, (64, REPEAT * 128), 1)
    row = lax.broadcasted_iota(jnp.int32, (64, REPEAT * 128), 0)
    low = (lane % 128) < 64
    ahead = row - lane % 64
    value = jnp.where(low, ahead - 1, -ahead)
    hidden = jnp.where(low, (1 - has_prev) * 1024, 0)
    return low, value >= 0, value - hidden >= 0


def heads_side(ref, size, start):
    return jnp.concatenate(
        [ref[h * size : (h + 1) * size, start : start + 128] for h in range(REPEAT)], axis=1
    )


def attend_kernel(micro, prev_ref, n_ref, msg_ref, qr_ref, pq_ref, *refs):
    *base_refs, o_ref, ot_ref, den_ref, s_ref = refs
    rows = n_ref.shape[2]
    low, mask_a, mask_first = pair_masks(prev_ref[0])
    low_row = (lax.broadcasted_iota(jnp.int32, (1, REPEAT * 128), 1) % 128) < 64
    key_lane = lax.broadcasted_iota(jnp.int32, (AUG, 128), 1) < 64
    for m in range(micro):
        ext = jnp.concatenate([msg_ref[0, m, :64], n_ref[0, m]], axis=0)
        ext_t = ext.astype(F32).T.astype(BF16)
        near = jnp.concatenate([msg_ref[0, m, 64:112, :128], msg_ref[0, m, 64:96, 128:]], axis=0)
        v_aug_all = jnp.concatenate([ext_t[192:256], jnp.ones((AUG - 64, rows + WIN), BF16)], axis=0)
        running = near.astype(F32)
        for base_ref in base_refs:
            running += base_ref[0, m].astype(F32)
        for p in range(rows // 128):
            start = m * rows + p * 128
            r0 = p * 128
            qr4 = heads_side(qr_ref, 64, start)
            pq4 = heads_side(pq_ref, 128, start)
            pk = ext[r0 : r0 + 128, :128]
            kr = ext[r0 : r0 + 192, 128:192]
            v_aug = v_aug_all[:, r0 : r0 + 128]
            zero = jnp.zeros_like(v_aug)
            spans = dot(
                jnp.concatenate(
                    [jnp.where(key_lane, v_aug, zero), jnp.where(key_lane, zero, v_aug)], axis=0
                ),
                pk,
            )
            if p == 0:
                running = running - spans[:AUG]
            state = jnp.concatenate([running, running + spans[:AUG]], axis=0).astype(BF16)
            running = running + spans[:AUG] + spans[AUG:]
            s_ref[0, m, p] = state
            from_state = dot(state, pq4)
            scores = dot(kr, qr4) * (1.0 / math.sqrt(HEAD_SIZE))
            linear = dot(pk, pq4)
            exp_a = jnp.exp(jnp.where(low, scores[:64], scores[128:]))
            exp_b = jnp.exp(scores[64:128])
            mask = mask_first if p == 0 else mask_a
            w_a = jnp.where(mask, exp_a, jnp.where(low, linear[:64], 0.0))
            w_b = jnp.where(mask_a, jnp.where(low, 0.0, linear[64:]), exp_b)
            den = (
                jnp.sum(w_a, axis=0, keepdims=True)
                + jnp.sum(w_b, axis=0, keepdims=True)
                + jnp.where(low_row, from_state[64:65], from_state[AUG + 64 : AUG + 65])
            )
            inv = 1.0 / den
            p_a = w_a * inv
            weights = jnp.concatenate(
                [jnp.where(low, p_a, 0.0), w_b * inv, jnp.where(low, 0.0, p_a)], axis=0
            ).astype(BF16)
            out = (
                dot(ext_t[192:256, r0 : r0 + 192], weights)
                + jnp.where(low, from_state[:64], from_state[AUG : AUG + 64]) * inv
            )
            for h in range(REPEAT):
                den_ref[0, h : h + 1, start : start + 128] = den[:, h * 128 : (h + 1) * 128]
            out_t = jnp.concatenate(
                [out[:, h * 128 : (h + 1) * 128] for h in range(REPEAT)], axis=0
            )
            ot_ref[:, start : start + 128] = out_t.astype(BF16)
            o_ref[start : start + 128, :] = out_t.T.astype(BF16)


def attend_back_kernel(micro, prev_ref, n_ref, msg_ref, s_ref, qr_ref, pq_ref, go_ref, ot_ref,
                       den_ref, f_ref, cos_ref, sin_ref,
                       gq_ref, df_ref, gn_ref, gs_ref, back_ref, total_ref,
                       gqr_ref, gmq_ref):
    rows = n_ref.shape[2]
    low, mask_a, mask_first = pair_masks(prev_ref[0])
    low_aug = (lax.broadcasted_iota(jnp.int32, (AUG, REPEAT * 128), 1) % 128) < 64
    low_feat = (lax.broadcasted_iota(jnp.int32, (128, REPEAT * 128), 1) % 128) < 64
    scale = 1.0 / math.sqrt(HEAD_SIZE)
    for m in range(micro):
        ext = jnp.concatenate([msg_ref[0, m, :64], n_ref[0, m]], axis=0)
        ext_t = ext.astype(F32).T.astype(BF16)
        tail = g_sum = None
        for p in range(rows // 128):
            start = m * rows + p * 128
            r0 = p * 128
            qr4 = heads_side(qr_ref, 64, start)
            pq4 = heads_side(pq_ref, 128, start)
            go4 = heads_side(go_ref, 64, start)
            o4 = heads_side(ot_ref, 64, start)
            den = jnp.concatenate(
                [den_ref[0, h : h + 1, start : start + 128] for h in range(REPEAT)], axis=1
            )
            inv = 1.0 / den
            pk = ext[r0 : r0 + 128, :128]
            kr = ext[r0 : r0 + 192, 128:192]
            v = ext[r0 : r0 + 192, 192:256]
            go_f = go4.astype(F32)
            delta = jnp.sum(go_f * o4.astype(F32), axis=0, keepdims=True)
            scores = dot(kr, qr4) * scale
            linear = dot(pk, pq4)
            g_p = dot(v, go4)
            mask = mask_first if p == 0 else mask_a
            exp_a = jnp.exp(jnp.where(low, scores[:64], scores[128:]))
            exp_b = jnp.exp(scores[64:128])
            p_a = jnp.where(mask, exp_a, jnp.where(low, linear[:64], 0.0)) * inv
            p_b = jnp.where(mask_a, jnp.where(low, 0.0, linear[64:]), exp_b) * inv
            weights = jnp.concatenate(
                [jnp.where(low, p_a, 0.0), p_b, jnp.where(low, 0.0, p_a)], axis=0
            ).astype(BF16)
            gw_a = (jnp.where(low, g_p[:64], g_p[128:]) - delta) * inv
            gw_b = (g_p[64:128] - delta) * inv
            gs_a = jnp.where(mask, gw_a * exp_a, 0.0)
            gs_b = jnp.where(mask_a, 0.0, gw_b * exp_b)
            g_scores = jnp.concatenate(
                [jnp.where(low, gs_a, 0.0), gs_b, jnp.where(low, 0.0, gs_a)], axis=0
            ).astype(BF16)
            g_linear = jnp.concatenate(
                [
                    jnp.where(mask_a, 0.0, jnp.where(low, gw_a, 0.0)),
                    jnp.where(mask_a, jnp.where(low, 0.0, gw_b), 0.0),
                ],
                axis=0,
            ).astype(BF16)
            go_aug = jnp.concatenate(
                [go_f * inv, -delta * inv, jnp.zeros((AUG - 65, REPEAT * 128), F32)], axis=0
            )
            go_aug_b = go_aug.astype(BF16)
            gqr = dot(ext_t[128:192, r0 : r0 + 192], g_scores) * scale
            state_t = s_ref[0, m, p].astype(F32).T.astype(BF16)
            gpq = dot(ext_t[:128, r0 : r0 + 128], g_linear) + jnp.where(
                low_feat, dot(state_t[:, :AUG], go_aug_b), dot(state_t[:, AUG:], go_aug_b)
            )
            zero = jnp.zeros_like(go_aug_b)
            g_spans = dot_nt(
                jnp.concatenate(
                    [jnp.where(low_aug, go_aug_b, zero), jnp.where(low_aug, zero, go_aug_b)], axis=0
                ),
                pq4,
            )
            gs_ref[0, m, p] = g_spans
            both = g_spans[:AUG] + g_spans[AUG:]
            g_sum = both if p == 0 else g_sum + both
            if p == 0:
                back_ref[0, m, 64:, :128] = g_spans[:AUG].astype(BF16)
            g_pk = dot_nt(g_linear, pq4)
            g_kr = dot_nt(g_scores, qr4) * scale
            g_v = dot_nt(weights, go4)
            g_keys = jnp.concatenate(
                [
                    jnp.concatenate([g_pk, jnp.zeros((64, 128), F32)], axis=0),
                    g_kr,
                    g_v,
                ],
                axis=1,
            )
            if p == 0:
                back_ref[0, m, :64] = g_keys[:64].astype(BF16)
            else:
                gn_ref[0, m, r0 - 64 : r0] = g_keys[:64] + tail
            gn_ref[0, m, r0 : r0 + 64] = g_keys[64:128]
            tail = g_keys[128:]
            if p == rows // 128 - 1:
                gn_ref[0, m, rows - 64 : rows] = tail
                total_ref[0, m] = g_sum.astype(BF16)
                back_ref[0, m, 64:, 128:] = g_sum.astype(BF16)
            pq_f = pq4.astype(F32)
            gmq = features_back_t(pq_f, gpq).astype(BF16)
            for h in range(REPEAT):
                gqr_ref[h * 64 : (h + 1) * 64, start : start + 128] = gqr[:, h * 128 : (h + 1) * 128]
                gmq_ref[h * 64 : (h + 1) * 64, start : start + 128] = gmq[:, h * 128 : (h + 1) * 128]
    cos_t, sin_t = cos_ref[...], sin_ref[...]
    grads = []
    for h in range(REPEAT):
        sl = slice(h * 64, (h + 1) * 64)
        gmq = gmq_ref[sl]
        df_ref[0, sl] = dot_nt(qr_ref[sl], gmq)
        grads.append(rotate_back_t(gqr_ref[sl] + dot(f_ref[h], gmq), cos_t, sin_t))
    gq_ref[0] = jnp.concatenate(grads, axis=0).T.astype(BF16)


def kv_back_kernel(kv_heads, micro, gn_ref, back_ref, n_ref, gs_ref, f_ref, cos_ref, sin_ref,
                   u_ref, b_ref, guq_ref, h1_ref, *refs):
    *next_refs, gkv_ref, df_ref, gu_ref, db_ref, dqkv_ref, acc_ref = refs
    rows = n_ref.shape[2]
    spans = rows // WIN
    cos_t, sin_t = cos_ref[...], sin_ref[...]
    keys, values = [], []
    unit = (lax.broadcasted_iota(jnp.int32, (64, AUG - 64), 1) == 0).astype(BF16)
    for g in range(kv_heads):
        parts = []
        for m in range(micro):
            natural = n_ref[g, m]
            later = [None] * spans
            after_here = back_ref[g, m, 64:, 128:].astype(F32)
            for ref in next_refs:
                after_here += ref[g, m].astype(F32)
            later[spans - 1] = after_here - back_ref[g, m, 64:, :128].astype(F32)
            later[spans - 2] = after_here
            for c in range(spans - 3, -1, -1):
                later[c] = later[c + 1] + gs_ref[g, m, (c + 2) // 2, ((c + 2) % 2) * AUG : ((c + 2) % 2 + 1) * AUG]
            for c in range(spans):
                part = natural[c * 64 : (c + 1) * 64]
                grad = gn_ref[g, m, c * 64 : (c + 1) * 64]
                if c == spans - 1:
                    grad = grad + back_ref[g, m, :64].astype(F32)
                big = later[c].astype(BF16)
                g_pk = dot(jnp.concatenate([part[:, 192:256], unit], axis=1), big)
                g_v = dot_nt(part[:, :128], big[:64])
                parts.append(
                    grad + jnp.concatenate([g_pk, jnp.zeros((64, 64), F32), g_v], axis=1)
                )
        grad_t = jnp.concatenate(parts, axis=0).T
        nat_t = jnp.concatenate([n_ref[g, m, :, :192] for m in range(micro)], axis=0).astype(F32).T
        gmk = features_back_t(nat_t[:128], grad_t[:128]).astype(BF16)
        df_ref[0, g * 64 : (g + 1) * 64] = dot_nt(nat_t[128:].astype(BF16), gmk)
        keys.append(rotate_back_t(grad_t[128:192] + dot(f_ref[g], gmk), cos_t, sin_t))
        values.append(grad_t[192:256])
    gkv = jnp.concatenate(keys + values, axis=0).T.astype(BF16)
    gkv_ref[0] = gkv
    db_ref[...] = dot(u_ref[...].astype(F32).T[:32].astype(BF16), gkv)
    rank_grad = dot_nt(gkv, b_ref[0])

    @pl.when(pl.program_id(0) == 0)
    def _():
        acc_ref[...] = guq_ref[...] + rank_grad

    @pl.when(pl.program_id(0) > 0)
    def _():
        acc_ref[...] += rank_grad

    @pl.when(pl.program_id(0) == pl.num_programs(0) - 1)
    def _():
        gu_ref[...] = acc_ref[...].astype(BF16)
        dqkv_ref[...] = dot(acc_ref[...].T[:32].astype(BF16), h1_ref[...])


def table_kernel(heads_ref, dqkv_ref, dao_ref, dbq_ref, dbo_ref, dg1_ref, dg2_ref, out_ref):
    width = dqkv_ref.shape[1]
    gains = jnp.concatenate([dg1_ref[...], dg2_ref[...], jnp.zeros((6, width), F32)], axis=0)
    rows = jnp.concatenate(
        [dqkv_ref[:24], dao_ref[:8], dbq_ref[:8], dbo_ref[:8], gains, jnp.zeros((8, width), F32)],
        axis=0,
    )
    out_ref[...] = jnp.concatenate([heads_ref[...], rows.T], axis=1)


def out_kernel(depth, n_dp, place_ref, o_ref, ao_ref, bo_ref, x_ref, gain_ref, *refs):
    *w_refs, x2_ref, h2_ref, uo_ref, r2_ref, acc_ref = refs
    uo = dot(o_ref[...], ao_ref[...]).astype(BF16)
    uo_ref[...] = uo
    for j in range(n_dp):
        cols = slice(j * depth, (j + 1) * depth)
        acc_ref[j] = x_ref[:, cols].astype(F32) + dot_nt(uo, bo_ref[cols])
    halves = w_refs[0].shape[2] // depth
    block = halves * depth
    for f, pieces in block_pieces(w_refs, place_ref, n_dp):
        for ref, start in pieces:
            for i in range(ref.shape[0]):
                total = None
                for a in range(halves):
                    e0 = f * block + a * depth
                    if not isinstance(f, int):
                        e0 = pl.multiple_of(e0, depth)
                    term = dot(o_ref[:, pl.ds(e0, depth)], ref[i, :, a * depth : (a + 1) * depth])
                    total = term if total is None else total + term
                acc_ref[start + i] += total
    squares = 0.0
    for j in range(n_dp):
        x2 = acc_ref[j]
        x2_ref[:, j * depth : (j + 1) * depth] = x2
        squares += jnp.sum(x2 * x2, axis=1, keepdims=True)
    r2 = lax.rsqrt(squares * (1.0 / (n_dp * depth)) + EPSILON)
    r2_ref[...] = r2
    for j in range(n_dp):
        cols = slice(j * depth, (j + 1) * depth)
        h2_ref[:, cols] = (acc_ref[j] * r2 * gain_ref[:, cols]).astype(BF16)


def go_kernel(depth, gb_ref, w_ref, ao_ref, guo_ref, o_ref, go_ref, dao_ref):
    groups = w_ref.shape[1]
    halves = w_ref.shape[3] // depth
    guo = guo_ref[...]
    low_rank = dot_nt(ao_ref[...], guo)
    for a in range(halves):
        total = low_rank[a * depth : (a + 1) * depth]
        for j in range(groups):
            total += dot_nt(
                w_ref[0, j, :, a * depth : (a + 1) * depth], gb_ref[:, j * depth : (j + 1) * depth]
            )
        go_ref[a * depth : (a + 1) * depth] = total.astype(BF16)
    dao_ref[...] = dot(guo.astype(F32).T[:16].astype(BF16), o_ref[...])


def gx_query_kernel(shards, gq_ref, wq_ref, u_ref, b_ref, out_ref, gu_ref, db_ref):
    total = dot_nt(gq_ref[0], wq_ref[0, 0])
    for f in range(1, shards):
        total += dot_nt(gq_ref[f], wq_ref[f, 0])
    out_ref[...] = total

    @pl.when(pl.program_id(0) == 0)
    def _():
        u_t = u_ref[...].astype(F32).T[:32].astype(BF16)
        cols = gq_ref.shape[2]
        rank_grad = 0.0
        for f in range(shards):
            rank_grad += dot_nt(gq_ref[f], b_ref[f])
            db_ref[:, f * cols : (f + 1) * cols] = dot(u_t, gq_ref[f])
        gu_ref[...] = rank_grad


def gx_kernel(shards, depth, part_ref, gkv_ref, wkv_ref, gu_ref, a_ref, x_ref, x_all_ref,
              gx2_ref, r1_ref, gain_ref, gx_ref, dg_ref, gh_all, dot_ref):
    j = pl.program_id(0)
    last = pl.num_programs(0) - 1

    @pl.when(j == 0)
    def _():
        dot_ref[...] = jnp.zeros_like(dot_ref)

    total = part_ref[...] + dot_nt(gu_ref[...], a_ref[...])
    for f in range(shards):
        total += dot_nt(gkv_ref[f], wkv_ref[f, 0])
    gh_all[j] = total
    hx = total * x_ref[...].astype(F32)
    dg_ref[...] = jnp.sum(hx * r1_ref[...], axis=0, keepdims=True)
    dot_ref[...] += jnp.sum(hx * gain_ref[0], axis=1, keepdims=True)

    @pl.when(j == last)
    def _():
        count = gh_all.shape[0]
        r1 = r1_ref[...]
        back = r1 * r1 * r1 * dot_ref[...] * (1.0 / (count * depth))
        for i in range(count):
            cols = slice(i * depth, (i + 1) * depth)
            gx_ref[:, cols] = (
                gx2_ref[:, cols]
                + r1 * gain_ref[i] * gh_all[i]
                - x_all_ref[:, cols].astype(F32) * back
            ).astype(BF16)


def pack_attention_kernel(wq_ref, wk_ref, wv_ref, wo_ref, qkv_ref, out_ref):
    depth, q_cols = wq_ref.shape
    qkv_ref[:, :q_cols] = wq_ref[...]
    qkv_ref[:, q_cols:] = jnp.concatenate([wk_ref[...], wv_ref[...]], axis=1)
    for a in range(wo_ref.shape[0] // depth):
        out_ref[:, a * depth : (a + 1) * depth] = wo_ref[a * depth : (a + 1) * depth]


def pack_ffn_kernel(cuts, wg_ref, wu_ref, wd_ref, *refs):
    for ref, start, stop in zip(refs, cuts, cuts[1:]):
        count = stop - start
        ref[:, :count] = wg_ref[:, start:stop]
        ref[:, count : 2 * count] = wu_ref[:, start:stop]
        step = min(256, count)
        for at in range(0, count, step):
            ref[:, 2 * count + at : 2 * count + at + step] = (
                wd_ref[start + at : start + at + step].astype(F32).T.astype(BF16)
            )


def joined(refs):
    own_a, own_b, x_a, y_a, y_b, x_b = refs
    left = own_a[0].astype(F32) + x_a[0].astype(F32) + y_a[...].astype(F32)
    right = own_b[0].astype(F32) + y_b[0].astype(F32) + x_b[...].astype(F32)
    return jnp.concatenate([left, right], axis=1)


def result_kernel(count, x2_ref, valid_ref, *refs):
    *parts, out_ref = refs
    total = joined(parts) if count == 6 else parts[0][...]
    out_ref[...] = jnp.where(valid_ref[...] > 0, x2_ref[...] + total, 0.0).astype(BF16)


def mid_back_kernel(count, x2_ref, r2_ref, gain_ref, gy_ref, uo_ref, bo_ref, *refs):
    gx2_ref, gb_ref, guo_ref, dg_ref, dbo_ref = refs[-5:]
    parts = refs[:count]
    gh = joined(parts) if count == 6 else parts[0][...]
    x2, r2 = x2_ref[...], r2_ref[...]
    gx = gh * x2
    scaled = gh * gain_ref[...]
    mean = jnp.mean(scaled * x2, axis=1, keepdims=True)
    gx2 = gy_ref[...].astype(F32) + r2 * scaled - x2 * (r2 * r2 * r2 * mean)
    gx2_ref[...] = gx2
    gb = gx2.astype(BF16)
    gb_ref[...] = gb
    guo_ref[...] = dot(gb, bo_ref[...]).astype(BF16)
    dg = jnp.sum(gx * r2, axis=0, keepdims=True)
    dbo = dot(uo_ref[...].astype(F32).T[:16].astype(BF16), gb)

    @pl.when(pl.program_id(0) == 0)
    def _():
        dg_ref[...] = dg
        dbo_ref[...] = dbo

    @pl.when(pl.program_id(0) > 0)
    def _():
        dg_ref[...] += dg
        dbo_ref[...] += dbo


def load_rows(refs, rows_ref):
    if len(refs) == 1:
        rows_ref[...] = refs[0][...]
        return
    own, from_x, from_y, diagonal_x, diagonal_y = refs
    count, width = own.shape

    @pl.when(pl.program_id(0) == 0)
    def _():
        rows_ref[:count] = own[...]
        rows_ref[count:] = from_x[...]

    @pl.when(pl.program_id(0) == 1)
    def _():
        rows_ref[:count] = from_y[...]
        rows_ref[count:, : width // 2] = diagonal_x[...]
        rows_ref[count:, width // 2 :] = diagonal_y[...]


def store_rows(value_ref, refs):
    if len(refs) == 1:
        refs[0][...] = value_ref[...].astype(BF16)
        return
    send_x, keep_x, send_y, keep_y = refs
    count, half = value_ref.shape[0] // 2, value_ref.shape[1] // 2
    keep_x[0] = value_ref[:count, :half].astype(BF16)
    send_x[0] = value_ref[count:, :half].astype(BF16)
    for here, ref in enumerate((keep_y, send_y)):

        @pl.when(pl.program_id(0) == here)
        def _(ref=ref):
            ref[0] = value_ref[:count, half:].astype(BF16)
            ref[1] = value_ref[count:, half:].astype(BF16)


def ffn_kernel(pieces, carries, split, wg_ref, wu_ref, wd_ref, *refs):
    h2_refs, gy_refs = refs[:pieces], refs[pieces : 2 * pieces]
    carried = refs[2 * pieces : 2 * pieces + carries]
    *out_refs, h2_ref, gy_ref, out_acc, gh_acc = refs[2 * pieces + carries :]
    j = pl.program_id(1)

    @pl.when(j == 0)
    def _():
        load_rows(h2_refs, h2_ref)
        load_rows(gy_refs, gy_ref)

    shape = (wg_ref.shape[0] * wg_ref.shape[1], wg_ref.shape[2])
    wg, wu, wd = wg_ref[...].reshape(shape), wu_ref[...].reshape(shape), wd_ref[...].reshape(shape)
    gate = dot(h2_ref[...], wg)
    up = dot(h2_ref[...], wu)
    g_hid = dot(gy_ref[...], wd)
    sig = 1.0 / (1.0 + jnp.exp(-gate))
    silu = gate * sig
    hid = (silu * up).astype(BF16)
    g_gate = (g_hid * up * sig * (1.0 + gate * (1.0 - sig))).astype(BF16)
    g_up = (g_hid * silu).astype(BF16)

    @pl.when(j == 0)
    def _():
        out, gh = dot_nt(hid, wd), dot_nt(g_gate, wg) + dot_nt(g_up, wu)
        if carries:
            out += carried[0][...].astype(F32)
            gh += carried[1][...].astype(F32)
        out_acc[...] = out
        gh_acc[...] = gh

    @pl.when(j > 0)
    def _():
        out_acc[...] += dot_nt(hid, wd)
        gh_acc[...] += dot_nt(g_gate, wg) + dot_nt(g_up, wu)

    @pl.when(j == pl.num_programs(1) - 1)
    def _():
        half = len(out_refs) // 2
        store_rows(out_acc, out_refs[:half])
        store_rows(gh_acc, out_refs[half:])


def ffn(tile, split, h2, gy, weights, *carried):
    total = sum(part.size for part in h2) // h2[0].shape[1]
    width = h2[0].shape[1]
    groups, depth, cols = weights.shape
    tiles = cols // (3 * tile)
    pieces = len(h2)
    row_tile = total // 2
    row_spec = pl.BlockSpec((row_tile, width), lambda r, j: (r, 0))

    def weight_spec(kind):
        return pl.BlockSpec((groups, depth, tile), lambda r, j: (0, 0, kind * tiles + j))

    if pieces == 1:
        piece_specs = [row_spec]
    else:
        piece_specs = [
            pl.BlockSpec(part.shape, lambda r, j: (0, 0), pipeline_mode=pl.Buffered(1)) for part in h2
        ]
    if split and pieces > 1:
        count, half = row_tile // 2, width // 2
        moving = pl.BlockSpec((1, count, half), lambda r, j: (r, 0, 0))
        fixed = pl.BlockSpec((2, count, half), lambda r, j: (0, 0, 0))
        out_specs = [moving, moving, fixed, fixed] * 2
        out_shape = [jax.ShapeDtypeStruct((2, count, half), BF16)] * 8
    else:
        out_specs = [row_spec, row_spec]
        out_shape = [jax.ShapeDtypeStruct((total, width), BF16)] * 2
    outs = pl.pallas_call(
        functools.partial(ffn_kernel, pieces, len(carried), split),
        grid=(total // row_tile, tiles),
        in_specs=[weight_spec(0), weight_spec(1), weight_spec(2)]
        + piece_specs * 2
        + [pl.BlockSpec((row_tile, width), lambda r, j: (r, 0), pipeline_mode=pl.Buffered(1))]
        * len(carried),
        out_specs=out_specs,
        out_shape=out_shape,
        scratch_shapes=[pltpu.VMEM((row_tile, width), BF16)] * 2
        + [pltpu.VMEM((row_tile, width), F32)] * 2,
        compiler_params=params(60, ("arbitrary", "arbitrary")),
        cost_estimate=cost(4 * total * width * cols, 2 * width * cols * (total // row_tile) + 12 * total * width),
        name="feed_forward",
    )(weights, weights, weights, *h2, *gy, *carried)
    return (outs[: len(outs) // 2], outs[len(outs) // 2 :]) if split else outs


def gather_first(rows, size):
    if size != 4:
        return (lax.all_gather(rows, "fsdp", axis=0, tiled=True),)
    return rows, by_x(rows), by_y(rows)


def gather_second(*first):
    if len(first) == 1:
        return first
    rows, from_x, from_y = first
    half = rows.shape[1] // 2
    return rows, from_x, from_y, by_x(from_y[:, :half]), by_y(from_x[:, half:])


def scatter_first(*parts, size):
    if size != 4:
        (part,) = parts
        part = part.reshape(size, part.shape[0] // size, part.shape[1])
        return (lax.all_to_all(part, "fsdp", split_axis=0, concat_axis=0, tiled=True),)
    send_x, keep_x, send_y, keep_y = parts
    return keep_x, keep_y, by_x(send_x), by_y(send_y)


def pass_on_kernel(keep_x, from_x, keep_y, from_y, a_ref, b_ref):
    a_ref[...] = (keep_x[...].astype(F32) + from_x[...].astype(F32)).astype(BF16)
    b_ref[...] = (keep_y[...].astype(F32) + from_y[...].astype(F32)).astype(BF16)


def scatter_second(*first):
    if len(first) == 1:
        return [jnp.sum(first[0].astype(F32), axis=0)]
    keep_x, keep_y, from_x, from_y = first
    _, count, half = keep_x.shape
    second = pl.BlockSpec((None, count, half), lambda _: (1, 0, 0))
    a_pass, b_pass = pl.pallas_call(
        pass_on_kernel,
        grid=(1,),
        in_specs=[second] * 4,
        out_specs=[pl.BlockSpec((count, half), lambda _: (0, 0))] * 2,
        out_shape=[jax.ShapeDtypeStruct((count, half), BF16)] * 2,
        compiler_params=params(60),
        name="pass_on",
    )(keep_x, from_x, keep_y, from_y)
    return [keep_x, keep_y, from_x, by_y(a_pass), from_y, by_x(b_pass)]


def term_specs(terms, row_tile, width):
    full = pl.BlockSpec((row_tile, width), lambda r: (r, 0))
    if len(terms) == 1:
        return [full]
    half = width // 2
    row = pl.BlockSpec((row_tile, half), lambda r: (r, 0))
    first = pl.BlockSpec((1, row_tile, half), lambda r: (0, r, 0))
    return [first, first, first, row, first, row]


def pair_swap(part):
    return lax.ppermute(part, "dp", [(i, i ^ 1) for i in range(lax.axis_size("dp"))])


def columns_share(block, size, group):
    half = block.shape[0] // 2
    return block if size != 4 else lax.dynamic_slice_in_dim(block, group % 2 * half, half, 0)


def columns_first(mine, size):
    if size != 4:
        return (lax.all_gather(mine, "fsdp", axis=0, tiled=False),)
    return by_x(mine), by_y(mine)


def columns_second(*first):
    if len(first) == 1:
        return first
    from_x, from_y = first
    share = from_x.shape[0] // 2
    return (
        from_x, from_y, by_x(from_y[:share]), by_y(from_x[share:]),
        pair_swap(from_x), pair_swap(from_y),
    )


def columns_third(block, *second):
    if len(second) == 1:
        return [second[0][f] for f in range(second[0].shape[0])]
    from_x, from_y, diagonal_x, diagonal_y, other_x, other_y = second
    return [
        block, from_x, from_y, diagonal_x, diagonal_y,
        other_x, other_y, pair_swap(diagonal_x), pair_swap(diagonal_y),
    ]


def assembled(pieces, group, shard):
    if len(pieces) != 9:
        return jnp.stack(pieces)
    block = pieces[0]
    half = block.shape[0] // 2
    core = group % 2
    out = jnp.zeros((4,) + block.shape, block.dtype)

    def put(out, part, f, at):
        return lax.dynamic_update_slice(out, part[None], (f, at, 0, 0))

    out = put(out, block, shard, 0)
    masks = ((1, 0), (2, 0), (3, 0), (3, half // 2))
    for side, at in ((pieces[1:5], core * half), (pieces[5:], (1 - core) * half)):
        for part, (mask, offset) in zip(side, masks):
            out = put(out, part, shard ^ mask, at + offset)
    return out


def shifted(array, size, direction):
    moved = []
    for step in range(2, size):
        if direction > 0:
            perm = [(i, i + step) for i in range(size - step)]
        else:
            perm = [(i + step, i) for i in range(size - step)]
        moved.append(lax.ppermute(array, "fsdp", perm))
    return moved


def deal_out(rows):
    count, width = rows.shape
    groups = lax.axis_size("dp")
    pieces = rows.reshape(groups, count // groups, width)
    return lax.all_to_all(pieces, "dp", split_axis=0, concat_axis=0, tiled=True)


def reorder_kernel(at_ref, in_ref, out_ref):
    for j in range(out_ref.shape[0]):
        out_ref[j] = in_ref[at_ref[j]]


def reordered(spread, order):
    return pl.pallas_call(
        reorder_kernel,
        in_specs=[pl.BlockSpec(memory_space=pltpu.SMEM), pl.BlockSpec(memory_space=pltpu.VMEM)],
        out_specs=pl.BlockSpec(memory_space=pltpu.VMEM),
        out_shape=jax.ShapeDtypeStruct(spread.shape, spread.dtype),
        compiler_params=pltpu.CompilerParams(vmem_limit_bytes=60 * MIB),
        name="reorder",
    )(order, spread)


def deal_in(ordered):
    groups, share, width = ordered.shape
    settled = lax.all_to_all(ordered, "dp", split_axis=0, concat_axis=0, tiled=True)
    return settled.reshape(groups * share, width)


def shards(
    inputs, cotangent, lengths, dealing, wq, wk, wv, wo, wg, wu, wd,
    down_ad, up_qo, up_kv, fmap_q, fmap_k, gains,
):
    n_dp = lax.axis_size("dp")
    n_f = lax.axis_size("fsdp")
    group = lax.axis_index("dp")
    quarter = lax.axis_index("fsdp")
    micro, rows, width = inputs.shape[1:]
    total = micro * rows
    depth = wq.shape[0]
    q_cols, k_cols = wq.shape[1], wk.shape[1]
    kv_heads = k_cols // HEAD_SIZE
    heads = q_cols // HEAD_SIZE
    halves = wo.shape[0] // depth
    n_all = n_dp * n_f
    x = inputs[0].reshape(total, width)

    small_parts = [down_ad, up_qo, up_kv, fmap_q, fmap_k, gains]
    flat = jnp.concatenate([part.reshape(-1) for part in small_parts])
    small_rows = -(-flat.shape[0] // (16 * 128)) * 16
    flat = jnp.pad(flat, (0, small_rows * 128 - flat.shape[0])).reshape(1, small_rows, 128)
    small = lax.all_gather(flat.reshape(small_rows, 128), "dp", axis=0, tiled=False)
    small = lax.all_gather(small, "fsdp", axis=0, tiled=False)
    small = small.transpose(1, 0, 2, 3).reshape(n_all, small_rows * 128)
    at = 0
    fetched = []
    for part in small_parts:
        fetched.append(
            small[:, at : at + part.size].reshape((n_all * part.shape[0],) + part.shape[1:])
        )
        at += part.size
    down_ad, up_qo, up_kv, fmap_q, fmap_k, gains = fetched

    pack_cols = q_cols + 2 * k_cols
    w_qkv, w_out = pl.pallas_call(
        pack_attention_kernel,
        out_shape=[
            jax.ShapeDtypeStruct((depth, pack_cols), BF16),
            jax.ShapeDtypeStruct((depth, q_cols), BF16),
        ],
        compiler_params=pltpu.CompilerParams(vmem_limit_bytes=60 * MIB),
        name="pack_attention",
    )(wq, wk, wv, wo)
    w_qkv = lax.all_gather(w_qkv, "dp", axis=0, tiled=False)
    near, spread = together(
        (functools.partial(columns_first, size=n_f), columns_share(w_qkv, n_f, group)),
        (deal_out, after(cotangent[0].reshape(total, width), small)),
    )
    w_out = lax.all_gather(after(w_out, near[-1]), "dp", axis=0, tiled=False)
    share_micro = group * (total // n_dp) // rows
    order = lax.dynamic_index_in_dim(dealing, share_micro, 0, keepdims=False)

    gain_one = gains[:, 0].astype(F32)
    gain_two = gains[:, 1].astype(F32)

    hidden = wg.shape[1]
    tile = hidden // 4
    cuts = (0, 2 * tile, hidden)
    w_ffn = pl.pallas_call(
        functools.partial(pack_ffn_kernel, cuts),
        out_shape=[
            jax.ShapeDtypeStruct((depth, 3 * (stop - start)), BF16)
            for start, stop in zip(cuts, cuts[1:])
        ],
        compiler_params=pltpu.CompilerParams(vmem_limit_bytes=60 * MIB),
        name="pack_feed_forward",
    )(wg, wu, wd)
    positions = quarter * rows + jnp.arange(rows, dtype=jnp.int32)
    seq_len = lax.dynamic_index_in_dim(lengths, group, 0, keepdims=False)
    valid = (positions[None, :] < seq_len[:, None]).reshape(total, 1)

    xf = x.astype(F32)
    r1 = lax.rsqrt(jnp.mean(xf * xf, axis=-1, keepdims=True) + EPSILON)
    h1 = (xf * r1 * gain_one).astype(BF16)
    rank = ADAPTER_RANK
    lanes = RANK_LANES
    a_qkv = jnp.pad(down_ad[:, : 3 * rank], ((0, 0), (0, lanes - 3 * rank)))
    a_o = jnp.pad(down_ad[:, 3 * rank :], ((0, 0), (0, lanes - rank)))
    u = dot(h1, a_qkv).astype(BF16)
    b_q = up_qo[:, :rank].reshape(n_f, q_cols, rank)
    b_k = up_kv[:, :rank].reshape(n_f, k_cols, rank)
    b_v = up_kv[:, rank:].reshape(n_f, k_cols, rank)
    b_o = jnp.pad(up_qo[:, rank:], ((0, 0), (0, lanes - rank)))

    def placed(block, at):
        return jnp.pad(block.transpose(0, 2, 1), ((0, 0), (at, lanes - at - rank), (0, 0)))

    b_q_t = placed(b_q, 0)
    b_kv_t = jnp.concatenate([placed(b_k, rank), placed(b_v, 2 * rank)], axis=2)
    fq = fmap_q.reshape(H, HEAD_SIZE, HEAD_SIZE)
    fk = fmap_k.reshape(KEY_VALUE_HEADS, HEAD_SIZE, HEAD_SIZE)
    fq_t = jnp.concatenate([fq.transpose(0, 2, 1), -fq.transpose(0, 2, 1)], axis=1)
    fk_t = jnp.concatenate([fk.transpose(0, 2, 1), -fk.transpose(0, 2, 1)], axis=1)
    cos_t, sin_t = rope_tables_t(jnp.tile(positions, micro))
    pairs = rows // 128
    prepared = (h1, u, a_qkv, a_o, b_q_t, b_kv_t, b_o, fq, fk, fq_t, fk_t, cos_t, sin_t)
    inverse = jnp.argsort(dealing, axis=1).astype(jnp.int32)
    prepared += (inverse,)
    second, cot, prepared = together(
        (columns_second, *near),
        (lambda spread, order: deal_in(reordered(spread, order)), spread, order),
        (lambda *arrays: arrays, *prepared),
    )
    h1, u, a_qkv, a_o, b_q_t, b_kv_t, b_o, fq, fk, fq_t, fk_t, cos_t, sin_t, inverse = prepared
    fetched_ffn = [lax.all_gather(after(w_ffn[0], cot), "dp", axis=0, tiled=False)]
    (qkv_pieces,) = together((columns_third, w_qkv, *second))

    place = jnp.stack([quarter, group % 2]).astype(jnp.int32)
    smem = pl.BlockSpec(memory_space=pltpu.SMEM)
    vmem = pl.BlockSpec(memory_space=pltpu.VMEM)

    def columns(pieces, size, at):
        return [
            pl.BlockSpec(part.shape[:2] + (size,), lambda _: (0, 0, at), pipeline_mode=pl.Buffered(1))
            for part in pieces
        ]

    def key_values(h1, u, *pieces):
        return pl.pallas_call(
            functools.partial(kv_kernel, kv_heads, micro, depth, n_dp),
            grid=(1,),
            in_specs=[smem] + [vmem] * 6 + columns(pieces, 2 * k_cols, q_cols // (2 * k_cols)),
            out_specs=[vmem] * 3,
            out_shape=[
                jax.ShapeDtypeStruct((KEY_VALUE_HEADS, micro, rows, 256), BF16),
                jax.ShapeDtypeStruct((KEY_VALUE_HEADS, micro, AUG, 128), BF16),
                jax.ShapeDtypeStruct((KEY_VALUE_HEADS, micro, 112, 256), BF16),
            ],
            compiler_params=params(40),
            cost_estimate=cost(4 * total * width * k_cols * n_f, 2 * (total * width + 2 * width * k_cols * n_f), 128 * 8 * total),
            name="key_value",
        )(place, h1, u, b_kv_t, cos_t, sin_t, fk_t, *pieces)

    def queries(h1, u, *pieces):
        return pl.pallas_call(
            functools.partial(q_kernel, heads, depth, n_dp),
            grid=(1,),
            in_specs=[smem] + [vmem] * 6 + columns(pieces, q_cols, 0),
            out_specs=[vmem, vmem],
            out_shape=[
                jax.ShapeDtypeStruct((H * 64, total), BF16),
                jax.ShapeDtypeStruct((H * 128, total), BF16),
            ],
            compiler_params=params(40),
            cost_estimate=cost(2 * total * width * q_cols * n_f, 2 * (total * width + width * q_cols * n_f + 3 * total * 2048), 128 * 32 * total),
            name="query",
        )(place, h1, u, b_q_t, cos_t, sin_t, fq_t, *pieces)

    forward_one = [(i, i + 1) for i in range(n_f - 1)]
    backward_one = [(i + 1, i) for i in range(n_f - 1)]

    (kv_natural, totals, message), out_near = together(
        (key_values, h1, u, *qkv_pieces),
        (functools.partial(columns_first, size=n_f), columns_share(w_out, n_f, group)),
    )

    def send_on(message, totals):
        return lax.ppermute(message, "fsdp", forward_one), shifted(totals, n_f, 1)

    (q_rot, q_feat), (message, bases) = together(
        (queries, h1, u, *qkv_pieces), (send_on, message, totals)
    )
    part = after(w_ffn[1], q_rot)
    fetched_ffn.append(lax.all_gather(part, "dp", axis=0, tiled=False))
    w_ffn = fetched_ffn

    has_prev = (quarter > 0).astype(jnp.int32).reshape(1)
    g4 = REPEAT * 64
    prev_spec = smem
    n_spec = pl.BlockSpec((1, micro, rows, 256), lambda g: (g, 0, 0, 0))
    message_spec = pl.BlockSpec((1, micro, 112, 256), lambda g: (g, 0, 0, 0))
    back_spec = pl.BlockSpec((1, micro, 64 + AUG, 256), lambda g: (g, 0, 0, 0))
    state_spec = pl.BlockSpec((1, micro, pairs, 2 * AUG, 128), lambda g: (g, 0, 0, 0, 0))
    head_spec = pl.BlockSpec((g4, total), lambda g: (g, 0))
    feat_spec = pl.BlockSpec((2 * g4, total), lambda g: (g, 0))
    den_spec = pl.BlockSpec((1, 8, total), lambda g: (g, 0, 0))
    base_spec = pl.BlockSpec((1, micro, AUG, 128), lambda g: (g, 0, 0, 0))
    attend_flops = H * total * 2 * (192 * 64 + 128 * 128 + 160 * 128 + 192 * 64)
    gy_both = jnp.where(valid, cot, jnp.zeros_like(cot))
    gy = [gy_both[m * rows : (m + 1) * rows] for m in range(micro)]
    attend = pl.pallas_call(
        functools.partial(attend_kernel, micro),
        grid=(KEY_VALUE_HEADS,),
        in_specs=[
            prev_spec,
            n_spec,
            message_spec,
            head_spec,
            feat_spec,
        ]
        + [base_spec] * (n_f - 2),
        out_specs=[pl.BlockSpec((total, g4), lambda g: (0, g)), head_spec, den_spec, state_spec],
        out_shape=[
            jax.ShapeDtypeStruct((total, H * 64), BF16),
            jax.ShapeDtypeStruct((H * 64, total), BF16),
            jax.ShapeDtypeStruct((KEY_VALUE_HEADS, 8, total), F32),
            jax.ShapeDtypeStruct((KEY_VALUE_HEADS, micro, pairs, 2 * AUG, 128), BF16),
        ],
        compiler_params=params(60),
        cost_estimate=cost(attend_flops, 14 * MIB, 128 * H * total),
        name="attend",
    )
    (o, o_t, den, states), gy_first, out_second = together(
        (attend, has_prev, kv_natural, message, q_rot, q_feat, *bases),
        (functools.partial(gather_first, size=n_f), gy[0]),
        (columns_second, *out_near),
    )
    (out_pieces,) = together((columns_third, w_out, *out_second))

    project_out = pl.pallas_call(
        functools.partial(out_kernel, depth, n_dp),
        grid=(1,),
        in_specs=[smem] + [vmem] * 5 + columns(out_pieces, q_cols, 0),
        out_specs=[vmem] * 4,
        out_shape=[
            jax.ShapeDtypeStruct((total, width), F32),
            jax.ShapeDtypeStruct((total, width), BF16),
            jax.ShapeDtypeStruct((total, lanes), BF16),
            jax.ShapeDtypeStruct((total, 1), F32),
        ],
        scratch_shapes=[pltpu.VMEM((n_dp, total, depth), F32)],
        compiler_params=params(40),
        cost_estimate=cost(2 * total * width * H * 64, 20 * MIB),
        name="output_projection",
    )
    (x2, h2, uo, r2), gy_zero = together(
        (project_out, place, o, a_o, b_o, x, gain_two.reshape(1, width), *out_pieces),
        (gather_second, *gy_first),
    )
    gather = functools.partial(gather_first, size=n_f)

    def assemble(*pieces):
        return assembled(pieces, group, quarter)

    (h2_first,) = together((gather, h2[:rows]))
    (h2_zero,) = together((gather_second, *h2_first))

    def piece(array, m):
        return array[m * rows : (m + 1) * rows]

    row_tile = min(128, rows)

    def finish(m, terms):
        return pl.pallas_call(
            functools.partial(result_kernel, len(terms)),
            grid=(rows // row_tile,),
            in_specs=[
                pl.BlockSpec((row_tile, width), lambda r: (m * (rows // row_tile) + r, 0)),
                pl.BlockSpec((row_tile, 1), lambda r: (m * (rows // row_tile) + r, 0)),
            ]
            + term_specs(terms, row_tile, width),
            out_specs=pl.BlockSpec((row_tile, width), lambda r: (r, 0)),
            out_shape=jax.ShapeDtypeStruct((rows, width), BF16),
            compiler_params=params(40),
            cost_estimate=cost(4 * rows * width, 10 * rows * width),
            name="result",
        )(x2, valid_rows, *terms)

    def mid_back(m, terms, gy, *whole_arrays):
        here = pl.BlockSpec((row_tile, width), lambda r: (m * (rows // row_tile) + r, 0))
        thin = pl.BlockSpec((row_tile, lanes), lambda r: (m * (rows // row_tile) + r, 0))
        count = 6 + len(terms)
        return pl.pallas_call(
            functools.partial(mid_back_kernel, len(terms)),
            grid=(rows // row_tile,),
            in_specs=[
                here,
                pl.BlockSpec((row_tile, 1), lambda r: (m * (rows // row_tile) + r, 0)),
                whole((1, width)),
                pl.BlockSpec((row_tile, width), lambda r: (r, 0)),
                thin,
                whole((width, lanes)),
            ]
            + term_specs(terms, row_tile, width)
            + [pl.BlockSpec(memory_space=pl.ANY)] * len(whole_arrays),
            out_specs=[here, here, thin, whole((1, width)), whole((16, width))],
            out_shape=[
                jax.ShapeDtypeStruct((total, width), F32),
                jax.ShapeDtypeStruct((total, width), BF16),
                jax.ShapeDtypeStruct((total, lanes), BF16),
                jax.ShapeDtypeStruct((1, width), F32),
                jax.ShapeDtypeStruct((16, width), F32),
            ],
            input_output_aliases={count + i: i for i in range(len(whole_arrays))},
            compiler_params=params(40),
            cost_estimate=cost(20 * rows * width, 16 * rows * width),
            name="mid_back",
        )(x2, r2, gain_two.reshape(1, width), gy, uo, b_o, *terms, *whole_arrays)

    valid_rows = valid.astype(jnp.int32)
    def feed(split):
        def run(h2, gy, weights, *carried):
            return ffn(tile, split, h2, gy, weights, *carried)

        return run

    scatter = functools.partial(scatter_first, size=n_f)
    head_zero, h2_first, gy_first = together(
        (feed(False), h2_zero, gy_zero, w_ffn[0]), (gather, h2[rows:]), (gather, gy[1])
    )
    h2_one, gy_one, w_qkv = together(
        (gather_second, *h2_first), (gather_second, *gy_first), (assemble, *qkv_pieces)
    )
    (head_one,) = together((feed(False), h2_one, gy_one, w_ffn[0]))
    h2_zero = after(h2_zero[0], head_one[0]), *h2_zero[1:]
    ((down_zero, gh_zero),) = together((feed(True), h2_zero, gy_zero, w_ffn[1], *head_zero))
    gh_zero_terms, down_zero_terms, (down_one, gh_one) = together(
        (scatter, *gh_zero),
        (scatter, *down_zero),
        (feed(True), h2_one, gy_one, w_ffn[1], *head_one),
    )
    gh_one_first, gh_zero_terms, w_out = together(
        (scatter, *gh_one), (scatter_second, *gh_zero_terms), (assemble, *out_pieces)
    )

    go_back = pl.pallas_call(
        functools.partial(go_kernel, depth),
        grid=(n_f,),
        in_specs=[
            whole((total, width)),
            pl.BlockSpec((1, n_dp, depth, q_cols), lambda f: (f, 0, 0, 0)),
            pl.BlockSpec((q_cols, lanes), lambda f: (f, 0)),
            whole((total, lanes)),
            pl.BlockSpec((total, q_cols), lambda f: (0, f)),
        ],
        out_specs=[
            pl.BlockSpec((q_cols, total), lambda f: (f, 0)),
            pl.BlockSpec((16, q_cols), lambda f: (0, f)),
        ],
        out_shape=[
            jax.ShapeDtypeStruct((H * 64, total), BF16),
            jax.ShapeDtypeStruct((16, H * 64), F32),
        ],
        compiler_params=params(60),
        cost_estimate=cost(2 * total * width * H * 64, 12 * MIB),
        name="output_projection_back",
    )

    attend_back = pl.pallas_call(
        functools.partial(attend_back_kernel, micro),
        grid=(KEY_VALUE_HEADS,),
        in_specs=[
            prev_spec,
            n_spec,
            message_spec,
            state_spec,
            head_spec,
            feat_spec,
            head_spec,
            head_spec,
            den_spec,
            pl.BlockSpec((REPEAT, 64, 64), lambda g: (g, 0, 0)),
            whole((32, total)),
            whole((32, total)),
        ],
        out_specs=[
            pl.BlockSpec((1, total, g4), lambda g: (g * g4 // q_cols, 0, g % (q_cols // g4))),
            pl.BlockSpec((1, g4, 64), lambda g: (g, 0, 0)),
            n_spec,
            state_spec,
            back_spec,
            base_spec,
        ],
        out_shape=[
            jax.ShapeDtypeStruct((n_f, total, q_cols), BF16),
            jax.ShapeDtypeStruct((KEY_VALUE_HEADS, g4, 64), F32),
            jax.ShapeDtypeStruct((KEY_VALUE_HEADS, micro, rows, 256), F32),
            jax.ShapeDtypeStruct((KEY_VALUE_HEADS, micro, pairs, 2 * AUG, 128), F32),
            jax.ShapeDtypeStruct((KEY_VALUE_HEADS, micro, 64 + AUG, 256), BF16),
            jax.ShapeDtypeStruct((KEY_VALUE_HEADS, micro, AUG, 128), BF16),
        ],
        scratch_shapes=[pltpu.VMEM((g4, total), F32), pltpu.VMEM((g4, total), BF16)],
        compiler_params=params(60),
        cost_estimate=cost(3 * attend_flops, 24 * MIB, 128 * H * total),
        name="attend_back",
    )
    gh_one_terms, down_zero_terms, zero = together(
        (scatter_second, *gh_one_first),
        (scatter_second, *down_zero_terms),
        (functools.partial(mid_back, 0), gh_zero_terms, gy[0]),
    )

    def norm_to_heads(gh_one, gy_one, *zero):
        gx2, gb, guo, *one = mid_back(1, gh_one, gy_one, *zero[:3])
        go_t, d_ao_t = go_back(gb, w_out, a_o, guo, o)
        back = attend_back(
            has_prev, kv_natural, message, states, q_rot, q_feat, go_t, o_t, den, fq, cos_t, sin_t
        )
        return back, gx2, d_ao_t, zero[3] + one[0], zero[4] + one[1]

    def finish_and_deal(m, terms):
        return deal_out(finish(m, terms))

    (back, gx2, d_ao_t, dg2, d_bo_t), spread_zero, down_one_terms = together(
        (norm_to_heads, gh_one_terms, gy[1], *zero),
        (functools.partial(finish_and_deal, 0), down_zero_terms),
        (scatter, *down_one),
    )
    gq, d_fq, g_keys, g_states, g_message, g_total = back

    query_part = pl.pallas_call(
        functools.partial(gx_query_kernel, n_f),
        grid=(n_dp,),
        in_specs=[
            whole((n_f, total, q_cols)),
            pl.BlockSpec((n_f, 1, depth, q_cols), lambda j: (0, j, 0, 0)),
            whole((total, lanes)),
            whole((n_f, lanes, q_cols)),
        ],
        out_specs=[
            pl.BlockSpec((total, depth), lambda j: (0, j)),
            whole((total, lanes)),
            whole((32, H * 64)),
        ],
        out_shape=[
            jax.ShapeDtypeStruct((total, width), F32),
            jax.ShapeDtypeStruct((total, lanes), F32),
            jax.ShapeDtypeStruct((32, H * 64), F32),
        ],
        compiler_params=params(60),
        cost_estimate=cost(2 * total * width * 2048, 16 * MIB),
        name="query_input_gradient",
    )

    def exchange(g_message, g_total):
        return lax.ppermute(g_message, "fsdp", backward_one), shifted(g_total, n_f, -1)

    (gh_q, gu_q, d_bq_t), (g_message, g_next), down_one_terms, out_zero = together(
        (query_part, gq, w_qkv, u, b_q_t),
        (exchange, g_message, g_total),
        (scatter_second, *down_one_terms),
        (deal_in, reordered(spread_zero, inverse[0])),
    )

    next_spec = pl.BlockSpec((kv_heads, micro, AUG, 128), lambda f: (f, 0, 0, 0))
    kv_back = pl.pallas_call(
        functools.partial(kv_back_kernel, kv_heads, micro),
        grid=(n_f,),
        in_specs=[
            pl.BlockSpec((kv_heads, micro, rows, 256), lambda f: (f, 0, 0, 0)),
            pl.BlockSpec((kv_heads, micro, 64 + AUG, 256), lambda f: (f, 0, 0, 0)),
            pl.BlockSpec((kv_heads, micro, rows, 256), lambda f: (f, 0, 0, 0)),
            pl.BlockSpec((kv_heads, micro, pairs, 2 * AUG, 128), lambda f: (f, 0, 0, 0, 0)),
            pl.BlockSpec((kv_heads, 64, 64), lambda f: (f, 0, 0)),
            whole((32, total)),
            whole((32, total)),
            whole((total, lanes)),
            pl.BlockSpec((1, lanes, 2 * k_cols), lambda f: (f, 0, 0)),
            whole((total, lanes)),
            whole((total, width)),
        ]
        + [next_spec] * (n_f - 2),
        out_specs=[
            pl.BlockSpec((1, total, 2 * k_cols), lambda f: (f, 0, 0)),
            pl.BlockSpec((1, k_cols, 64), lambda f: (f, 0, 0)),
            whole((total, lanes)),
            pl.BlockSpec((None, 32, 2 * k_cols), lambda f: (f, 0, 0)),
            whole((32, width)),
        ],
        out_shape=[
            jax.ShapeDtypeStruct((n_f, total, 2 * k_cols), BF16),
            jax.ShapeDtypeStruct((n_f, k_cols, 64), F32),
            jax.ShapeDtypeStruct((total, lanes), BF16),
            jax.ShapeDtypeStruct((n_f, 32, 2 * k_cols), F32),
            jax.ShapeDtypeStruct((32, width), F32),
        ],
        scratch_shapes=[pltpu.VMEM((total, lanes), F32)],
        compiler_params=params(60),
        cost_estimate=cost(8 * total * 128 * 128, 8 * MIB),
        name="key_value_back",
    )
    input_back = pl.pallas_call(
        functools.partial(gx_kernel, n_f, depth),
        grid=(n_dp,),
        in_specs=[
            pl.BlockSpec((total, depth), lambda j: (0, j)),
            whole((n_f, total, 2 * k_cols)),
            pl.BlockSpec((n_f, 1, depth, 2 * k_cols), lambda j: (0, j, 0, q_cols // (2 * k_cols))),
            whole((total, lanes)),
            pl.BlockSpec((depth, lanes), lambda j: (j, 0)),
            pl.BlockSpec((total, depth), lambda j: (0, j)),
            whole((total, width)),
            whole((total, width)),
            whole((total, 1)),
            whole((n_dp, 1, depth)),
        ],
        out_specs=[whole((total, width)), pl.BlockSpec((1, depth), lambda j: (0, j))],
        out_shape=[
            jax.ShapeDtypeStruct((total, width), BF16),
            jax.ShapeDtypeStruct((1, width), F32),
        ],
        scratch_shapes=[pltpu.VMEM((n_dp, total, depth), F32), pltpu.VMEM((total, 1), F32)],
        compiler_params=params(60),
        cost_estimate=cost(2 * total * width * 1024, 30 * MIB),
        name="input_gradient",
    )
    def heads_to_input(g_keys, g_message, g_next, gu_q, gh_q):
        gkv, d_fk, gu, d_bkv_t, d_qkv_t = kv_back(
            g_keys, g_message, kv_natural, g_states, fk, cos_t, sin_t, u, b_kv_t, gu_q, h1,
            *g_next,
        )
        gx, dg1 = input_back(
            gh_q, gkv, w_qkv, gu, a_qkv, x, x, gx2, r1, gain_one.reshape(n_dp, 1, depth)
        )
        return gx, dg1, d_fk, d_bkv_t, d_qkv_t

    (gx, dg1, d_fk, d_bkv_t, d_qkv_t), spread_one = together(
        (heads_to_input, g_keys, g_message, g_next, gu_q, gh_q),
        (functools.partial(finish_and_deal, 1), down_one_terms),
    )
    output = [out_zero, deal_in(reordered(spread_one, inverse[1]))]

    wide = pl.pallas_call(
        table_kernel,
        out_shape=jax.ShapeDtypeStruct((width, lanes), F32),
        compiler_params=pltpu.CompilerParams(vmem_limit_bytes=60 * MIB),
        name="table",
    )(d_fq.reshape(H * 64, 64), d_qkv_t, d_ao_t, d_bq_t, d_bo_t, dg1, dg2)
    kv_rows = KEY_VALUE_HEADS * 64
    d_bk = d_bkv_t[:, rank : 2 * rank, :k_cols].transpose(0, 2, 1).reshape(kv_rows, rank)
    d_bv = d_bkv_t[:, 2 * rank : 3 * rank, k_cols:].transpose(0, 2, 1).reshape(kv_rows, rank)
    narrow = jnp.concatenate(
        [d_fk.reshape(kv_rows, 64), d_bk, d_bv, jnp.zeros((kv_rows, lanes - 80), F32)], axis=1
    )
    wide = wide.reshape(n_all, width // n_all, lanes)
    narrow = narrow.reshape(n_all, kv_rows // n_all, lanes)
    table = jnp.concatenate([wide, narrow], axis=1).astype(BF16)
    moved = lax.all_to_all(table, ("dp", "fsdp"), split_axis=0, concat_axis=0, tiled=True)
    table = jnp.sum(moved.astype(F32), axis=0)
    wide, narrow = table[: width // n_all], table[width // n_all :]
    shares = (
        wide[:, 64:96],
        wide[:, 96:112],
        narrow[:, 64:80],
        wide[:, :64],
        narrow[:, :64],
        wide[:, 112:114],
    )
    return (jnp.stack(output)[None], gx.reshape(1, micro, rows, width), *shares)


def solution(mesh):
    every = ("dp", "fsdp")
    blocks = P("dp", None, "fsdp", None)
    in_specs = (
        blocks,
        blocks,
        P(),
        P(),
        P("dp", "fsdp"),
        P("dp", "fsdp"),
        P("dp", "fsdp"),
        P("fsdp", "dp"),
        P("dp", "fsdp"),
        P("dp", "fsdp"),
        P("fsdp", "dp"),
    ) + (P(every, None),) * 6
    out_specs = (blocks, blocks) + (P(every, None),) * 6
    return jax.shard_map(shards, mesh=mesh, in_specs=in_specs, out_specs=out_specs, check_vma=False)
```

time: 1230 us -> 861 us (0.70)
  waiting for transfers between devices: 626 us -> 235 us
  Pallas kernels: 234 us -> 336 us
  blocking collectives: 101 us -> 27.7 us
  between operations: 76.5 us -> 15.4 us
  local copies, waits for them, and re-layouts: 79.1 us -> 123 us
  starting transfers between devices: 53.1 us -> 92.8 us
  other arithmetic: 46.7 us -> 18.9 us
    all_gather x6 -> x4, waiting for transfers between devices: 336 us -> 8.28 us  [the longest x1 8.27 us: shards(): w_qkv = lax.all_gather(w_qkv, 'dp', axis=0, tiled=False)]
    all_to_all x6 -> x7, waiting for transfers between devices: 285 us -> 79.4 us  [the longest x3 62.3 us: deal_in(): lax.all_to_all(ordered, 'dp', split_axis=0, concat_axis=0, tiled=True)]
    ppermute x9 -> x54, waiting for transfers between devices: 3.76 us -> 147 us  [the longest x20 107 us: by_x(): return lax.ppermute(rows, 'fsdp', X_PAIRS)]
    pallas_call x9 -> x27, Pallas kernels: 234 us -> 336 us  [the longest x4 163 us: ffn(): pl.pallas_call(functools.partial(ffn_kernel, pieces, len(carried), split)...]
    all_to_all x1 -> x0, blocking collectives: 101 us -> none  [scatter(): lax.all_to_all(part.reshape(n_f, total, width), 'fsdp', split_axis=0, con...]
    ppermute x9 -> x54, starting transfers between devices: 18.3 us -> 60.9 us  [the longest x20 22.8 us: by_y(): return lax.ppermute(rows, 'fsdp', Y_PAIRS)]
    all_gather x0 -> x2, blocking collectives: none -> 27.7 us  [the longest x1 16.1 us: shards(): lax.all_gather(flat.reshape(small_rows, 128), 'dp', axis=0, tiled=False)]
    dynamic_update_slice x0 -> x18, local copies, waits for them, and re-layouts: none -> 26.7 us  [put(): return lax.dynamic_update_slice(out, part[None], (f, at, 0, 0))]
  transfers between devices with their start and end apart: 21 -> 65, of which waited for: 11 -> 26; matrix products, arithmetic and copies ran while one was open for 7% -> 11% of each run, Pallas kernels for 6% -> 32%
where the time goes in v2:
time: 861 us; the launch traced here: 850 us
  Pallas kernels  336 us (39%)
  waiting for transfers between devices  235 us (27%)
  local copies, waits for them, and re-layouts  123 us (14%)
  starting transfers between devices  92.8 us (11%)
  blocking collectives  27.7 us (3%)
  other arithmetic  18.9 us (2%)
  between operations  15.4 us (2%)
    pallas_call x4, Pallas kernels, ffn(): pl.pallas_call(functools.partial(ffn_kernel, pieces, len(carried), split)...  163 us
    ppermute x20, waiting for transfers between devices, by_x(): return lax.ppermute(rows, 'fsdp', X_PAIRS)  107 us
    all_to_all x3, waiting for transfers between devices, deal_in(): lax.all_to_all(ordered, 'dp', split_axis=0, concat_axis=0, tiled=True)  62.3 us
    pallas_call x3, Pallas kernels, together(): job[0](*args)  45.2 us
    unnamed x178, local copies, waits for them, and re-layouts  44.1 us
    pallas_call x1, Pallas kernels, norm_to_heads(): attend_back(has_prev, kv_natural, message, states, q_rot, q_feat, go_t, o...  26.7 us
    dynamic_update_slice x18, local copies, waits for them, and re-layouts, put(): return lax.dynamic_update_slice(out, part[None], (f, at, 0, 0))  26.7 us
    ppermute x4, waiting for transfers between devices, shifted(): moved.append(lax.ppermute(array, 'fsdp', perm))  25.6 us
  transfers between devices with their start and end apart: 65, of which 26 were waited for; matrix products, arithmetic and copies ran while one was open for 11% of the time, Pallas kernels for 32%

profile of v2, /device:TPU:0, one launch (start us, length us, event | category | flops | bytes accessed | tf_op | source)
XLA Modules:
  0.0 849.5 jit_solution(16434528494181200370)
XLA Ops:
  15.4 16.1 %all_gather.35 = bf16[8,80,128]{2,1,0:T(8,128)(2,1)S(1)} all-gather(bf16[1,80,128]{2,1,0:T(8,128)(2,1)S(1)} %pad_bitcast_fusion), channel_id=1, replica_groups=mesh['dp'=8,'fsdp'=4] {'dp'}, dimensions={0}, use_global_device_ids=true | all-gather | bytes 184320 | tf_op jit(solution)/shard_map/all_gather | solution.py:892
  31.5 11.6 %all-gather.1 = bf16[32,80,128]{2,1,0:T(8,128)(2,1)S(1)} all-gather(bf16[8,80,128]{2,1,0:T(8,128)(2,1)S(1)} %all_gather.35), channel_id=3, replica_groups=mesh['dp'=8,'fsdp'=4] {'fsdp'}, dimensions={0}, use_global_device_ids=true | all-gather | bytes 819200 | tf_op jit(solution)/shard_map/all_gather | solution.py:893
  85.3 26.6 %collective-permute-done.refs_1_ = bf16[4,256,768]{2,1,0:T(8,128)(2,1)} collective-permute-done((bf16[4,256,768]{2,1,0:T(8,128)(2,1)}, bf16[4,256,768]{2,1,0:T(8,128)(2,1)}, u32[]{:S(2)}, u32[]{:S(2)}) %collective-permute-start) | collective-permute-done | bytes 1572896 | tf_op jit(solution)/shard_map/ppermute | solution.py:61
  132.5 14.2 %collective-permute-done.2.refs_3_ = bf16[2,256,768]{2,1,0:T(8,128)(2,1)S(1)} collective-permute-done((bf16[2,256,768]{2,1,0:T(8,128)(2,1)}, bf16[2,256,768]{2,1,0:T(8,128)(2,1)S(1)}, u32[]{:S(2)}, u32[]{:S(2)}) %collective-permute-start.2) | collective-permute-done | bytes 786464 | tf_op jit(solution)/shard_map/ppermute | solution.py:61
  147.1 40.0 %all-to-all-done.1 = bf16[8,64,2048]{2,1,0:T(8,128)(2,1)} async-done(((bf16[8,64,2048]{2,1,0:T(8,128)(2,1)}), bf16[8,64,2048]{2,1,0:T(8,128)(2,1)}, u32[]{:S(2)}, u32[]{:S(2)}) %all-to-all-start.1) | async-done | bytes 2097184 | tf_op jit(solution)/shard_map/all_to_all | solution.py:866
  198.7 11.3 %key_value.1 = (bf16[8,2,256,256]{3,2,1,0:T(8,128)(2,1)S(1)}, bf16[8,2,80,128]{3,2,1,0:T(8,128)(2,1)S(1)}, bf16[8,2,112,256]{3,2,1,0:T(8,128)(2,1)}) custom-call(s32[2]{0:T(128)S(1)} %pad_add_fusion.place_ref, bf16[512,2048]{1,0:T(8,128)(2,1)} %copy-done.57, bf16[512,128]{1,0:T(8,128)(2,1)S(1)} %convolution_convert_fusion.u_ref, ...), custom_call_target="tpu_custom_call" | custom-call | flops 2147483648 | bytes 6291456 | tf_op jit(solution)/shard_map/key_value/pallas_call | solution.py:989
  233.0 14.4 %query.1 = (bf16[2048,512]{1,0:T(8,128)(2,1)S(1)}, bf16[4096,512]{1,0:T(8,128)(2,1)}) custom-call(s32[2]{0:T(128)S(1)} %pad_add_fusion.place_ref, bf16[512,2048]{1,0:T(8,128)(2,1)} %copy-done.57, bf16[512,128]{1,0:T(8,128)(2,1)S(1)} %convolution_convert_fusion.u_ref, bf16[4,128,512]{2,1,0:T(8,128)(2,1)S(1)} %copy-done.30, f32[32,512]{1,0:T(8,128)S(1)} %copy-done.37, ...), custom_call_target="tpu_custom_call" | custom-call | flops 4294967296 | bytes 16777216 | tf_op jit(solution)/shard_map/query/pallas_call | solution.py:1005
  270.8 19.7 %attend.1 = (bf16[512,2048]{1,0:T(8,128)(2,1)}, bf16[2048,512]{1,0:T(8,128)(2,1)}, f32[8,8,512]{2,1,0:T(8,128)}, bf16[8,2,2,160,128]{4,3,2,1,0:T(8,128)(2,1)}) custom-call(s32[1]{0:T(128)} %bitcast.prev_ref, bf16[8,2,256,256]{3,2,1,0:T(8,128)(2,1)} %copy-done.8, bf16[8,2,112,256]{3,2,1,0:T(8,128)(2,1)} %collective-permute-done.10.msg_ref, ...), custom_call_target="tpu_custom_call" | custom-call | flops 2013265920 | bytes 14680064 | tf_op jit(solution)/shard_map/attend/pallas_call | solution.py:57
  302.8 13.0 %output_projection.1 = (f32[512,2048]{1,0:T(8,128)}, bf16[512,2048]{1,0:T(8,128)(2,1)S(1)}, bf16[512,128]{1,0:T(8,128)(2,1)S(1)}, f32[512,1]{1,0:T(8,128)S(1)}) custom-call(s32[2]{0:T(128)S(1)} %pad_add_fusion.place_ref, bf16[512,2048]{1,0:T(8,128)(2,1)S(1)} %copy-done.55, bf16[2048,128]{1,0:T(8,128)(2,1)S(1)} %copy-done.51, ...), custom_call_target="tpu_custom_call" | custom-call | flops 4294967296 | bytes 20971520 | tf_op jit(solution)/shard_map/output_projection/pallas_call | solution.py:57
  318.4 22.9 %collective-permute-done.23.refs_1_ = bf16[256,2048]{1,0:T(8,128)(2,1)S(1)} collective-permute-done((bf16[256,2048]{1,0:T(8,128)(2,1)S(1)}, bf16[256,2048]{1,0:T(8,128)(2,1)S(1)}, u32[]{:S(2)}, u32[]{:S(2)}) %collective-permute-start.23) | collective-permute-done | bytes 1048608 | tf_op jit(solution)/shard_map/ppermute | solution.py:61
  346.1 10.1 %collective-permute-done.25.refs_3_ = bf16[256,1024]{1,0:T(8,128)(2,1)} collective-permute-done((bf16[256,1024]{1,0:T(8,128)(2,1)}, bf16[256,1024]{1,0:T(8,128)(2,1)}, u32[]{:S(2)}, u32[]{:S(2)}) %collective-permute-start.25) | collective-permute-done | bytes 524320 | tf_op jit(solution)/shard_map/ppermute | solution.py:61
  362.5 37.9 %feed_forward.4 = (bf16[1024,2048]{1,0:T(8,128)(2,1)}, bf16[1024,2048]{1,0:T(8,128)(2,1)}) custom-call(bf16[8,256,3072]{2,1,0:T(8,128)(2,1)} %bitcast.153, bf16[8,256,3072]{2,1,0:T(8,128)(2,1)} %bitcast.154, bf16[8,256,3072]{2,1,0:T(8,128)(2,1)} %bitcast.155, bf16[256,2048]{1,0:T(8,128)(2,1)} %copy-done.66, bf16[256,2048]{1,0:T(8,128)(2,1)} %copy-done.69, ...), custom_call_target="tpu_custom_call" | custom-call | flops 25769803776 | bytes 50331648 | tf_op jit(solution)/shard_map/feed_forward/pallas_call | solution.py:701
  438.0 37.9 %feed_forward.5 = (bf16[1024,2048]{1,0:T(8,128)(2,1)}, bf16[1024,2048]{1,0:T(8,128)(2,1)}) custom-call(bf16[8,256,3072]{2,1,0:T(8,128)(2,1)} %bitcast.156, bf16[8,256,3072]{2,1,0:T(8,128)(2,1)} %bitcast.157, bf16[8,256,3072]{2,1,0:T(8,128)(2,1)} %bitcast.158, bf16[256,2048]{1,0:T(8,128)(2,1)} %copy-done.65, ...), custom_call_target="tpu_custom_call" | custom-call | flops 25769803776 | bytes 50331648 | tf_op jit(solution)/shard_map/feed_forward/pallas_call | solution.py:701
  475.9 43.9 %feed_forward.6 = (bf16[2,256,1024]{2,1,0:T(8,128)(2,1)}, bf16[2,256,1024]{2,1,0:T(8,128)(2,1)}, bf16[2,256,1024]{2,1,0:T(8,128)(2,1)}, bf16[2,256,1024]{2,1,0:T...) custom-call(bf16[8,256,3072]{2,1,0:T(8,128)(2,1)} %bitcast.159, ...), custom_call_target="tpu_custom_call" | custom-call | flops 25769803776 | bytes 50331648 | tf_op jit(solution)/shard_map/feed_forward/pallas_call | solution.py:701
  524.0 43.5 %feed_forward.7 = (bf16[2,256,1024]{2,1,0:T(8,128)(2,1)}, bf16[2,256,1024]{2,1,0:T(8,128)(2,1)}, bf16[2,256,1024]{2,1,0:T(8,128)(2,1)}, bf16[2,256,1024]{2,1,0:T...) custom-call(bf16[8,256,3072]{2,1,0:T(8,128)(2,1)} %bitcast.162, ...), custom_call_target="tpu_custom_call" | custom-call | flops 25769803776 | bytes 50331648 | tf_op jit(solution)/shard_map/feed_forward/pallas_call | solution.py:701
  588.1 15.7 %collective-permute-done.39.from_x.refs_2_ = bf16[2,256,1024]{2,1,0:T(8,128)(2,1)} collective-permute-done((bf16[2,256,1024]{2,1,0:T(8,128)(2,1)}, bf16[2,256,1024]{2,1,0:T(8,128)(2,1)}, u32[]{:S(2)}, u32[]{:S(2)}) %collective-permute-start.39) | collective-permute-done | bytes 1048608 | tf_op jit(solution)/shard_map/ppermute | solution.py:61
  649.7 10.3 %output_projection_back.1 = (bf16[2048,512]{1,0:T(8,128)(2,1)}, f32[16,2048]{1,0:T(8,128)}) custom-call(bf16[512,2048]{1,0:T(8,128)(2,1)} %copy-done.33, bf16[4,8,256,512]{3,2,1,0:T(8,128)(2,1)} %copy-done.59, bf16[2048,128]{1,0:T(8,128)(2,1)} %pad.29.ao_ref, bf16[512,128]{1,0:T(8,128)(2,1)} %copy-done.52, bf16[512,2048]{1,0:T(8,128)(2,1)} %get-tuple-element.646.o_ref), custom_call_target="tpu_custom_call" | custom-call | flops 4294967296 | bytes 12582912 | tf_op jit(solution)/shard_map/output_projection_back/pallas_call | solution.py:1255
  660.0 26.7 %attend_back.1 = (bf16[4,512,512]{2,1,0:T(8,128)(2,1)}, f32[8,256,64]{2,1,0:T(8,128)}, f32[8,2,256,256]{3,2,1,0:T(8,128)}, f32[8,2,2,160,128]{4,3,2,1,0:T(8,128)...) custom-call(s32[1]{0:T(128)} %bitcast.prev_ref, bf16[8,2,256,256]{3,2,1,0:T(8,128)(2,1)} %copy-done.8, ...), custom_call_target="tpu_custom_call" | custom-call | flops 6039797760 | bytes 25165824 | tf_op jit(solution)/shard_map/attend_back/pallas_call | solution.py:1256
  705.3 12.5 %query_input_gradient.1 = (f32[512,2048]{1,0:T(8,128)}, f32[512,128]{1,0:T(8,128)}, f32[32,2048]{1,0:T(8,128)}) custom-call(bf16[4,512,512]{2,1,0:T(8,128)(2,1)} %get-tuple-element.935.gq_ref, bf16[4,8,256,768]{3,2,1,0:T(8,128)(2,1)} %bitcast_dynamic-update-slice_fusion.10.wq_ref.wkv_ref, bf16[512,128]{1,0:T(8,128)(2,1)} %copy-done.28, ...), custom_call_target="tpu_custom_call" | custom-call | flops 4294967296 | bytes 16777216 | tf_op jit(solution)/shard_map/query_input_gradient/pallas_call | solution.py:57
  720.2 23.2 %collective-permute-done.51.refs_1_ = bf16[8,2,80,128]{3,2,1,0:T(8,128)(2,1)} collective-permute-done((bf16[8,2,80,128]{3,2,1,0:T(8,128)(2,1)}, bf16[8,2,80,128]{3,2,1,0:T(8,128)(2,1)}, u32[]{:S(2)}, u32[]{:S(2)}) %collective-permute-start.51) | collective-permute-done | bytes 327712 | tf_op jit(solution)/shard_map/ppermute | solution.py:837
  754.5 11.5 %key_value_back.1 = (bf16[4,512,256]{2,1,0:T(8,128)(2,1)}, f32[4,128,64]{2,1,0:T(8,128)}, bf16[512,128]{1,0:T(8,128)(2,1)}, f32[4,32,256]{2,1,0:T(8,128)}, f32[32,2048]{1,0:T(8,128)}) custom-call(f32[8,2,256,256]{3,2,1,0:T(8,128)} %get-tuple-element.965.gn_ref, bf16[8,2,144,256]{3,2,1,0:T(8,128)(2,1)} %collective-permute-done.49.back_ref, ...), custom_call_target="tpu_custom_call" | custom-call | flops 67108864 | bytes 8388608 | tf_op jit(solution)/shard_map/key_value_back/pallas_call | solution.py:1368
  766.0 13.4 %input_gradient.1 = (bf16[512,2048]{1,0:T(8,128)(2,1)}, f32[1,2048]{1,0:T(1,128)}) custom-call(f32[512,2048]{1,0:T(8,128)} %get-tuple-element.964.part_ref, bf16[4,512,256]{2,1,0:T(8,128)(2,1)} %get-tuple-element.972.gkv_ref, bf16[4,8,256,768]{3,2,1,0:T(8,128)(2,1)} %bitcast_dynamic-update-slice_fusion.10.wq_ref.wkv_ref, ...), custom_call_target="tpu_custom_call" | custom-call | flops 2147483648 | bytes 31457280 | tf_op jit(solution)/shard_map/input_gradient/pallas_call | solution.py:1372
  793.3 16.5 %all-to-all-done.6 = bf16[32,80,128]{2,1,0:T(8,128)(2,1)S(1)} async-done(((bf16[32,80,128]{2,1,0:T(8,128)(2,1)}), bf16[32,80,128]{2,1,0:T(8,128)(2,1)S(1)}, u32[]{:S(2)}, u32[]{:S(2)}) %all-to-all-start.6) | async-done | bytes 655392 | tf_op jit(solution)/shard_map/all_to_all | solution.py:1398
  817.5 22.3 %all-to-all-done.5 = bf16[8,32,2048]{2,1,0:T(8,128)(2,1)S(1)} async-done(((bf16[8,32,2048]{2,1,0:T(8,128)(2,1)}), bf16[8,32,2048]{2,1,0:T(8,128)(2,1)S(1)}, u32[]{:S(2)}, u32[]{:S(2)}) %all-to-all-start.5) | async-done | bytes 1048608 | tf_op jit(solution)/shard_map/all_to_all | solution.py:866
  (426 shorter events, 319.2 us)
Async XLA Ops:
  7.2 44.8 %all-gather.10.cloned.1.call-start = ((), (), s32[]{:S(2)}) async-start(), calls=%async_computation.7 | async-start | bytes 3538944 | tf_op jit(solution)/shard_map/all_gather | solution.py:914
  54.7 58.5 %all-to-all-start = ((bf16[8,64,2048]{2,1,0:T(8,128)(2,1)}), bf16[8,64,2048]{2,1,0:T(8,128)(2,1)}, u32[]{:S(2)}, u32[]{:S(2)}) async-start(bf16[8,64,2048]{2,1,0:T(8,128)(2,1)} %bitcast.139), calls=%async_computation | async-start | bytes 4194304 | tf_op jit(solution)/shard_map/all_to_all | solution.py:845
  75.0 37.0 %collective-permute-start = (bf16[4,256,768]{2,1,0:T(8,128)(2,1)}, bf16[4,256,768]{2,1,0:T(8,128)(2,1)}, u32[]{:S(2)}, u32[]{:S(2)}) collective-permute-start(bf16[4,256,768]{2,1,0:T(8,128)(2,1)} %constant_dynamic-slice_fusion.3), channel_id=1, source_target_pairs={{0,1},{1,0},{2,3},{3,2},{4,5},{5,4},{6,7},{7,6},{8,9},{9,8},{10,11... | collective-permute-start | bytes 4718600 | tf_op jit(solution)/shard_map/ppermute | solution.py:61
  116.2 70.8 %all-to-all-start.1 = ((bf16[8,64,2048]{2,1,0:T(8,128)(2,1)}), bf16[8,64,2048]{2,1,0:T(8,128)(2,1)}, u32[]{:S(2)}, u32[]{:S(2)}) async-start(bf16[8,64,2048]{2,1,0:T(8,128)(2,1)} %reorder.3), calls=%async_computation.1 | async-start | bytes 4194304 | tf_op jit(solution)/shard_map/all_to_all | solution.py:866
  121.0 66.9 %all-gather.12.cloned.1.call-start = ((), (), s32[]{:S(2)}) async-start(), calls=%async_computation.8 | async-start | bytes 2359296 | tf_op jit(solution)/shard_map/all_gather | solution.py:919
  121.7 236.7 %all-gather.14.cloned.1.call-start = ((), (), s32[]{:S(2)}) async-start(), calls=%async_computation.9 | async-start | bytes 14155776 | tf_op jit(solution)/shard_map/all_gather | solution.py:975
  187.0 288.9 %all-gather.16.cloned.1.call-start = ((), (), s32[]{:S(2)}) async-start(), calls=%async_computation.10 | async-start | bytes 14155776 | tf_op jit(solution)/shard_map/all_gather | solution.py:1034
  254.8 37.6 %collective-permute-start.13 = (bf16[256,2048]{1,0:T(8,128)(2,1)}, bf16[256,2048]{1,0:T(8,128)(2,1)}, u32[]{:S(2)}, u32[]{:S(2)}) collective-permute-start(bf16[256,2048]{1,0:T(8,128)(2,1)} %get-tuple-element.852.refs_5_.gy_ref), channel_id=1, source_target_pairs={{0,1},{1,0},{2,3},{3,2},{4,5},{5,4},{6,7},{7,6},{8,9},{9,8},{10,11... | collective-permute-start | bytes 3145736 | tf_op jit(solution)/shard_map/ppermute | solution.py:61
  358.5 41.9 %collective-permute-start.27 = (bf16[256,2048]{1,0:T(8,128)(2,1)S(1)}, bf16[256,2048]{1,0:T(8,128)(2,1)}, u32[]{:S(2)}, u32[]{:S(2)}) collective-permute-start(bf16[256,2048]{1,0:T(8,128)(2,1)S(1)} %get-tuple-element.779.refs_0_), channel_id=1, source_target_pairs={{0,1},{1,0},{2,3},{3,2},{4,5},{5,4},{6,7},{7,6},{8,9},{9,8},{10,11... | collective-permute-start | bytes 3145736 | tf_op jit(solution)/shard_map/ppermute | solution.py:61
  358.9 41.5 %collective-permute-start.28 = (bf16[256,2048]{1,0:T(8,128)(2,1)S(1)}, bf16[256,2048]{1,0:T(8,128)(2,1)}, u32[]{:S(2)}, u32[]{:S(2)}) collective-permute-start(bf16[256,2048]{1,0:T(8,128)(2,1)S(1)} %get-tuple-element.779.refs_0_), channel_id=1, source_target_pairs={{0,2},{1,3},{2,0},{3,1},{4,6},{5,7},{6,4},{7,5},{8,10},{9,11},{10,... | collective-permute-start | bytes 3145736 | tf_op jit(solution)/shard_map/ppermute | solution.py:65
  359.4 44.2 %collective-permute-start.29 = (bf16[256,2048]{1,0:T(8,128)(2,1)S(1)}, bf16[256,2048]{1,0:T(8,128)(2,1)}, u32[]{:S(2)}, u32[]{:S(2)}) collective-permute-start(bf16[256,2048]{1,0:T(8,128)(2,1)S(1)} %copy-done.10), channel_id=1, source_target_pairs={{0,1},{1,0},{2,3},{3,2},{4,5},{5,4},{6,7},{7,6},{8,9},{9,8},{10,11... | collective-permute-start | bytes 3145736 | tf_op jit(solution)/shard_map/ppermute | solution.py:61
  361.1 42.6 %collective-permute-start.30 = (bf16[256,2048]{1,0:T(8,128)(2,1)S(1)}, bf16[256,2048]{1,0:T(8,128)(2,1)}, u32[]{:S(2)}, u32[]{:S(2)}) collective-permute-start(bf16[256,2048]{1,0:T(8,128)(2,1)S(1)} %copy-done.10), channel_id=1, source_target_pairs={{0,2},{1,3},{2,0},{3,1},{4,6},{5,7},{6,4},{7,5},{8,10},{9,11},{10,... | collective-permute-start | bytes 3145736 | tf_op jit(solution)/shard_map/ppermute | solution.py:65
  519.9 47.6 %collective-permute-start.35 = (bf16[2,256,1024]{2,1,0:T(8,128)(2,1)}, bf16[2,256,1024]{2,1,0:T(8,128)(2,1)S(1)}, u32[]{:S(2)}, u32[]{:S(2)}) collective-permute-start(bf16[2,256,1024]{2,1,0:T(8,128)(2,1)} %get-tuple-element.772), channel_id=1, source_target_pairs={{0,1},{1,0},{2,3},{3,2},{4,5},{5,4},{6,7},{7,6},{8,9},{9,8},{10,11... | collective-permute-start | bytes 3145736 | tf_op jit(solution)/shard_map/ppermute | solution.py:61
  521.6 45.9 %collective-permute-start.36 = (bf16[2,256,1024]{2,1,0:T(8,128)(2,1)}, bf16[2,256,1024]{2,1,0:T(8,128)(2,1)S(1)}, u32[]{:S(2)}, u32[]{:S(2)}) collective-permute-start(bf16[2,256,1024]{2,1,0:T(8,128)(2,1)} %get-tuple-element.773), channel_id=1, source_target_pairs={{0,2},{1,3},{2,0},{3,1},{4,6},{5,7},{6,4},{7,5},{8,10},{9,11},{10,... | collective-permute-start | bytes 3145736 | tf_op jit(solution)/shard_map/ppermute | solution.py:65
  522.4 45.1 %collective-permute-start.37 = (bf16[2,256,1024]{2,1,0:T(8,128)(2,1)}, bf16[2,256,1024]{2,1,0:T(8,128)(2,1)S(1)}, u32[]{:S(2)}, u32[]{:S(2)}) collective-permute-start(bf16[2,256,1024]{2,1,0:T(8,128)(2,1)} %get-tuple-element.776), channel_id=1, source_target_pairs={{0,1},{1,0},{2,3},{3,2},{4,5},{5,4},{6,7},{7,6},{8,9},{9,8},{10,11... | collective-permute-start | bytes 3145736 | tf_op jit(solution)/shard_map/ppermute | solution.py:61
  522.8 44.8 %collective-permute-start.38 = (bf16[2,256,1024]{2,1,0:T(8,128)(2,1)}, bf16[2,256,1024]{2,1,0:T(8,128)(2,1)}, u32[]{:S(2)}, u32[]{:S(2)}) collective-permute-start(bf16[2,256,1024]{2,1,0:T(8,128)(2,1)} %get-tuple-element.777), channel_id=1, source_target_pairs={{0,2},{1,3},{2,0},{3,1},{4,6},{5,7},{6,4},{7,5},{8,10},{9,11},{10,... | collective-permute-start | bytes 3145736 | tf_op jit(solution)/shard_map/ppermute | solution.py:65
  629.2 57.6 %all-to-all-start.2 = ((bf16[8,32,2048]{2,1,0:T(8,128)(2,1)}), bf16[8,32,2048]{2,1,0:T(8,128)(2,1)}, u32[]{:S(2)}, u32[]{:S(2)}) async-start(bf16[8,32,2048]{2,1,0:T(8,128)(2,1)} %bitcast.113), calls=%async_computation.2 | async-start | bytes 2097152 | tf_op jit(solution)/shard_map/all_to_all | solution.py:845
  633.4 53.3 %collective-permute-start.47 = (bf16[2,256,1024]{2,1,0:T(8,128)(2,1)}, bf16[2,256,1024]{2,1,0:T(8,128)(2,1)}, u32[]{:S(2)}, u32[]{:S(2)}) collective-permute-start(bf16[2,256,1024]{2,1,0:T(8,128)(2,1)} %get-tuple-element.923), channel_id=1, source_target_pairs={{0,1},{1,0},{2,3},{3,2},{4,5},{5,4},{6,7},{7,6},{8,9},{9,8},{10,11... | collective-permute-start | bytes 3145736 | tf_op jit(solution)/shard_map/ppermute | solution.py:61
  634.9 51.9 %collective-permute-start.48 = (bf16[2,256,1024]{2,1,0:T(8,128)(2,1)}, bf16[2,256,1024]{2,1,0:T(8,128)(2,1)}, u32[]{:S(2)}, u32[]{:S(2)}) collective-permute-start(bf16[2,256,1024]{2,1,0:T(8,128)(2,1)} %get-tuple-element.924), channel_id=1, source_target_pairs={{0,2},{1,3},{2,0},{3,1},{4,6},{5,7},{6,4},{7,5},{8,10},{9,11},{10,... | collective-permute-start | bytes 3145736 | tf_op jit(solution)/shard_map/ppermute | solution.py:65
  689.0 54.3 %all-to-all-start.3 = ((bf16[8,32,2048]{2,1,0:T(8,128)(2,1)}), bf16[8,32,2048]{2,1,0:T(8,128)(2,1)}, u32[]{:S(2)}, u32[]{:S(2)}) async-start(bf16[8,32,2048]{2,1,0:T(8,128)(2,1)} %reorder.4), calls=%async_computation.3 | async-start | bytes 2097152 | tf_op jit(solution)/shard_map/all_to_all | solution.py:866
  694.0 49.4 %collective-permute-start.49 = (bf16[8,2,144,256]{3,2,1,0:T(8,128)(2,1)}, bf16[8,2,144,256]{3,2,1,0:T(8,128)(2,1)}, u32[]{:S(2)}, u32[]{:S(2)}) collective-permute-start(bf16[8,2,144,256]{3,2,1,0:T(8,128)(2,1)} %get-tuple-element.942), channel_id=1, source_target_pairs={{1,0},{2,1},{3,2},{5,4},{6,5},{7,6},{9,8},{10,9},{11,10},{13,12},{... | collective-permute-start | bytes 3538952 | tf_op jit(solution)/shard_map/ppermute | solution.py:1296
  697.9 45.4 %collective-permute-start.52 = (bf16[256,1024]{1,0:T(8,128)(2,1)}, bf16[256,1024]{1,0:T(8,128)(2,1)S(1)}, u32[]{:S(2)}, u32[]{:S(2)}) collective-permute-start(bf16[256,1024]{1,0:T(8,128)(2,1)} %get-tuple-element.948), channel_id=1, source_target_pairs={{0,2},{1,3},{2,0},{3,1},{4,6},{5,7},{6,4},{7,5},{8,10},{9,11},{10,... | collective-permute-start | bytes 1572872 | tf_op jit(solution)/shard_map/ppermute | solution.py:65
  700.7 42.7 %collective-permute-start.53 = (bf16[256,1024]{1,0:T(8,128)(2,1)}, bf16[256,1024]{1,0:T(8,128)(2,1)S(1)}, u32[]{:S(2)}, u32[]{:S(2)}) collective-permute-start(bf16[256,1024]{1,0:T(8,128)(2,1)} %get-tuple-element.949), channel_id=1, source_target_pairs={{0,1},{1,0},{2,3},{3,2},{4,5},{5,4},{6,7},{7,6},{8,9},{9,8},{10,11... | collective-permute-start | bytes 1572872 | tf_op jit(solution)/shard_map/ppermute | solution.py:61
  704.0 39.4 %collective-permute-start.51 = (bf16[8,2,80,128]{3,2,1,0:T(8,128)(2,1)}, bf16[8,2,80,128]{3,2,1,0:T(8,128)(2,1)}, u32[]{:S(2)}, u32[]{:S(2)}) collective-permute-start(bf16[8,2,80,128]{3,2,1,0:T(8,128)(2,1)} %get-tuple-element.943), channel_id=1, source_target_pairs={{3,0},{7,4},{11,8},{15,12},{19,16},{23,20},{27,24},{31,28}} | collective-permute-start | bytes 983048 | tf_op jit(solution)/shard_map/ppermute | solution.py:837
  (120 other events, 2090.5 us)
Sparse Core Ops, SparseCore 0:
  10.2 41.7 all-gather.9
  123.4 56.7 all-gather.11
  187.2 114.6 all-gather.13
  303.4 114.9 all-gather.15

commit v3 on v2

--- a/solution.py
+++ b/solution.py
@@ -593,23 +593,22 @@
         dbo_ref[...] += dbo
 
 
-def load_rows(refs, rows_ref):
+def row_copies(refs, rows_ref, sems, r):
+    tile, width = rows_ref.shape[1:]
+    half_tile, half = tile // 2, width // 2
     if len(refs) == 1:
-        rows_ref[...] = refs[0][...]
-        return
-    own, from_x, from_y, diagonal_x, diagonal_y = refs
-    count, width = own.shape
-
-    @pl.when(pl.program_id(0) == 0)
-    def _():
-        rows_ref[:count] = own[...]
-        rows_ref[count:] = from_x[...]
-
-    @pl.when(pl.program_id(0) == 1)
-    def _():
-        rows_ref[:count] = from_y[...]
-        rows_ref[count:, : width // 2] = diagonal_x[...]
-        rows_ref[count:, width // 2 :] = diagonal_y[...]
+        parts = [(refs[0].at[r * tile : (r + 1) * tile], rows_ref.at[r])]
+    elif r == 0:
+        parts = [(refs[i], rows_ref.at[0, i * half_tile : (i + 1) * half_tile]) for i in range(2)]
+    else:
+        parts = [(refs[2], rows_ref.at[1, :half_tile])]
+        parts += [
+            (refs[3 + i], rows_ref.at[1, half_tile:, i * half : (i + 1) * half]) for i in range(2)
+        ]
+    return [
+        pltpu.make_async_copy(source, target, sems.at[r, i])
+        for i, (source, target) in enumerate(parts)
+    ]
 
 
 def store_rows(value_ref, refs):
@@ -628,22 +627,34 @@
             ref[1] = value_ref[count:, half:].astype(BF16)
 
 
-def ffn_kernel(pieces, carries, split, wg_ref, wu_ref, wd_ref, *refs):
+def ffn_kernel(pieces, carries, wg_ref, wu_ref, wd_ref, *refs):
     h2_refs, gy_refs = refs[:pieces], refs[pieces : 2 * pieces]
     carried = refs[2 * pieces : 2 * pieces + carries]
-    *out_refs, h2_ref, gy_ref, out_acc, gh_acc = refs[2 * pieces + carries :]
-    j = pl.program_id(1)
-
-    @pl.when(j == 0)
+    *out_refs, h2_ref, gy_ref, out_acc, gh_acc, h2_sems, gy_sems = refs[2 * pieces + carries :]
+    r, j = pl.program_id(0), pl.program_id(1)
+    copies = [
+        row_copies(h2_refs, h2_ref, h2_sems, tile) + row_copies(gy_refs, gy_ref, gy_sems, tile)
+        for tile in range(2)
+    ]
+
+    @pl.when((r == 0) & (j == 0))
     def _():
-        load_rows(h2_refs, h2_ref)
-        load_rows(gy_refs, gy_ref)
-
+        for copy in copies[0] + copies[1]:
+            copy.start()
+        for copy in copies[0]:
+            copy.wait()
+
+    @pl.when((r == 1) & (j == 0))
+    def _():
+        for copy in copies[1]:
+            copy.wait()
+
+    h2, gy = h2_ref[r], gy_ref[r]
     shape = (wg_ref.shape[0] * wg_ref.shape[1], wg_ref.shape[2])
     wg, wu, wd = wg_ref[...].reshape(shape), wu_ref[...].reshape(shape), wd_ref[...].reshape(shape)
-    gate = dot(h2_ref[...], wg)
-    up = dot(h2_ref[...], wu)
-    g_hid = dot(gy_ref[...], wd)
+    gate = dot(h2, wg)
+    up = dot(h2, wu)
+    g_hid = dot(gy, wd)
     sig = 1.0 / (1.0 + jnp.exp(-gate))
     silu = gate * sig
     hid = (silu * up).astype(BF16)
@@ -683,12 +694,7 @@
     def weight_spec(kind):
         return pl.BlockSpec((groups, depth, tile), lambda r, j: (0, 0, kind * tiles + j))
 
-    if pieces == 1:
-        piece_specs = [row_spec]
-    else:
-        piece_specs = [
-            pl.BlockSpec(part.shape, lambda r, j: (0, 0), pipeline_mode=pl.Buffered(1)) for part in h2
-        ]
+    piece_specs = [pl.BlockSpec(memory_space=pl.ANY)] * pieces
     if split and pieces > 1:
         count, half = row_tile // 2, width // 2
         moving = pl.BlockSpec((1, count, half), lambda r, j: (r, 0, 0))
@@ -699,16 +705,16 @@
         out_specs = [row_spec, row_spec]
         out_shape = [jax.ShapeDtypeStruct((total, width), BF16)] * 2
     outs = pl.pallas_call(
-        functools.partial(ffn_kernel, pieces, len(carried), split),
+        functools.partial(ffn_kernel, pieces, len(carried)),
         grid=(total // row_tile, tiles),
         in_specs=[weight_spec(0), weight_spec(1), weight_spec(2)]
         + piece_specs * 2
-        + [pl.BlockSpec((row_tile, width), lambda r, j: (r, 0), pipeline_mode=pl.Buffered(1))]
-        * len(carried),
+        + [row_spec] * len(carried),
         out_specs=out_specs,
         out_shape=out_shape,
-        scratch_shapes=[pltpu.VMEM((row_tile, width), BF16)] * 2
-        + [pltpu.VMEM((row_tile, width), F32)] * 2,
+        scratch_shapes=[pltpu.VMEM((2, row_tile, width), BF16)] * 2
+        + [pltpu.VMEM((row_tile, width), F32)] * 2
+        + [pltpu.SemaphoreType.DMA((2, 3))] * 2,
         compiler_params=params(60, ("arbitrary", "arbitrary")),
         cost_estimate=cost(4 * total * width * cols, 2 * width * cols * (total // row_tile) + 12 * total * width),
         name="feed_forward",
@@ -865,6 +871,23 @@
     groups, share, width = ordered.shape
     settled = lax.all_to_all(ordered, "dp", split_axis=0, concat_axis=0, tiled=True)
     return settled.reshape(groups * share, width)
+
+
+def halved(table):
+    n_dp, n_f = lax.axis_size("dp"), lax.axis_size("fsdp")
+    dp_bits, f_bits = n_dp.bit_length() - 1, n_f.bit_length() - 1
+    bits = [("dp", b) for b in range(dp_bits)][::-1] + [("fsdp", b) for b in range(f_bits)][::-1]
+    left = table.reshape((2,) * len(bits) + table.shape[1:])
+    order = [("dp", 0)] + [("fsdp", b) for b in range(f_bits)] + [("dp", b) for b in range(1, dp_bits)]
+    for axis, bit in order:
+        at = bits.index((axis, bit))
+        bits.pop(at)
+        mine = (lax.axis_index(axis) >> bit) & 1
+        keep = lax.dynamic_index_in_dim(left, mine, at, keepdims=False)
+        send = lax.dynamic_index_in_dim(left, 1 - mine, at, keepdims=False).astype(BF16)
+        perm = [(i, i ^ (1 << bit)) for i in range(lax.axis_size(axis))]
+        left = keep + lax.ppermute(send, axis, perm).astype(F32)
+    return left
 
 
 def shards(
@@ -912,11 +935,11 @@
         name="pack_attention",
     )(wq, wk, wv, wo)
     w_qkv = lax.all_gather(w_qkv, "dp", axis=0, tiled=False)
+    w_out = lax.all_gather(w_out, "dp", axis=0, tiled=False)
     near, spread = together(
         (functools.partial(columns_first, size=n_f), columns_share(w_qkv, n_f, group)),
         (deal_out, after(cotangent[0].reshape(total, width), small)),
     )
-    w_out = lax.all_gather(after(w_out, near[-1]), "dp", axis=0, tiled=False)
     share_micro = group * (total // n_dp) // rows
     order = lax.dynamic_index_in_dim(dealing, share_micro, 0, keepdims=False)
 
@@ -925,7 +948,7 @@
 
     hidden = wg.shape[1]
     tile = hidden // 4
-    cuts = (0, 2 * tile, hidden)
+    cuts = (0, 3 * tile, hidden)
     w_ffn = pl.pallas_call(
         functools.partial(pack_ffn_kernel, cuts),
         out_shape=[
@@ -966,8 +989,9 @@
     prepared = (h1, u, a_qkv, a_o, b_q_t, b_kv_t, b_o, fq, fk, fq_t, fk_t, cos_t, sin_t)
     inverse = jnp.argsort(dealing, axis=1).astype(jnp.int32)
     prepared += (inverse,)
-    second, cot, prepared = together(
+    second, out_near, cot, prepared = together(
         (columns_second, *near),
+        (functools.partial(columns_first, size=n_f), columns_share(w_out, n_f, group)),
         (lambda spread, order: deal_in(reordered(spread, order)), spread, order),
         (lambda *arrays: arrays, *prepared),
     )
@@ -1019,9 +1043,11 @@
     forward_one = [(i, i + 1) for i in range(n_f - 1)]
     backward_one = [(i + 1, i) for i in range(n_f - 1)]
 
-    (kv_natural, totals, message), out_near = together(
-        (key_values, h1, u, *qkv_pieces),
-        (functools.partial(columns_first, size=n_f), columns_share(w_out, n_f, group)),
+    gy_both = jnp.where(valid, cot, jnp.zeros_like(cot))
+    gy = [gy_both[m * rows : (m + 1) * rows] for m in range(micro)]
+    gather = functools.partial(gather_first, size=n_f)
+    (kv_natural, totals, message), out_second = together(
+        (key_values, h1, u, *qkv_pieces), (columns_second, *out_near)
     )
 
     def send_on(message, totals):
@@ -1046,8 +1072,6 @@
     den_spec = pl.BlockSpec((1, 8, total), lambda g: (g, 0, 0))
     base_spec = pl.BlockSpec((1, micro, AUG, 128), lambda g: (g, 0, 0, 0))
     attend_flops = H * total * 2 * (192 * 64 + 128 * 128 + 160 * 128 + 192 * 64)
-    gy_both = jnp.where(valid, cot, jnp.zeros_like(cot))
-    gy = [gy_both[m * rows : (m + 1) * rows] for m in range(micro)]
     attend = pl.pallas_call(
         functools.partial(attend_kernel, micro),
         grid=(KEY_VALUE_HEADS,),
@@ -1066,17 +1090,15 @@
             jax.ShapeDtypeStruct((KEY_VALUE_HEADS, 8, total), F32),
             jax.ShapeDtypeStruct((KEY_VALUE_HEADS, micro, pairs, 2 * AUG, 128), BF16),
         ],
-        compiler_params=params(60),
+        compiler_params=params(40),
         cost_estimate=cost(attend_flops, 14 * MIB, 128 * H * total),
         name="attend",
     )
-    (o, o_t, den, states), gy_first, out_second = together(
+    (o, o_t, den, states), gy_first, out_pieces = together(
         (attend, has_prev, kv_natural, message, q_rot, q_feat, *bases),
-        (functools.partial(gather_first, size=n_f), gy[0]),
-        (columns_second, *out_near),
-    )
-    (out_pieces,) = together((columns_third, w_out, *out_second))
-
+        (gather, gy[0]),
+        (columns_third, w_out, *out_second),
+    )
     project_out = pl.pallas_call(
         functools.partial(out_kernel, depth, n_dp),
         grid=(1,),
@@ -1102,7 +1124,7 @@
     def assemble(*pieces):
         return assembled(pieces, group, quarter)
 
-    (h2_first,) = together((gather, h2[:rows]))
+    h2_first, w_qkv = together((gather, h2[:rows]), (assemble, *qkv_pieces))
     (h2_zero,) = together((gather_second, *h2_first))
 
     def piece(array, m):
@@ -1159,28 +1181,27 @@
 
     valid_rows = valid.astype(jnp.int32)
     def feed(split):
-        def run(h2, gy, weights, *carried):
-            return ffn(tile, split, h2, gy, weights, *carried)
+        def run(h2, gy, *carried):
+            return ffn(tile, split, h2, gy, w_ffn[1 if split else 0], *carried)
 
         return run
 
     scatter = functools.partial(scatter_first, size=n_f)
     head_zero, h2_first, gy_first = together(
-        (feed(False), h2_zero, gy_zero, w_ffn[0]), (gather, h2[rows:]), (gather, gy[1])
-    )
-    h2_one, gy_one, w_qkv = together(
-        (gather_second, *h2_first), (gather_second, *gy_first), (assemble, *qkv_pieces)
-    )
-    (head_one,) = together((feed(False), h2_one, gy_one, w_ffn[0]))
-    h2_zero = after(h2_zero[0], head_one[0]), *h2_zero[1:]
-    ((down_zero, gh_zero),) = together((feed(True), h2_zero, gy_zero, w_ffn[1], *head_zero))
-    gh_zero_terms, down_zero_terms, (down_one, gh_one) = together(
-        (scatter, *gh_zero),
-        (scatter, *down_zero),
-        (feed(True), h2_one, gy_one, w_ffn[1], *head_one),
-    )
-    gh_one_first, gh_zero_terms, w_out = together(
-        (scatter, *gh_one), (scatter_second, *gh_zero_terms), (assemble, *out_pieces)
+        (feed(False), h2_zero, gy_zero), (gather, h2[rows:]), (gather, gy[1])
+    )
+    (down_zero, gh_zero), h2_one, gy_one = together(
+        (feed(True), h2_zero, gy_zero, *head_zero),
+        (gather_second, *h2_first),
+        (gather_second, *gy_first),
+    )
+    head_one, gh_zero_terms, down_zero_terms = together(
+        (feed(False), h2_one, gy_one), (scatter, *gh_zero), (scatter, *down_zero)
+    )
+    (down_one, gh_one), gh_zero_terms, down_zero_terms = together(
+        (feed(True), h2_one, gy_one, *head_one),
+        (scatter_second, *gh_zero_terms),
+        (scatter_second, *down_zero_terms),
     )
 
     go_back = pl.pallas_call(
@@ -1244,27 +1265,26 @@
         cost_estimate=cost(3 * attend_flops, 24 * MIB, 128 * H * total),
         name="attend_back",
     )
-    gh_one_terms, down_zero_terms, zero = together(
-        (scatter_second, *gh_one_first),
-        (scatter_second, *down_zero_terms),
+    gh_one_terms, zero, result_zero, w_out = together(
+        (scatter, *gh_one),
         (functools.partial(mid_back, 0), gh_zero_terms, gy[0]),
-    )
-
-    def norm_to_heads(gh_one, gy_one, *zero):
+        (functools.partial(finish, 0), down_zero_terms),
+        (assemble, *out_pieces),
+    )
+    (gh_one_terms,) = together((scatter_second, *gh_one_terms))
+
+    def norm_to_output(gh_one, gy_one, *zero):
         gx2, gb, guo, *one = mid_back(1, gh_one, gy_one, *zero[:3])
         go_t, d_ao_t = go_back(gb, w_out, a_o, guo, o)
-        back = attend_back(
-            has_prev, kv_natural, message, states, q_rot, q_feat, go_t, o_t, den, fq, cos_t, sin_t
-        )
-        return back, gx2, d_ao_t, zero[3] + one[0], zero[4] + one[1]
-
-    def finish_and_deal(m, terms):
-        return deal_out(finish(m, terms))
-
-    (back, gx2, d_ao_t, dg2, d_bo_t), spread_zero, down_one_terms = together(
-        (norm_to_heads, gh_one_terms, gy[1], *zero),
-        (functools.partial(finish_and_deal, 0), down_zero_terms),
-        (scatter, *down_one),
+        return gx2, go_t, d_ao_t, zero[3] + one[0], zero[4] + one[1]
+
+    (gx2, go_t, d_ao_t, dg2, d_bo_t), down_one_terms = together(
+        (norm_to_output, gh_one_terms, gy[1], *zero), (scatter, *down_one)
+    )
+    back, down_one_terms, spread_zero = together(
+        (attend_back, has_prev, kv_natural, message, states, q_rot, q_feat, go_t, o_t, den, fq, cos_t, sin_t),
+        (scatter_second, *down_one_terms),
+        (deal_out, result_zero),
     )
     gq, d_fq, g_keys, g_states, g_message, g_total = back
 
@@ -1295,11 +1315,11 @@
     def exchange(g_message, g_total):
         return lax.ppermute(g_message, "fsdp", backward_one), shifted(g_total, n_f, -1)
 
-    (gh_q, gu_q, d_bq_t), (g_message, g_next), down_one_terms, out_zero = together(
+    (gh_q, gu_q, d_bq_t), (g_message, g_next), out_zero, result_one = together(
         (query_part, gq, w_qkv, u, b_q_t),
         (exchange, g_message, g_total),
-        (scatter_second, *down_one_terms),
-        (deal_in, reordered(spread_zero, inverse[0])),
+        (lambda spread, order: deal_in(reordered(spread, order)), spread_zero, inverse[0]),
+        (functools.partial(finish, 1), down_one_terms),
     )
 
     next_spec = pl.BlockSpec((kv_heads, micro, AUG, 128), lambda f: (f, 0, 0, 0))
@@ -1376,9 +1396,8 @@
 
     (gx, dg1, d_fk, d_bkv_t, d_qkv_t), spread_one = together(
         (heads_to_input, g_keys, g_message, g_next, gu_q, gh_q),
-        (functools.partial(finish_and_deal, 1), down_one_terms),
-    )
-    output = [out_zero, deal_in(reordered(spread_one, inverse[1]))]
+        (deal_out, result_one),
+    )
 
     wide = pl.pallas_call(
         table_kernel,
@@ -1394,9 +1413,11 @@
     )
     wide = wide.reshape(n_all, width // n_all, lanes)
     narrow = narrow.reshape(n_all, kv_rows // n_all, lanes)
-    table = jnp.concatenate([wide, narrow], axis=1).astype(BF16)
-    moved = lax.all_to_all(table, ("dp", "fsdp"), split_axis=0, concat_axis=0, tiled=True)
-    table = jnp.sum(moved.astype(F32), axis=0)
+    table = jnp.concatenate([wide, narrow], axis=1)
+    table, out_one = together(
+        (halved, table), (lambda spread, order: deal_in(reordered(spread, order)), spread_one, inverse[1])
+    )
+    output = [out_zero, out_one]
     wide, narrow = table[: width // n_all], table[width // n_all :]
     shares = (
         wide[:, 64:96],

time: 861 us -> 787 us (0.914)
  waiting for transfers between devices: 235 us -> 141 us
  local copies, waits for them, and re-layouts: 123 us -> 153 us
  Pallas kernels: 336 us -> 322 us
  starting transfers between devices: 92.8 us -> 103 us
    ppermute x20, waiting for transfers between devices: 107 us -> 37.2 us  [by_x(): return lax.ppermute(rows, 'fsdp', X_PAIRS)]
    all_to_all x3, waiting for transfers between devices: 62.3 us -> 3.2 us  [deal_in(): lax.all_to_all(ordered, 'dp', split_axis=0, concat_axis=0, tiled=True)]
    pallas_call x6 -> x5, Pallas kernels: 200 us -> 162 us  [the longest x4 152 us: ffn(): pl.pallas_call(functools.partial(ffn_kernel, pieces, len(carried)), grid=...]
    pallas_call x3 -> x4, Pallas kernels: 45.2 us -> 70.9 us  [together(): job[0](*args)]
    ppermute x20, waiting for transfers between devices: 10.5 us -> 32.7 us  [by_y(): return lax.ppermute(rows, 'fsdp', Y_PAIRS)]
    ppermute x0 -> x5, waiting for transfers between devices: none -> 18.1 us  [halved(): left = keep + lax.ppermute(send, axis, perm).astype(F32)]
    all_to_all x1 -> x0, waiting for transfers between devices: 16.5 us -> none  [shards(): lax.all_to_all(table, ('dp', 'fsdp'), split_axis=0, concat_axis=0, tiled=...]
    all_gather x1, waiting for transfers between devices: 0.01 us -> 14.1 us  [shards(): w_out = lax.all_gather(w_out, 'dp', axis=0, tiled=False)]
  transfers between devices with their start and end apart: 65 -> 69, of which waited for: 26 -> 19; matrix products, arithmetic and copies ran while one was open for 11% -> 14% of each run, Pallas kernels for 32% -> 39%
where the time goes in v3:
time: 787 us; the launch traced here: 780 us
  Pallas kernels  322 us (41%)
  local copies, waits for them, and re-layouts  153 us (19%)
  waiting for transfers between devices  141 us (18%)
  starting transfers between devices  103 us (13%)
  blocking collectives  27.7 us (4%)
  other arithmetic  18 us (2%)
  between operations  15.1 us (2%)
    pallas_call x4, Pallas kernels, ffn(): pl.pallas_call(functools.partial(ffn_kernel, pieces, len(carried)), grid=...  152 us
    pallas_call x4, Pallas kernels, together(): job[0](*args)  70.9 us
    unnamed x210, local copies, waits for them, and re-layouts  57 us
    ppermute x20, waiting for transfers between devices, by_x(): return lax.ppermute(rows, 'fsdp', X_PAIRS)  37.2 us
    dynamic_update_slice x18, local copies, waits for them, and re-layouts, put(): return lax.dynamic_update_slice(out, part[None], (f, at, 0, 0))  34.5 us
    ppermute x20, waiting for transfers between devices, by_y(): return lax.ppermute(rows, 'fsdp', Y_PAIRS)  32.7 us
    ppermute x20, starting transfers between devices, by_y(): return lax.ppermute(rows, 'fsdp', Y_PAIRS)  23.1 us
    ppermute x20, starting transfers between devices, by_x(): return lax.ppermute(rows, 'fsdp', X_PAIRS)  20.3 us
  transfers between devices with their start and end apart: 69, of which 19 were waited for; matrix products, arithmetic and copies ran while one was open for 14% of the time, Pallas kernels for 39%

profile of v3, /device:TPU:0, one launch (start us, length us, event | category | flops | bytes accessed | tf_op | source)
XLA Modules:
  0.0 780.2 jit_solution(11054909687780607458)
XLA Ops:
  16.2 16.1 %all_gather.35 = bf16[8,80,128]{2,1,0:T(8,128)(2,1)S(1)} all-gather(bf16[1,80,128]{2,1,0:T(8,128)(2,1)S(1)} %pad_bitcast_fusion), channel_id=1, replica_groups=mesh['dp'=8,'fsdp'=4] {'dp'}, dimensions={0}, use_global_device_ids=true | all-gather | bytes 184320 | tf_op jit(solution)/shard_map/all_gather | solution.py:915
  32.3 11.6 %all-gather.1 = bf16[32,80,128]{2,1,0:T(8,128)(2,1)S(1)} all-gather(bf16[8,80,128]{2,1,0:T(8,128)(2,1)S(1)} %all_gather.35), channel_id=3, replica_groups=mesh['dp'=8,'fsdp'=4] {'fsdp'}, dimensions={0}, use_global_device_ids=true | all-gather | bytes 819200 | tf_op jit(solution)/shard_map/all_gather | solution.py:916
  85.3 14.1 %all-gather.12.cloned.1.call-done = bf16[2048,512]{1,0:T(8,128)(2,1)} async-done(((bf16[256,512]{1,0:T(8,128)(2,1)}), bf16[2048,512]{1,0:T(8,128)(2,1)}) %all-gather.12.cloned.1.call-update) | async-done | bytes 2097168 | tf_op jit(solution)/shard_map/all_gather | solution.py:938
  101.6 10.9 %collective-permute-done.refs_1_ = bf16[4,256,768]{2,1,0:T(8,128)(2,1)} collective-permute-done((bf16[4,256,768]{2,1,0:T(8,128)(2,1)}, bf16[4,256,768]{2,1,0:T(8,128)(2,1)}, u32[]{:S(2)}, u32[]{:S(2)}) %collective-permute-start) | collective-permute-done | bytes 1572896 | tf_op jit(solution)/shard_map/ppermute | solution.py:61
  113.7 11.4 %all-to-all-done.in_ref = bf16[8,64,2048]{2,1,0:T(8,128)(2,1)} async-done(((bf16[8,64,2048]{2,1,0:T(8,128)(2,1)}), bf16[8,64,2048]{2,1,0:T(8,128)(2,1)}, u32[]{:S(2)}, u32[]{:S(2)}) %all-to-all-start) | async-done | bytes 2097184 | tf_op jit(solution)/shard_map/all_to_all | solution.py:851
  139.9 14.3 %collective-permute-done.2.refs_3_ = bf16[2,256,768]{2,1,0:T(8,128)(2,1)S(1)} collective-permute-done((bf16[2,256,768]{2,1,0:T(8,128)(2,1)S(1)}, bf16[2,256,768]{2,1,0:T(8,128)(2,1)S(1)}, u32[]{:S(2)}, u32[]{:S(2)}) %collective-permute-start.2) | collective-permute-done | bytes 786464 | tf_op jit(solution)/shard_map/ppermute | solution.py:61
  159.6 18.7 %collective-permute-done.3.refs_4_ = bf16[2,256,768]{2,1,0:T(8,128)(2,1)} collective-permute-done((bf16[2,256,768]{2,1,0:T(8,128)(2,1)}, bf16[2,256,768]{2,1,0:T(8,128)(2,1)}, u32[]{:S(2)}, u32[]{:S(2)}) %collective-permute-start.3) | collective-permute-done | bytes 786464 | tf_op jit(solution)/shard_map/ppermute | solution.py:65
  181.6 9.9 %all-gather.14.cloned.1.call-start = ((), (), s32[]{:S(2)}) async-start(), calls=%async_computation.8 | async-start | bytes 7077888 | tf_op jit(solution)/shard_map/all_gather | solution.py:1060
  212.1 11.3 %key_value.1 = (bf16[8,2,256,256]{3,2,1,0:T(8,128)(2,1)S(1)}, bf16[8,2,80,128]{3,2,1,0:T(8,128)(2,1)S(1)}, bf16[8,2,112,256]{3,2,1,0:T(8,128)(2,1)}) custom-call(s32[2]{0:T(128)S(1)} %pad_add_fusion.place_ref, bf16[512,2048]{1,0:T(8,128)(2,1)} %copy-done.77, bf16[512,128]{1,0:T(8,128)(2,1)S(1)} %convolution_convert_fusion.u_ref, ...), custom_call_target="tpu_custom_call" | custom-call | flops 2147483648 | bytes 6291456 | tf_op jit(solution)/shard_map/key_value/pallas_call | solution.py:1013
  240.9 13.8 %query.1 = (bf16[2048,512]{1,0:T(8,128)(2,1)S(1)}, bf16[4096,512]{1,0:T(8,128)(2,1)}) custom-call(s32[2]{0:T(128)S(1)} %pad_add_fusion.place_ref, bf16[512,2048]{1,0:T(8,128)(2,1)} %copy-done.77, bf16[512,128]{1,0:T(8,128)(2,1)S(1)} %convolution_convert_fusion.u_ref, bf16[4,128,512]{2,1,0:T(8,128)(2,1)S(1)} %copy-done.41, f32[32,512]{1,0:T(8,128)S(1)} %copy-done.48, ...), custom_call_target="tpu_custom_call" | custom-call | flops 4294967296 | bytes 16777216 | tf_op jit(solution)/shard_map/query/pallas_call | solution.py:1029
  264.7 18.7 %attend.1 = (bf16[512,2048]{1,0:T(8,128)(2,1)S(1)}, bf16[2048,512]{1,0:T(8,128)(2,1)S(1)}, f32[8,8,512]{2,1,0:T(8,128)S(1)}, bf16[8,2,2,160,128]{4,3,2,1,0:T(8,128)(2,1)S(1)}) custom-call(s32[1]{0:T(128)} %bitcast.prev_ref, bf16[8,2,256,256]{3,2,1,0:T(8,128)(2,1)S(1)} %copy-done.9, bf16[8,2,112,256]{3,2,1,0:T(8,128)(2,1)} %collective-permute-done.14.msg_ref, ...), custom_call_target="tpu_custom_call" | custom-call | flops 2013265920 | bytes 14680064 | tf_op jit(solution)/shard_map/attend/pallas_call | solution.py:57
  298.3 13.2 %output_projection.1 = (f32[512,2048]{1,0:T(8,128)}, bf16[512,2048]{1,0:T(8,128)(2,1)S(1)}, bf16[512,128]{1,0:T(8,128)(2,1)S(1)}, f32[512,1]{1,0:T(8,128)S(1)}) custom-call(s32[2]{0:T(128)S(1)} %pad_add_fusion.place_ref, bf16[512,2048]{1,0:T(8,128)(2,1)S(1)} %copy-done.73, bf16[2048,128]{1,0:T(8,128)(2,1)S(1)} %copy-done.59, ...), custom_call_target="tpu_custom_call" | custom-call | flops 4294967296 | bytes 20971520 | tf_op jit(solution)/shard_map/output_projection/pallas_call | solution.py:57
  344.9 8.7 %collective-permute-done.25.refs_3_ = bf16[256,1024]{1,0:T(8,128)(2,1)} collective-permute-done((bf16[256,1024]{1,0:T(8,128)(2,1)}, bf16[256,1024]{1,0:T(8,128)(2,1)}, u32[]{:S(2)}, u32[]{:S(2)}) %collective-permute-start.25) | collective-permute-done | bytes 524320 | tf_op jit(solution)/shard_map/ppermute | solution.py:61
  360.8 51.9 %feed_forward.4 = (bf16[1024,2048]{1,0:T(8,128)(2,1)}, bf16[1024,2048]{1,0:T(8,128)(2,1)}) custom-call(bf16[8,256,4608]{2,1,0:T(8,128)(2,1)} %bitcast.176, bf16[8,256,4608]{2,1,0:T(8,128)(2,1)} %bitcast.177, bf16[8,256,4608]{2,1,0:T(8,128)(2,1)} %bitcast.178, bf16[256,2048]{1,0:T(8,128)(2,1)} %get-tuple-element.752.refs_0_, ...), custom_call_target="tpu_custom_call" | custom-call | flops 38654705664 | bytes 62914560 | tf_op jit(solution)/shard_map/feed_forward/pallas_call | solution.py:707
  421.4 23.7 %feed_forward.5 = (bf16[2,256,1024]{2,1,0:T(8,128)(2,1)}, bf16[2,256,1024]{2,1,0:T(8,128)(2,1)}, bf16[2,256,1024]{2,1,0:T(8,128)(2,1)}, bf16[2,256,1024]{2,1,0:T...) custom-call(bf16[8,256,1536]{2,1,0:T(8,128)(2,1)} %bitcast.182, ...), custom_call_target="tpu_custom_call" | custom-call | flops 12884901888 | bytes 37748736 | tf_op jit(solution)/shard_map/feed_forward/pallas_call | solution.py:707
  449.3 51.8 %feed_forward.6 = (bf16[1024,2048]{1,0:T(8,128)(2,1)}, bf16[1024,2048]{1,0:T(8,128)(2,1)}) custom-call(bf16[8,256,4608]{2,1,0:T(8,128)(2,1)} %bitcast.179, bf16[8,256,4608]{2,1,0:T(8,128)(2,1)} %bitcast.180, bf16[8,256,4608]{2,1,0:T(8,128)(2,1)} %bitcast.181, bf16[256,2048]{1,0:T(8,128)(2,1)} %copy-done.83, ...), custom_call_target="tpu_custom_call" | custom-call | flops 38654705664 | bytes 62914560 | tf_op jit(solution)/shard_map/feed_forward/pallas_call | solution.py:707
  511.5 24.2 %feed_forward.7 = (bf16[2,256,1024]{2,1,0:T(8,128)(2,1)}, bf16[2,256,1024]{2,1,0:T(8,128)(2,1)}, bf16[2,256,1024]{2,1,0:T(8,128)(2,1)}, bf16[2,256,1024]{2,1,0:T...) custom-call(bf16[8,256,1536]{2,1,0:T(8,128)(2,1)} %bitcast.185, ...), custom_call_target="tpu_custom_call" | custom-call | flops 12884901888 | bytes 37748736 | tf_op jit(solution)/shard_map/feed_forward/pallas_call | solution.py:707
  573.1 9.7 %collective-permute-done.45.refs_3_ = bf16[256,1024]{1,0:T(8,128)(2,1)S(1)} collective-permute-done((bf16[256,1024]{1,0:T(8,128)(2,1)}, bf16[256,1024]{1,0:T(8,128)(2,1)S(1)}, u32[]{:S(2)}, u32[]{:S(2)}) %collective-permute-start.45) | collective-permute-done | bytes 524320 | tf_op jit(solution)/shard_map/ppermute | solution.py:65
  602.5 10.2 %output_projection_back.1 = (bf16[2048,512]{1,0:T(8,128)(2,1)}, f32[16,2048]{1,0:T(8,128)}) custom-call(bf16[512,2048]{1,0:T(8,128)(2,1)} %copy-done.44, bf16[4,8,256,512]{3,2,1,0:T(8,128)(2,1)} %bitcast_dynamic-update-slice_fusion.14.w_ref, bf16[2048,128]{1,0:T(8,128)(2,1)} %pad.29.ao_ref, bf16[512,128]{1,0:T(8,128)(2,1)} %copy-done.68, ...), custom_call_target="tpu_custom_call" | custom-call | flops 4294967296 | bytes 12582912 | tf_op jit(solution)/shard_map/output_projection_back/pallas_call | solution.py:1278
  622.5 26.7 %attend_back.1 = (bf16[4,512,512]{2,1,0:T(8,128)(2,1)}, f32[8,256,64]{2,1,0:T(8,128)}, f32[8,2,256,256]{3,2,1,0:T(8,128)}, f32[8,2,2,160,128]{4,3,2,1,0:T(8,128)...) custom-call(s32[1]{0:T(128)} %bitcast.prev_ref, bf16[8,2,256,256]{3,2,1,0:T(8,128)(2,1)} %copy-done.8, ...), custom_call_target="tpu_custom_call" | custom-call | flops 6039797760 | bytes 25165824 | tf_op jit(solution)/shard_map/attend_back/pallas_call | solution.py:57
  667.4 12.4 %query_input_gradient.1 = (f32[512,2048]{1,0:T(8,128)}, f32[512,128]{1,0:T(8,128)}, f32[32,2048]{1,0:T(8,128)}) custom-call(bf16[4,512,512]{2,1,0:T(8,128)(2,1)} %get-tuple-element.1001.gq_ref, bf16[4,8,256,768]{3,2,1,0:T(8,128)(2,1)} %bitcast_dynamic-update-slice_fusion.10.wq_ref.wkv_ref, bf16[512,128]{1,0:T(8,128)(2,1)} %copy-done.38, ...), custom_call_target="tpu_custom_call" | custom-call | flops 4294967296 | bytes 16777216 | tf_op jit(solution)/shard_map/query_input_gradient/pallas_call | solution.py:57
  679.8 15.4 %collective-permute-done.53.refs_1_ = bf16[8,2,80,128]{3,2,1,0:T(8,128)(2,1)} collective-permute-done((bf16[8,2,80,128]{3,2,1,0:T(8,128)(2,1)}, bf16[8,2,80,128]{3,2,1,0:T(8,128)(2,1)}, u32[]{:S(2)}, u32[]{:S(2)}) %collective-permute-start.53) | collective-permute-done | bytes 327712 | tf_op jit(solution)/shard_map/ppermute | solution.py:843
  701.0 11.5 %key_value_back.1 = (bf16[4,512,256]{2,1,0:T(8,128)(2,1)}, f32[4,128,64]{2,1,0:T(8,128)}, bf16[512,128]{1,0:T(8,128)(2,1)}, f32[4,32,256]{2,1,0:T(8,128)}, f32[32,2048]{1,0:T(8,128)}) custom-call(f32[8,2,256,256]{3,2,1,0:T(8,128)} %get-tuple-element.1028.gn_ref, bf16[8,2,144,256]{3,2,1,0:T(8,128)(2,1)} %collective-permute-done.51.back_ref, ...), custom_call_target="tpu_custom_call" | custom-call | flops 67108864 | bytes 8388608 | tf_op jit(solution)/shard_map/key_value_back/pallas_call | solution.py:1388
  712.5 13.4 %input_gradient.1 = (bf16[512,2048]{1,0:T(8,128)(2,1)}, f32[1,2048]{1,0:T(1,128)}) custom-call(f32[512,2048]{1,0:T(8,128)} %get-tuple-element.1027.part_ref, bf16[4,512,256]{2,1,0:T(8,128)(2,1)} %get-tuple-element.1035.gkv_ref, bf16[4,8,256,768]{3,2,1,0:T(8,128)(2,1)} %bitcast_dynamic-update-slice_fusion.10.wq_ref.wkv_ref, ...), custom_call_target="tpu_custom_call" | custom-call | flops 2147483648 | bytes 31457280 | tf_op jit(solution)/shard_map/input_gradient/pallas_call | solution.py:1392
  (472 shorter events, 341.6 us)
Async XLA Ops:
  7.2 44.9 %all-gather.10.cloned.1.call-start = ((), (), s32[]{:S(2)}) async-start(), calls=%async_computation.6 | async-start | bytes 3538944 | tf_op jit(solution)/shard_map/all_gather | solution.py:937
  9.4 89.9 %all-gather.12.cloned.1.call-start = ((), (), s32[]{:S(2)}) async-start(), calls=%async_computation.7 | async-start | bytes 2359296 | tf_op jit(solution)/shard_map/all_gather | solution.py:938
  54.8 70.3 %all-to-all-start = ((bf16[8,64,2048]{2,1,0:T(8,128)(2,1)}), bf16[8,64,2048]{2,1,0:T(8,128)(2,1)}, u32[]{:S(2)}, u32[]{:S(2)}) async-start(bf16[8,64,2048]{2,1,0:T(8,128)(2,1)} %bitcast.162), calls=%async_computation | async-start | bytes 4194304 | tf_op jit(solution)/shard_map/all_to_all | solution.py:851
  75.5 37.0 %collective-permute-start = (bf16[4,256,768]{2,1,0:T(8,128)(2,1)}, bf16[4,256,768]{2,1,0:T(8,128)(2,1)}, u32[]{:S(2)}, u32[]{:S(2)}) collective-permute-start(bf16[4,256,768]{2,1,0:T(8,128)(2,1)} %constant_dynamic-slice_fusion.3), channel_id=1, source_target_pairs={{0,1},{1,0},{2,3},{3,2},{4,5},{5,4},{6,7},{7,6},{8,9},{9,8},{10,11... | collective-permute-start | bytes 4718600 | tf_op jit(solution)/shard_map/ppermute | solution.py:61
  77.0 36.7 %collective-permute-start.1 = (bf16[4,256,768]{2,1,0:T(8,128)(2,1)}, bf16[4,256,768]{2,1,0:T(8,128)(2,1)}, u32[]{:S(2)}, u32[]{:S(2)}) collective-permute-start(bf16[4,256,768]{2,1,0:T(8,128)(2,1)} %constant_dynamic-slice_fusion.3), channel_id=1, source_target_pairs={{0,2},{1,3},{2,0},{3,1},{4,6},{5,7},{6,4},{7,5},{8,10},{9,11},{10,... | collective-permute-start | bytes 4718600 | tf_op jit(solution)/shard_map/ppermute | solution.py:65
  128.1 53.4 %all-to-all-start.1 = ((bf16[8,64,2048]{2,1,0:T(8,128)(2,1)}), bf16[8,64,2048]{2,1,0:T(8,128)(2,1)}, u32[]{:S(2)}, u32[]{:S(2)}) async-start(bf16[8,64,2048]{2,1,0:T(8,128)(2,1)} %reorder.3), calls=%async_computation.1 | async-start | bytes 4194304 | tf_op jit(solution)/shard_map/all_to_all | solution.py:872
  132.5 228.3 %all-gather.16.cloned.1.call-start = ((), (), s32[]{:S(2)}) async-start(), calls=%async_computation.9 | async-start | bytes 21233664 | tf_op jit(solution)/shard_map/all_gather | solution.py:999
  135.2 43.1 %collective-permute-start.4 = (bf16[4,256,768]{2,1,0:T(8,128)(2,1)}, bf16[4,256,768]{2,1,0:T(8,128)(2,1)}, u32[]{:S(2)}, u32[]{:S(2)}) collective-permute-start(bf16[4,256,768]{2,1,0:T(8,128)(2,1)} %collective-permute-done.refs_1_), channel_id=1, source_target_pairs={{0,4},{4,0},{8,12},{12,8},{16,20},{20,16},{24,28},{28,24},{1,5},{5... | collective-permute-start | bytes 4718600 | tf_op jit(solution)/shard_map/ppermute | solution.py:782
  135.3 43.0 %collective-permute-start.5 = (bf16[4,256,768]{2,1,0:T(8,128)(2,1)}, bf16[4,256,768]{2,1,0:T(8,128)(2,1)}, u32[]{:S(2)}, u32[]{:S(2)}) collective-permute-start(bf16[4,256,768]{2,1,0:T(8,128)(2,1)} %collective-permute-done.1.refs_2_), channel_id=1, source_target_pairs={{0,4},{4,0},{8,12},{12,8},{16,20},{20,16},{24,28},{28,24},{1,5},{5... | collective-permute-start | bytes 4718600 | tf_op jit(solution)/shard_map/ppermute | solution.py:782
  135.8 42.6 %collective-permute-start.6 = (bf16[4,256,512]{2,1,0:T(8,128)(2,1)}, bf16[4,256,512]{2,1,0:T(8,128)(2,1)}, u32[]{:S(2)}, u32[]{:S(2)}) collective-permute-start(bf16[4,256,512]{2,1,0:T(8,128)(2,1)} %constant_dynamic-slice_fusion.2), channel_id=1, source_target_pairs={{0,1},{1,0},{2,3},{3,2},{4,5},{5,4},{6,7},{7,6},{8,9},{9,8},{10,11... | collective-permute-start | bytes 3145736 | tf_op jit(solution)/shard_map/ppermute | solution.py:61
  136.3 42.0 %collective-permute-start.7 = (bf16[4,256,512]{2,1,0:T(8,128)(2,1)}, bf16[4,256,512]{2,1,0:T(8,128)(2,1)}, u32[]{:S(2)}, u32[]{:S(2)}) collective-permute-start(bf16[4,256,512]{2,1,0:T(8,128)(2,1)} %constant_dynamic-slice_fusion.2), channel_id=1, source_target_pairs={{0,2},{1,3},{2,0},{3,1},{4,6},{5,7},{6,4},{7,5},{8,10},{9,11},{10,... | collective-permute-start | bytes 3145736 | tf_op jit(solution)/shard_map/ppermute | solution.py:65
  181.6 239.8 %all-gather.14.cloned.1.call-start = ((), (), s32[]{:S(2)}) async-start(), calls=%async_computation.8 | async-start | bytes 7077888 | tf_op jit(solution)/shard_map/all_gather | solution.py:1060
  356.7 56.0 %collective-permute-start.27 = (bf16[256,2048]{1,0:T(8,128)(2,1)S(1)}, bf16[256,2048]{1,0:T(8,128)(2,1)}, u32[]{:S(2)}, u32[]{:S(2)}) collective-permute-start(bf16[256,2048]{1,0:T(8,128)(2,1)S(1)} %get-tuple-element.826.refs_0_), channel_id=1, source_target_pairs={{0,1},{1,0},{2,3},{3,2},{4,5},{5,4},{6,7},{7,6},{8,9},{9,8},{10,11... | collective-permute-start | bytes 3145736 | tf_op jit(solution)/shard_map/ppermute | solution.py:61
  357.2 55.5 %collective-permute-start.28 = (bf16[256,2048]{1,0:T(8,128)(2,1)S(1)}, bf16[256,2048]{1,0:T(8,128)(2,1)}, u32[]{:S(2)}, u32[]{:S(2)}) collective-permute-start(bf16[256,2048]{1,0:T(8,128)(2,1)S(1)} %get-tuple-element.826.refs_0_), channel_id=1, source_target_pairs={{0,2},{1,3},{2,0},{3,1},{4,6},{5,7},{6,4},{7,5},{8,10},{9,11},{10,... | collective-permute-start | bytes 3145736 | tf_op jit(solution)/shard_map/ppermute | solution.py:65
  357.8 54.9 %collective-permute-start.29 = (bf16[256,2048]{1,0:T(8,128)(2,1)S(1)}, bf16[256,2048]{1,0:T(8,128)(2,1)}, u32[]{:S(2)}, u32[]{:S(2)}) collective-permute-start(bf16[256,2048]{1,0:T(8,128)(2,1)S(1)} %copy-done.19), channel_id=1, source_target_pairs={{0,1},{1,0},{2,3},{3,2},{4,5},{5,4},{6,7},{7,6},{8,9},{9,8},{10,11... | collective-permute-start | bytes 3145736 | tf_op jit(solution)/shard_map/ppermute | solution.py:61
  359.0 53.7 %collective-permute-start.30 = (bf16[256,2048]{1,0:T(8,128)(2,1)S(1)}, bf16[256,2048]{1,0:T(8,128)(2,1)}, u32[]{:S(2)}, u32[]{:S(2)}) collective-permute-start(bf16[256,2048]{1,0:T(8,128)(2,1)S(1)} %copy-done.19), channel_id=1, source_target_pairs={{0,2},{1,3},{2,0},{3,1},{4,6},{5,7},{6,4},{7,5},{8,10},{9,11},{10,... | collective-permute-start | bytes 3145736 | tf_op jit(solution)/shard_map/ppermute | solution.py:65
  445.1 56.0 %collective-permute-start.35 = (bf16[2,256,1024]{2,1,0:T(8,128)(2,1)}, bf16[2,256,1024]{2,1,0:T(8,128)(2,1)S(1)}, u32[]{:S(2)}, u32[]{:S(2)}) collective-permute-start(bf16[2,256,1024]{2,1,0:T(8,128)(2,1)} %get-tuple-element.810), channel_id=1, source_target_pairs={{0,1},{1,0},{2,3},{3,2},{4,5},{5,4},{6,7},{7,6},{8,9},{9,8},{10,11... | collective-permute-start | bytes 3145736 | tf_op jit(solution)/shard_map/ppermute | solution.py:61
  445.7 55.4 %collective-permute-start.36 = (bf16[2,256,1024]{2,1,0:T(8,128)(2,1)}, bf16[2,256,1024]{2,1,0:T(8,128)(2,1)S(1)}, u32[]{:S(2)}, u32[]{:S(2)}) collective-permute-start(bf16[2,256,1024]{2,1,0:T(8,128)(2,1)} %get-tuple-element.811), channel_id=1, source_target_pairs={{0,2},{1,3},{2,0},{3,1},{4,6},{5,7},{6,4},{7,5},{8,10},{9,11},{10,... | collective-permute-start | bytes 3145736 | tf_op jit(solution)/shard_map/ppermute | solution.py:65
  446.3 54.9 %collective-permute-start.37 = (bf16[2,256,1024]{2,1,0:T(8,128)(2,1)}, bf16[2,256,1024]{2,1,0:T(8,128)(2,1)S(1)}, u32[]{:S(2)}, u32[]{:S(2)}) collective-permute-start(bf16[2,256,1024]{2,1,0:T(8,128)(2,1)} %get-tuple-element.814), channel_id=1, source_target_pairs={{0,1},{1,0},{2,3},{3,2},{4,5},{5,4},{6,7},{7,6},{8,9},{9,8},{10,11... | collective-permute-start | bytes 3145736 | tf_op jit(solution)/shard_map/ppermute | solution.py:61
  447.5 53.7 %collective-permute-start.38 = (bf16[2,256,1024]{2,1,0:T(8,128)(2,1)}, bf16[2,256,1024]{2,1,0:T(8,128)(2,1)}, u32[]{:S(2)}, u32[]{:S(2)}) collective-permute-start(bf16[2,256,1024]{2,1,0:T(8,128)(2,1)} %get-tuple-element.815), channel_id=1, source_target_pairs={{0,2},{1,3},{2,0},{3,1},{4,6},{5,7},{6,4},{7,5},{8,10},{9,11},{10,... | collective-permute-start | bytes 3145736 | tf_op jit(solution)/shard_map/ppermute | solution.py:65
  612.8 37.3 %all-to-all-start.2 = ((bf16[8,32,2048]{2,1,0:T(8,128)(2,1)}), bf16[8,32,2048]{2,1,0:T(8,128)(2,1)}, u32[]{:S(2)}, u32[]{:S(2)}) async-start(bf16[8,32,2048]{2,1,0:T(8,128)(2,1)} %bitcast.41), calls=%async_computation.2 | async-start | bytes 2097152 | tf_op jit(solution)/shard_map/all_to_all | solution.py:851
  652.4 42.9 %all-to-all-start.3 = ((bf16[8,32,2048]{2,1,0:T(8,128)(2,1)}), bf16[8,32,2048]{2,1,0:T(8,128)(2,1)}, u32[]{:S(2)}, u32[]{:S(2)}) async-start(bf16[8,32,2048]{2,1,0:T(8,128)(2,1)} %reorder.4), calls=%async_computation.3 | async-start | bytes 2097152 | tf_op jit(solution)/shard_map/all_to_all | solution.py:872
  657.5 37.8 %collective-permute-start.51 = (bf16[8,2,144,256]{3,2,1,0:T(8,128)(2,1)}, bf16[8,2,144,256]{3,2,1,0:T(8,128)(2,1)}, u32[]{:S(2)}, u32[]{:S(2)}) collective-permute-start(bf16[8,2,144,256]{3,2,1,0:T(8,128)(2,1)} %get-tuple-element.1008), channel_id=1, source_target_pairs={{1,0},{2,1},{3,2},{5,4},{6,5},{7,6},{9,8},{10,9},{11,10},{13,12},{... | collective-permute-start | bytes 3538952 | tf_op jit(solution)/shard_map/ppermute | solution.py:1316
  660.0 35.2 %collective-permute-start.53 = (bf16[8,2,80,128]{3,2,1,0:T(8,128)(2,1)}, bf16[8,2,80,128]{3,2,1,0:T(8,128)(2,1)}, u32[]{:S(2)}, u32[]{:S(2)}) collective-permute-start(bf16[8,2,80,128]{3,2,1,0:T(8,128)(2,1)} %get-tuple-element.1009), channel_id=1, source_target_pairs={{3,0},{7,4},{11,8},{15,12},{19,16},{23,20},{27,24},{31,28}} | collective-permute-start | bytes 983048 | tf_op jit(solution)/shard_map/ppermute | solution.py:843
  (140 other events, 2022.1 us)
Sparse Core Ops, SparseCore 0:
  10.2 41.8 all-gather.9
  53.7 45.5 all-gather.11
  181.7 167.1 all-gather.15
  350.3 62.9 all-gather.13

commit v4 on v3

--- a/solution.py
+++ b/solution.py
@@ -820,12 +820,11 @@
     block = pieces[0]
     half = block.shape[0] // 2
     core = group % 2
-    out = jnp.zeros((4,) + block.shape, block.dtype)
+    out = jnp.broadcast_to(block[None], (4,) + block.shape)
 
     def put(out, part, f, at):
         return lax.dynamic_update_slice(out, part[None], (f, at, 0, 0))
 
-    out = put(out, block, shard, 0)
     masks = ((1, 0), (2, 0), (3, 0), (3, half // 2))
     for side, at in ((pieces[1:5], core * half), (pieces[5:], (1 - core) * half)):
         for part, (mask, offset) in zip(side, masks):
@@ -1090,7 +1089,7 @@
             jax.ShapeDtypeStruct((KEY_VALUE_HEADS, 8, total), F32),
             jax.ShapeDtypeStruct((KEY_VALUE_HEADS, micro, pairs, 2 * AUG, 128), BF16),
         ],
-        compiler_params=params(40),
+        compiler_params=params(60),
         cost_estimate=cost(attend_flops, 14 * MIB, 128 * H * total),
         name="attend",
     )
@@ -1111,7 +1110,7 @@
             jax.ShapeDtypeStruct((total, 1), F32),
         ],
         scratch_shapes=[pltpu.VMEM((n_dp, total, depth), F32)],
-        compiler_params=params(40),
+        compiler_params=params(60),
         cost_estimate=cost(2 * total * width * H * 64, 20 * MIB),
         name="output_projection",
     )
@@ -1125,7 +1124,7 @@
         return assembled(pieces, group, quarter)
 
     h2_first, w_qkv = together((gather, h2[:rows]), (assemble, *qkv_pieces))
-    (h2_zero,) = together((gather_second, *h2_first))
+    h2_zero, w_out = together((gather_second, *h2_first), (assemble, *out_pieces))
 
     def piece(array, m):
         return array[m * rows : (m + 1) * rows]
@@ -1143,7 +1142,7 @@
             + term_specs(terms, row_tile, width),
             out_specs=pl.BlockSpec((row_tile, width), lambda r: (r, 0)),
             out_shape=jax.ShapeDtypeStruct((rows, width), BF16),
-            compiler_params=params(40),
+            compiler_params=params(60),
             cost_estimate=cost(4 * rows * width, 10 * rows * width),
             name="result",
         )(x2, valid_rows, *terms)
@@ -1174,7 +1173,7 @@
                 jax.ShapeDtypeStruct((16, width), F32),
             ],
             input_output_aliases={count + i: i for i in range(len(whole_arrays))},
-            compiler_params=params(40),
+            compiler_params=params(60),
             cost_estimate=cost(20 * rows * width, 16 * rows * width),
             name="mid_back",
         )(x2, r2, gain_two.reshape(1, width), gy, uo, b_o, *terms, *whole_arrays)
@@ -1265,11 +1264,10 @@
         cost_estimate=cost(3 * attend_flops, 24 * MIB, 128 * H * total),
         name="attend_back",
     )
-    gh_one_terms, zero, result_zero, w_out = together(
+    gh_one_terms, zero, result_zero = together(
         (scatter, *gh_one),
         (functools.partial(mid_back, 0), gh_zero_terms, gy[0]),
         (functools.partial(finish, 0), down_zero_terms),
-        (assemble, *out_pieces),
     )
     (gh_one_terms,) = together((scatter_second, *gh_one_terms))
 

time: 787 us -> 772 us (0.981)
  local copies, waits for them, and re-layouts: 153 us -> 122 us
  Pallas kernels: 322 us -> 333 us
  starting transfers between devices: 103 us -> 93.1 us
  waiting for transfers between devices: 141 us -> 149 us
    unnamed x210 -> x142, local copies, waits for them, and re-layouts: 57 us -> 32.1 us
    all_gather x1, starting transfers between devices: 9.86 us -> 0.51 us  [shards(): fetched_ffn.append(lax.all_gather(part, 'dp', axis=0, tiled=False))]
    all_to_all x3, waiting for transfers between devices: 12.1 us -> 21.1 us  [deal_out(): return lax.all_to_all(pieces, 'dp', split_axis=0, concat_axis=0, tiled=True)]
    dynamic_update_slice x18 -> x16, local copies, waits for them, and re-layouts: 34.5 us -> 31.1 us  [put(): return lax.dynamic_update_slice(out, part[None], (f, at, 0, 0))]
  transfers between devices with their start and end apart: 69 -> 69, of which waited for: 19 -> 25; matrix products, arithmetic and copies ran while one was open for 14% -> 14% of each run, Pallas kernels for 39% -> 42%
where the time goes in v4:
time: 772 us; the launch traced here: 761 us
  Pallas kernels  333 us (43%)
  waiting for transfers between devices  149 us (19%)
  local copies, waits for them, and re-layouts  122 us (16%)
  starting transfers between devices  93.1 us (12%)
  blocking collectives  27.7 us (4%)
  other arithmetic  20.5 us (3%)
  between operations  15.2 us (2%)
    pallas_call x4, Pallas kernels, ffn(): pl.pallas_call(functools.partial(ffn_kernel, pieces, len(carried)), grid=...  154 us
    pallas_call x4, Pallas kernels, together(): job[0](*args)  74.4 us
    ppermute x20, waiting for transfers between devices, by_x(): return lax.ppermute(rows, 'fsdp', X_PAIRS)  33.6 us
    unnamed x142, local copies, waits for them, and re-layouts  32.1 us
    dynamic_update_slice x16, local copies, waits for them, and re-layouts, put(): return lax.dynamic_update_slice(out, part[None], (f, at, 0, 0))  31.1 us
    ppermute x20, waiting for transfers between devices, by_y(): return lax.ppermute(rows, 'fsdp', Y_PAIRS)  29.8 us
    ppermute x20, starting transfers between devices, by_y(): return lax.ppermute(rows, 'fsdp', Y_PAIRS)  24.3 us
    all_to_all x3, waiting for transfers between devices, deal_out(): return lax.all_to_all(pieces, 'dp', split_axis=0, concat_axis=0, tiled=True)  21.1 us
  transfers between devices with their start and end apart: 69, of which 25 were waited for; matrix products, arithmetic and copies ran while one was open for 14% of the time, Pallas kernels for 42%

profile of v4, /device:TPU:0, one launch (start us, length us, event | category | flops | bytes accessed | tf_op | source)
XLA Modules:
  0.0 761.5 jit_solution(14848211268049023264)
XLA Ops:
  16.2 16.1 %all_gather.35 = bf16[8,80,128]{2,1,0:T(8,128)(2,1)S(1)} all-gather(bf16[1,80,128]{2,1,0:T(8,128)(2,1)S(1)} %pad_bitcast_fusion), channel_id=1, replica_groups=mesh['dp'=8,'fsdp'=4] {'dp'}, dimensions={0}, use_global_device_ids=true | all-gather | bytes 184320 | tf_op jit(solution)/shard_map/all_gather | solution.py:914
  32.3 11.6 %all-gather.1 = bf16[32,80,128]{2,1,0:T(8,128)(2,1)S(1)} all-gather(bf16[8,80,128]{2,1,0:T(8,128)(2,1)S(1)} %all_gather.35), channel_id=3, replica_groups=mesh['dp'=8,'fsdp'=4] {'fsdp'}, dimensions={0}, use_global_device_ids=true | all-gather | bytes 819200 | tf_op jit(solution)/shard_map/all_gather | solution.py:915
  80.0 19.3 %all-gather.12.cloned.1.call-done = bf16[2048,512]{1,0:T(8,128)(2,1)} async-done(((bf16[256,512]{1,0:T(8,128)(2,1)}), bf16[2048,512]{1,0:T(8,128)(2,1)}) %all-gather.12.cloned.1.call-update) | async-done | bytes 2097168 | tf_op jit(solution)/shard_map/all_gather | solution.py:937
  104.8 20.3 %all-to-all-done.in_ref = bf16[8,64,2048]{2,1,0:T(8,128)(2,1)} async-done(((bf16[8,64,2048]{2,1,0:T(8,128)(2,1)}), bf16[8,64,2048]{2,1,0:T(8,128)(2,1)}, u32[]{:S(2)}, u32[]{:S(2)}) %all-to-all-start) | async-done | bytes 2097184 | tf_op jit(solution)/shard_map/all_to_all | solution.py:850
  137.6 15.5 %collective-permute-done.2.refs_3_ = bf16[2,256,768]{2,1,0:T(8,128)(2,1)} collective-permute-done((bf16[2,256,768]{2,1,0:T(8,128)(2,1)S(1)}, bf16[2,256,768]{2,1,0:T(8,128)(2,1)}, u32[]{:S(2)}, u32[]{:S(2)}) %collective-permute-start.2) | collective-permute-done | bytes 786464 | tf_op jit(solution)/shard_map/ppermute | solution.py:61
  158.5 18.7 %collective-permute-done.3.refs_4_ = bf16[2,256,768]{2,1,0:T(8,128)(2,1)} collective-permute-done((bf16[2,256,768]{2,1,0:T(8,128)(2,1)}, bf16[2,256,768]{2,1,0:T(8,128)(2,1)}, u32[]{:S(2)}, u32[]{:S(2)}) %collective-permute-start.3) | collective-permute-done | bytes 786464 | tf_op jit(solution)/shard_map/ppermute | solution.py:65
  200.7 10.9 %key_value.1 = (bf16[8,2,256,256]{3,2,1,0:T(8,128)(2,1)S(1)}, bf16[8,2,80,128]{3,2,1,0:T(8,128)(2,1)S(1)}, bf16[8,2,112,256]{3,2,1,0:T(8,128)(2,1)}) custom-call(s32[2]{0:T(128)S(1)} %pad_add_fusion.place_ref, bf16[512,2048]{1,0:T(8,128)(2,1)} %copy-done.23, bf16[512,128]{1,0:T(8,128)(2,1)S(1)} %convolution_convert_fusion.u_ref, ...), custom_call_target="tpu_custom_call" | custom-call | flops 2147483648 | bytes 6291456 | tf_op jit(solution)/shard_map/key_value/pallas_call | solution.py:1012
  230.7 13.4 %query.1 = (bf16[2048,512]{1,0:T(8,128)(2,1)S(1)}, bf16[4096,512]{1,0:T(8,128)(2,1)}) custom-call(s32[2]{0:T(128)S(1)} %pad_add_fusion.place_ref, bf16[512,2048]{1,0:T(8,128)(2,1)} %copy-done.23, bf16[512,128]{1,0:T(8,128)(2,1)S(1)} %convolution_convert_fusion.u_ref, bf16[4,128,512]{2,1,0:T(8,128)(2,1)S(1)} %copy-done.15, f32[32,512]{1,0:T(8,128)S(1)} %copy-done.19, ...), custom_call_target="tpu_custom_call" | custom-call | flops 4294967296 | bytes 16777216 | tf_op jit(solution)/shard_map/query/pallas_call | solution.py:1028
  250.8 19.4 %attend.1 = (bf16[512,2048]{1,0:T(8,128)(2,1)}, bf16[2048,512]{1,0:T(8,128)(2,1)}, f32[8,8,512]{2,1,0:T(8,128)}, bf16[8,2,2,160,128]{4,3,2,1,0:T(8,128)(2,1)}) custom-call(s32[1]{0:T(128)} %bitcast.prev_ref, bf16[8,2,256,256]{3,2,1,0:T(8,128)(2,1)} %copy-done.2, bf16[8,2,112,256]{3,2,1,0:T(8,128)(2,1)} %collective-permute-done.14.msg_ref, ...), custom_call_target="tpu_custom_call" | custom-call | flops 2013265920 | bytes 14680064 | tf_op jit(solution)/shard_map/attend/pallas_call | solution.py:57
  280.7 15.9 %output_projection.1 = (f32[512,2048]{1,0:T(8,128)}, bf16[512,2048]{1,0:T(8,128)(2,1)}, bf16[512,128]{1,0:T(8,128)(2,1)}, f32[512,1]{1,0:T(8,128)}) custom-call(s32[2]{0:T(128)} %copy-done.21, bf16[512,2048]{1,0:T(8,128)(2,1)} %get-tuple-element.676.o_ref, bf16[2048,128]{1,0:T(8,128)(2,1)} %pad.29.ao_ref, bf16[2048,128]{1,0:T(8,128)(2,1)} %pad.33.bo_ref, ...), custom_call_target="tpu_custom_call" | custom-call | flops 4294967296 | bytes 20971520 | tf_op jit(solution)/shard_map/output_projection/pallas_call | solution.py:57
  300.4 8.1 %broadcast_in_dim.85 = bf16[4,8,256,768]{3,2,1,0:T(8,128)(2,1)} broadcast(bf16[8,256,768]{2,1,0:T(8,128)(2,1)} %bitcast.131), dimensions={1,2,3} | broadcast | bytes 15728640 | tf_op jit(solution)/shard_map/broadcast_in_dim | solution.py:823
  354.8 53.3 %feed_forward.4 = (bf16[1024,2048]{1,0:T(8,128)(2,1)}, bf16[1024,2048]{1,0:T(8,128)(2,1)}) custom-call(bf16[8,256,4608]{2,1,0:T(8,128)(2,1)} %bitcast.173, bf16[8,256,4608]{2,1,0:T(8,128)(2,1)} %bitcast.174, bf16[8,256,4608]{2,1,0:T(8,128)(2,1)} %bitcast.175, bf16[256,2048]{1,0:T(8,128)(2,1)} %get-tuple-element.761.refs_0_, ...), custom_call_target="tpu_custom_call" | custom-call | flops 38654705664 | bytes 62914560 | tf_op jit(solution)/shard_map/feed_forward/pallas_call | solution.py:707
  416.1 23.9 %feed_forward.5 = (bf16[2,256,1024]{2,1,0:T(8,128)(2,1)}, bf16[2,256,1024]{2,1,0:T(8,128)(2,1)}, bf16[2,256,1024]{2,1,0:T(8,128)(2,1)}, bf16[2,256,1024]{2,1,0:T...) custom-call(bf16[8,256,1536]{2,1,0:T(8,128)(2,1)} %bitcast.179, ...), custom_call_target="tpu_custom_call" | custom-call | flops 12884901888 | bytes 37748736 | tf_op jit(solution)/shard_map/feed_forward/pallas_call | solution.py:707
  444.2 52.3 %feed_forward.6 = (bf16[1024,2048]{1,0:T(8,128)(2,1)}, bf16[1024,2048]{1,0:T(8,128)(2,1)}) custom-call(bf16[8,256,4608]{2,1,0:T(8,128)(2,1)} %bitcast.176, bf16[8,256,4608]{2,1,0:T(8,128)(2,1)} %bitcast.177, bf16[8,256,4608]{2,1,0:T(8,128)(2,1)} %bitcast.178, bf16[256,2048]{1,0:T(8,128)(2,1)} %get-tuple-element.835.refs_0_, bf16[256,2048]{1,0:T(8,128)(2,1)} %copy-done.52, ...), custom_call_target="tpu_custom_call" | custom-call | flops 38654705664 | bytes 62914560 | tf_op jit(solution)/shard_map/feed_forward/pallas_call | solution.py:707
  506.9 24.1 %feed_forward.7 = (bf16[2,256,1024]{2,1,0:T(8,128)(2,1)}, bf16[2,256,1024]{2,1,0:T(8,128)(2,1)}, bf16[2,256,1024]{2,1,0:T(8,128)(2,1)}, bf16[2,256,1024]{2,1,0:T...) custom-call(bf16[8,256,1536]{2,1,0:T(8,128)(2,1)} %bitcast.182, ...), custom_call_target="tpu_custom_call" | custom-call | flops 12884901888 | bytes 37748736 | tf_op jit(solution)/shard_map/feed_forward/pallas_call | solution.py:707
  543.6 8.8 %collective-permute-done.43.from_x.refs_2_ = bf16[2,256,1024]{2,1,0:T(8,128)(2,1)S(1)} collective-permute-done((bf16[2,256,1024]{2,1,0:T(8,128)(2,1)}, bf16[2,256,1024]{2,1,0:T(8,128)(2,1)S(1)}, u32[]{:S(2)}, u32[]{:S(2)}) %collective-permute-start.43) | collective-permute-done | bytes 1048608 | tf_op jit(solution)/shard_map/ppermute | solution.py:61
  559.3 8.2 %collective-permute-done.45.refs_3_ = bf16[256,1024]{1,0:T(8,128)(2,1)S(1)} collective-permute-done((bf16[256,1024]{1,0:T(8,128)(2,1)}, bf16[256,1024]{1,0:T(8,128)(2,1)S(1)}, u32[]{:S(2)}, u32[]{:S(2)}) %collective-permute-start.45) | collective-permute-done | bytes 524320 | tf_op jit(solution)/shard_map/ppermute | solution.py:65
  571.9 5.4 mid_back.3
  580.2 10.3 %output_projection_back.1 = (bf16[2048,512]{1,0:T(8,128)(2,1)}, f32[16,2048]{1,0:T(8,128)}) custom-call(bf16[512,2048]{1,0:T(8,128)(2,1)} %get-tuple-element.942.gb_ref, bf16[4,8,256,512]{3,2,1,0:T(8,128)(2,1)} %bitcast_dynamic-update-slice_fusion.12.w_ref, bf16[2048,128]{1,0:T(8,128)(2,1)} %pad.29.ao_ref, bf16[512,128]{1,0:T(8,128)(2,1)} %get-tuple-element.944.guo_ref, ...), custom_call_target="tpu_custom_call" | custom-call | flops 4294967296 | bytes 12582912 | tf_op jit(solution)/shard_map/output_projection_back/pallas_call | solution.py:1276
  600.8 26.7 %attend_back.1 = (bf16[4,512,512]{2,1,0:T(8,128)(2,1)}, f32[8,256,64]{2,1,0:T(8,128)}, f32[8,2,256,256]{3,2,1,0:T(8,128)}, f32[8,2,2,160,128]{4,3,2,1,0:T(8,128)...) custom-call(s32[1]{0:T(128)} %bitcast.prev_ref, bf16[8,2,256,256]{3,2,1,0:T(8,128)(2,1)} %copy-done.2, ...), custom_call_target="tpu_custom_call" | custom-call | flops 6039797760 | bytes 25165824 | tf_op jit(solution)/shard_map/attend_back/pallas_call | solution.py:57
  644.5 12.4 %query_input_gradient.1 = (f32[512,2048]{1,0:T(8,128)}, f32[512,128]{1,0:T(8,128)}, f32[32,2048]{1,0:T(8,128)}) custom-call(bf16[4,512,512]{2,1,0:T(8,128)(2,1)} %get-tuple-element.1001.gq_ref, bf16[4,8,256,768]{3,2,1,0:T(8,128)(2,1)} %bitcast_dynamic-update-slice_fusion.8.wq_ref.wkv_ref, bf16[512,128]{1,0:T(8,128)(2,1)} %copy-done.13, ...), custom_call_target="tpu_custom_call" | custom-call | flops 4294967296 | bytes 16777216 | tf_op jit(solution)/shard_map/query_input_gradient/pallas_call | solution.py:57
  656.9 17.5 %collective-permute-done.53.refs_1_ = bf16[8,2,80,128]{3,2,1,0:T(8,128)(2,1)S(1)} collective-permute-done((bf16[8,2,80,128]{3,2,1,0:T(8,128)(2,1)}, bf16[8,2,80,128]{3,2,1,0:T(8,128)(2,1)S(1)}, u32[]{:S(2)}, u32[]{:S(2)}) %collective-permute-start.53) | collective-permute-done | bytes 327712 | tf_op jit(solution)/shard_map/ppermute | solution.py:842
  680.9 11.5 %key_value_back.1 = (bf16[4,512,256]{2,1,0:T(8,128)(2,1)}, f32[4,128,64]{2,1,0:T(8,128)}, bf16[512,128]{1,0:T(8,128)(2,1)}, f32[4,32,256]{2,1,0:T(8,128)}, f32[32,2048]{1,0:T(8,128)}) custom-call(f32[8,2,256,256]{3,2,1,0:T(8,128)} %get-tuple-element.1028.gn_ref, bf16[8,2,144,256]{3,2,1,0:T(8,128)(2,1)} %copy-done.41, bf16[8,2,256,256]{3,2,1,0:T(8,128)(2,1)} %copy-done.2, ...), custom_call_target="tpu_custom_call" | custom-call | flops 67108864 | bytes 8388608 | tf_op jit(solution)/shard_map/key_value_back/pallas_call | solution.py:1386
  692.5 13.3 %input_gradient.1 = (bf16[512,2048]{1,0:T(8,128)(2,1)}, f32[1,2048]{1,0:T(1,128)}) custom-call(f32[512,2048]{1,0:T(8,128)} %get-tuple-element.1027.part_ref, bf16[4,512,256]{2,1,0:T(8,128)(2,1)} %get-tuple-element.1035.gkv_ref, bf16[4,8,256,768]{3,2,1,0:T(8,128)(2,1)} %bitcast_dynamic-update-slice_fusion.8.wq_ref.wkv_ref, ...), custom_call_target="tpu_custom_call" | custom-call | flops 2147483648 | bytes 31457280 | tf_op jit(solution)/shard_map/input_gradient/pallas_call | solution.py:1390
  (402 shorter events, 309.3 us)
Async XLA Ops:
  7.2 44.9 %all-gather.10.cloned.1.call-start = ((), (), s32[]{:S(2)}) async-start(), calls=%async_computation.6 | async-start | bytes 3538944 | tf_op jit(solution)/shard_map/all_gather | solution.py:936
  9.4 89.9 %all-gather.12.cloned.1.call-start = ((), (), s32[]{:S(2)}) async-start(), calls=%async_computation.7 | async-start | bytes 2359296 | tf_op jit(solution)/shard_map/all_gather | solution.py:937
  54.8 70.3 %all-to-all-start = ((bf16[8,64,2048]{2,1,0:T(8,128)(2,1)}), bf16[8,64,2048]{2,1,0:T(8,128)(2,1)}, u32[]{:S(2)}, u32[]{:S(2)}) async-start(bf16[8,64,2048]{2,1,0:T(8,128)(2,1)} %bitcast.156), calls=%async_computation | async-start | bytes 4194304 | tf_op jit(solution)/shard_map/all_to_all | solution.py:850
  66.6 36.9 %collective-permute-start = (bf16[4,256,768]{2,1,0:T(8,128)(2,1)}, bf16[4,256,768]{2,1,0:T(8,128)(2,1)S(1)}, u32[]{:S(2)}, u32[]{:S(2)}) collective-permute-start(bf16[4,256,768]{2,1,0:T(8,128)(2,1)} %constant_dynamic-slice_fusion.3), channel_id=1, source_target_pairs={{0,1},{1,0},{2,3},{3,2},{4,5},{5,4},{6,7},{7,6},{8,9},{9,8},{10,11... | collective-permute-start | bytes 4718600 | tf_op jit(solution)/shard_map/ppermute | solution.py:61
  68.2 36.6 %collective-permute-start.1 = (bf16[4,256,768]{2,1,0:T(8,128)(2,1)}, bf16[4,256,768]{2,1,0:T(8,128)(2,1)S(1)}, u32[]{:S(2)}, u32[]{:S(2)}) collective-permute-start(bf16[4,256,768]{2,1,0:T(8,128)(2,1)} %constant_dynamic-slice_fusion.3), channel_id=1, source_target_pairs={{0,2},{1,3},{2,0},{3,1},{4,6},{5,7},{6,4},{7,5},{8,10},{9,11},{10,... | collective-permute-start | bytes 4718600 | tf_op jit(solution)/shard_map/ppermute | solution.py:65
  128.1 53.4 %all-to-all-start.1 = ((bf16[8,64,2048]{2,1,0:T(8,128)(2,1)}), bf16[8,64,2048]{2,1,0:T(8,128)(2,1)}, u32[]{:S(2)}, u32[]{:S(2)}) async-start(bf16[8,64,2048]{2,1,0:T(8,128)(2,1)} %reorder.3), calls=%async_computation.1 | async-start | bytes 4194304 | tf_op jit(solution)/shard_map/all_to_all | solution.py:871
  132.5 222.3 %all-gather.16.cloned.1.call-start = ((), (), s32[]{:S(2)}) async-start(), calls=%async_computation.9 | async-start | bytes 21233664 | tf_op jit(solution)/shard_map/all_gather | solution.py:998
  134.1 43.1 %collective-permute-start.4 = (bf16[4,256,768]{2,1,0:T(8,128)(2,1)S(1)}, bf16[4,256,768]{2,1,0:T(8,128)(2,1)}, u32[]{:S(2)}, u32[]{:S(2)}) collective-permute-start(bf16[4,256,768]{2,1,0:T(8,128)(2,1)S(1)} %collective-permute-done.refs_1_), channel_id=1, source_target_pairs={{0,4},{4,0},{8,12},{12,8},{16,20},{20,16},{24,28},{28,24},{1,5},{5... | collective-permute-start | bytes 4718600 | tf_op jit(solution)/shard_map/ppermute | solution.py:782
  134.2 43.0 %collective-permute-start.5 = (bf16[4,256,768]{2,1,0:T(8,128)(2,1)S(1)}, bf16[4,256,768]{2,1,0:T(8,128)(2,1)}, u32[]{:S(2)}, u32[]{:S(2)}) collective-permute-start(bf16[4,256,768]{2,1,0:T(8,128)(2,1)S(1)} %collective-permute-done.1.refs_2_), channel_id=1, source_target_pairs={{0,4},{4,0},{8,12},{12,8},{16,20},{20,16},{24,28},{28,24},{1,5},{5... | collective-permute-start | bytes 4718600 | tf_op jit(solution)/shard_map/ppermute | solution.py:782
  134.6 42.6 %collective-permute-start.6 = (bf16[4,256,512]{2,1,0:T(8,128)(2,1)}, bf16[4,256,512]{2,1,0:T(8,128)(2,1)}, u32[]{:S(2)}, u32[]{:S(2)}) collective-permute-start(bf16[4,256,512]{2,1,0:T(8,128)(2,1)} %constant_dynamic-slice_fusion.2), channel_id=1, source_target_pairs={{0,1},{1,0},{2,3},{3,2},{4,5},{5,4},{6,7},{7,6},{8,9},{9,8},{10,11... | collective-permute-start | bytes 3145736 | tf_op jit(solution)/shard_map/ppermute | solution.py:61
  135.2 42.0 %collective-permute-start.7 = (bf16[4,256,512]{2,1,0:T(8,128)(2,1)}, bf16[4,256,512]{2,1,0:T(8,128)(2,1)}, u32[]{:S(2)}, u32[]{:S(2)}) collective-permute-start(bf16[4,256,512]{2,1,0:T(8,128)(2,1)} %constant_dynamic-slice_fusion.2), channel_id=1, source_target_pairs={{0,2},{1,3},{2,0},{3,1},{4,6},{5,7},{6,4},{7,5},{8,10},{9,11},{10,... | collective-permute-start | bytes 3145736 | tf_op jit(solution)/shard_map/ppermute | solution.py:65
  181.6 234.6 %all-gather.14.cloned.1.call-start = ((), (), s32[]{:S(2)}) async-start(), calls=%async_computation.8 | async-start | bytes 7077888 | tf_op jit(solution)/shard_map/all_gather | solution.py:1059
  350.7 57.4 %collective-permute-start.27 = (bf16[256,2048]{1,0:T(8,128)(2,1)S(1)}, bf16[256,2048]{1,0:T(8,128)(2,1)S(1)}, u32[]{:S(2)}, u32[]{:S(2)}) collective-permute-start(bf16[256,2048]{1,0:T(8,128)(2,1)S(1)} %copy-done.42), channel_id=1, source_target_pairs={{0,1},{1,0},{2,3},{3,2},{4,5},{5,4},{6,7},{7,6},{8,9},{9,8},{10,11... | collective-permute-start | bytes 3145736 | tf_op jit(solution)/shard_map/ppermute | solution.py:61
  350.8 57.3 %collective-permute-start.28 = (bf16[256,2048]{1,0:T(8,128)(2,1)S(1)}, bf16[256,2048]{1,0:T(8,128)(2,1)}, u32[]{:S(2)}, u32[]{:S(2)}) collective-permute-start(bf16[256,2048]{1,0:T(8,128)(2,1)S(1)} %copy-done.42), channel_id=1, source_target_pairs={{0,2},{1,3},{2,0},{3,1},{4,6},{5,7},{6,4},{7,5},{8,10},{9,11},{10,... | collective-permute-start | bytes 3145736 | tf_op jit(solution)/shard_map/ppermute | solution.py:65
  352.1 56.1 %collective-permute-start.29 = (bf16[256,2048]{1,0:T(8,128)(2,1)S(1)}, bf16[256,2048]{1,0:T(8,128)(2,1)}, u32[]{:S(2)}, u32[]{:S(2)}) collective-permute-start(bf16[256,2048]{1,0:T(8,128)(2,1)S(1)} %copy-done.31), channel_id=1, source_target_pairs={{0,1},{1,0},{2,3},{3,2},{4,5},{5,4},{6,7},{7,6},{8,9},{9,8},{10,11... | collective-permute-start | bytes 3145736 | tf_op jit(solution)/shard_map/ppermute | solution.py:61
  353.7 54.5 %collective-permute-start.30 = (bf16[256,2048]{1,0:T(8,128)(2,1)S(1)}, bf16[256,2048]{1,0:T(8,128)(2,1)}, u32[]{:S(2)}, u32[]{:S(2)}) collective-permute-start(bf16[256,2048]{1,0:T(8,128)(2,1)S(1)} %copy-done.31), channel_id=1, source_target_pairs={{0,2},{1,3},{2,0},{3,1},{4,6},{5,7},{6,4},{7,5},{8,10},{9,11},{10,... | collective-permute-start | bytes 3145736 | tf_op jit(solution)/shard_map/ppermute | solution.py:65
  440.1 56.4 %collective-permute-start.35 = (bf16[2,256,1024]{2,1,0:T(8,128)(2,1)}, bf16[2,256,1024]{2,1,0:T(8,128)(2,1)S(1)}, u32[]{:S(2)}, u32[]{:S(2)}) collective-permute-start(bf16[2,256,1024]{2,1,0:T(8,128)(2,1)} %get-tuple-element.819), channel_id=1, source_target_pairs={{0,1},{1,0},{2,3},{3,2},{4,5},{5,4},{6,7},{7,6},{8,9},{9,8},{10,11... | collective-permute-start | bytes 3145736 | tf_op jit(solution)/shard_map/ppermute | solution.py:61
  440.4 56.1 %collective-permute-start.36 = (bf16[2,256,1024]{2,1,0:T(8,128)(2,1)}, bf16[2,256,1024]{2,1,0:T(8,128)(2,1)S(1)}, u32[]{:S(2)}, u32[]{:S(2)}) collective-permute-start(bf16[2,256,1024]{2,1,0:T(8,128)(2,1)} %get-tuple-element.820), channel_id=1, source_target_pairs={{0,2},{1,3},{2,0},{3,1},{4,6},{5,7},{6,4},{7,5},{8,10},{9,11},{10,... | collective-permute-start | bytes 3145736 | tf_op jit(solution)/shard_map/ppermute | solution.py:65
  441.7 54.8 %collective-permute-start.37 = (bf16[2,256,1024]{2,1,0:T(8,128)(2,1)}, bf16[2,256,1024]{2,1,0:T(8,128)(2,1)S(1)}, u32[]{:S(2)}, u32[]{:S(2)}) collective-permute-start(bf16[2,256,1024]{2,1,0:T(8,128)(2,1)} %get-tuple-element.823), channel_id=1, source_target_pairs={{0,1},{1,0},{2,3},{3,2},{4,5},{5,4},{6,7},{7,6},{8,9},{9,8},{10,11... | collective-permute-start | bytes 3145736 | tf_op jit(solution)/shard_map/ppermute | solution.py:61
  443.2 53.4 %collective-permute-start.38 = (bf16[2,256,1024]{2,1,0:T(8,128)(2,1)}, bf16[2,256,1024]{2,1,0:T(8,128)(2,1)}, u32[]{:S(2)}, u32[]{:S(2)}) collective-permute-start(bf16[2,256,1024]{2,1,0:T(8,128)(2,1)} %get-tuple-element.824), channel_id=1, source_target_pairs={{0,2},{1,3},{2,0},{3,1},{4,6},{5,7},{6,4},{7,5},{8,10},{9,11},{10,... | collective-permute-start | bytes 3145736 | tf_op jit(solution)/shard_map/ppermute | solution.py:65
  590.6 37.7 %all-to-all-start.2 = ((bf16[8,32,2048]{2,1,0:T(8,128)(2,1)}), bf16[8,32,2048]{2,1,0:T(8,128)(2,1)S(1)}, u32[]{:S(2)}, u32[]{:S(2)}) async-start(bf16[8,32,2048]{2,1,0:T(8,128)(2,1)} %bitcast.39), calls=%async_computation.2 | async-start | bytes 2097152 | tf_op jit(solution)/shard_map/all_to_all | solution.py:850
  631.7 43.5 %all-to-all-start.3 = ((bf16[8,32,2048]{2,1,0:T(8,128)(2,1)}), bf16[8,32,2048]{2,1,0:T(8,128)(2,1)S(1)}, u32[]{:S(2)}, u32[]{:S(2)}) async-start(bf16[8,32,2048]{2,1,0:T(8,128)(2,1)} %reorder.4), calls=%async_computation.3 | async-start | bytes 2097152 | tf_op jit(solution)/shard_map/all_to_all | solution.py:871
  636.8 38.4 %collective-permute-start.51 = (bf16[8,2,144,256]{3,2,1,0:T(8,128)(2,1)}, bf16[8,2,144,256]{3,2,1,0:T(8,128)(2,1)S(1)}, u32[]{:S(2)}, u32[]{:S(2)}) collective-permute-start(bf16[8,2,144,256]{3,2,1,0:T(8,128)(2,1)} %get-tuple-element.1008), channel_id=1, source_target_pairs={{1,0},{2,1},{3,2},{5,4},{6,5},{7,6},{9,8},{10,9},{11,10},{13,12},{... | collective-permute-start | bytes 3538952 | tf_op jit(solution)/shard_map/ppermute | solution.py:1314
  639.4 35.1 %collective-permute-start.53 = (bf16[8,2,80,128]{3,2,1,0:T(8,128)(2,1)}, bf16[8,2,80,128]{3,2,1,0:T(8,128)(2,1)S(1)}, u32[]{:S(2)}, u32[]{:S(2)}) collective-permute-start(bf16[8,2,80,128]{3,2,1,0:T(8,128)(2,1)} %get-tuple-element.1009), channel_id=1, source_target_pairs={{3,0},{7,4},{11,8},{15,12},{19,16},{23,20},{27,24},{31,28}} | collective-permute-start | bytes 983048 | tf_op jit(solution)/shard_map/ppermute | solution.py:842
  (106 other events, 1860.9 us)
Sparse Core Ops, SparseCore 0:
  10.2 41.8 all-gather.9
  53.7 45.5 all-gather.11
  181.7 167.1 all-gather.15
  350.3 62.9 all-gather.13

commit v5 on v4

--- a/solution.py
+++ b/solution.py
@@ -439,7 +439,10 @@
 
 
 def out_kernel(depth, n_dp, place_ref, o_ref, ao_ref, bo_ref, x_ref, gain_ref, *refs):
-    *w_refs, x2_ref, h2_ref, uo_ref, r2_ref, acc_ref = refs
+    *h2_refs, acc_ref = refs
+    *w_refs, x2_ref, uo_ref, r2_ref = h2_refs[:-2]
+    h2_refs = h2_refs[-2:]
+    rows = h2_refs[0].shape[0]
     uo = dot(o_ref[...], ao_ref[...]).astype(BF16)
     uo_ref[...] = uo
     for j in range(n_dp):
@@ -467,7 +470,9 @@
     r2_ref[...] = r2
     for j in range(n_dp):
         cols = slice(j * depth, (j + 1) * depth)
-        h2_ref[:, cols] = (acc_ref[j] * r2 * gain_ref[:, cols]).astype(BF16)
+        h2 = (acc_ref[j] * r2 * gain_ref[:, cols]).astype(BF16)
+        for m, h2_ref in enumerate(h2_refs):
+            h2_ref[:, cols] = h2[m * rows : (m + 1) * rows]
 
 
 def go_kernel(depth, gb_ref, w_ref, ao_ref, guo_ref, o_ref, go_ref, dao_ref):
@@ -1102,19 +1107,19 @@
         functools.partial(out_kernel, depth, n_dp),
         grid=(1,),
         in_specs=[smem] + [vmem] * 5 + columns(out_pieces, q_cols, 0),
-        out_specs=[vmem] * 4,
+        out_specs=[vmem] * (3 + micro),
         out_shape=[
             jax.ShapeDtypeStruct((total, width), F32),
-            jax.ShapeDtypeStruct((total, width), BF16),
             jax.ShapeDtypeStruct((total, lanes), BF16),
             jax.ShapeDtypeStruct((total, 1), F32),
-        ],
+        ]
+        + [jax.ShapeDtypeStruct((rows, width), BF16)] * micro,
         scratch_shapes=[pltpu.VMEM((n_dp, total, depth), F32)],
         compiler_params=params(60),
         cost_estimate=cost(2 * total * width * H * 64, 20 * MIB),
         name="output_projection",
     )
-    (x2, h2, uo, r2), gy_zero = together(
+    (x2, uo, r2, *h2), gy_zero = together(
         (project_out, place, o, a_o, b_o, x, gain_two.reshape(1, width), *out_pieces),
         (gather_second, *gy_first),
     )
@@ -1123,7 +1128,7 @@
     def assemble(*pieces):
         return assembled(pieces, group, quarter)
 
-    h2_first, w_qkv = together((gather, h2[:rows]), (assemble, *qkv_pieces))
+    h2_first, w_qkv = together((gather, h2[0]), (assemble, *qkv_pieces))
     h2_zero, w_out = together((gather_second, *h2_first), (assemble, *out_pieces))
 
     def piece(array, m):
@@ -1187,7 +1192,7 @@
 
     scatter = functools.partial(scatter_first, size=n_f)
     head_zero, h2_first, gy_first = together(
-        (feed(False), h2_zero, gy_zero), (gather, h2[rows:]), (gather, gy[1])
+        (feed(False), h2_zero, gy_zero), (gather, h2[1]), (gather, gy[1])
     )
     (down_zero, gh_zero), h2_one, gy_one = together(
         (feed(True), h2_zero, gy_zero, *head_zero),
@@ -1425,7 +1430,9 @@
         narrow[:, :64],
         wide[:, 112:114],
     )
-    return (jnp.stack(output)[None], gx.reshape(1, micro, rows, width), *shares)
+    held = jnp.broadcast_to(output[0][None], (micro, rows, width))
+    held = lax.dynamic_update_slice(held, output[1][None], (1, 0, 0))
+    return (held[None], gx.reshape(1, micro, rows, width), *shares)
 
 
 def solution(mesh):

time: 772 us -> 772 us (level)
  transfers between devices with their start and end apart: 69 -> 69, of which waited for: 25 -> 26; matrix products, arithmetic and copies ran while one was open for 14% -> 13% of each run, Pallas kernels for 42% -> 42%
where the time goes in v5:
time: 772 us; the launch traced here: 761 us
  Pallas kernels  334 us (43%)
  waiting for transfers between devices  153 us (20%)
  local copies, waits for them, and re-layouts  118 us (15%)
  starting transfers between devices  92.8 us (12%)
  blocking collectives  27.7 us (4%)
  other arithmetic  19 us (2%)
  between operations  15.3 us (2%)
    pallas_call x4, Pallas kernels, ffn(): pl.pallas_call(functools.partial(ffn_kernel, pieces, len(carried)), grid=...  154 us
    pallas_call x4, Pallas kernels, together(): job[0](*args)  74.9 us
    ppermute x20, waiting for transfers between devices, by_x(): return lax.ppermute(rows, 'fsdp', X_PAIRS)  35.3 us
    unnamed x142, local copies, waits for them, and re-layouts  33.2 us
    dynamic_update_slice x16, local copies, waits for them, and re-layouts, put(): return lax.dynamic_update_slice(out, part[None], (f, at, 0, 0))  31.2 us
    ppermute x20, waiting for transfers between devices, by_y(): return lax.ppermute(rows, 'fsdp', Y_PAIRS)  30.7 us
    ppermute x20, starting transfers between devices, by_y(): return lax.ppermute(rows, 'fsdp', Y_PAIRS)  23.4 us
    all_to_all x3, waiting for transfers between devices, deal_out(): return lax.all_to_all(pieces, 'dp', split_axis=0, concat_axis=0, tiled=True)  20.9 us
  transfers between devices with their start and end apart: 69, of which 26 were waited for; matrix products, arithmetic and copies ran while one was open for 13% of the time, Pallas kernels for 42%

profile of v5, /device:TPU:0, one launch (start us, length us, event | category | flops | bytes accessed | tf_op | source)
XLA Modules:
  0.0 760.6 jit_solution(5938753531930632803)
XLA Ops:
  16.1 16.1 %all_gather.35 = bf16[8,80,128]{2,1,0:T(8,128)(2,1)S(1)} all-gather(bf16[1,80,128]{2,1,0:T(8,128)(2,1)S(1)} %pad_bitcast_fusion), channel_id=1, replica_groups=mesh['dp'=8,'fsdp'=4] {'dp'}, dimensions={0}, use_global_device_ids=true | all-gather | bytes 184320 | tf_op jit(solution)/shard_map/all_gather | solution.py:919
  32.3 11.6 %all-gather.1 = bf16[32,80,128]{2,1,0:T(8,128)(2,1)S(1)} all-gather(bf16[8,80,128]{2,1,0:T(8,128)(2,1)S(1)} %all_gather.35), channel_id=3, replica_groups=mesh['dp'=8,'fsdp'=4] {'fsdp'}, dimensions={0}, use_global_device_ids=true | all-gather | bytes 819200 | tf_op jit(solution)/shard_map/all_gather | solution.py:920
  80.1 19.2 %all-gather.12.cloned.1.call-done = bf16[2048,512]{1,0:T(8,128)(2,1)} async-done(((bf16[256,512]{1,0:T(8,128)(2,1)}), bf16[2048,512]{1,0:T(8,128)(2,1)}) %all-gather.12.cloned.1.call-update) | async-done | bytes 2097168 | tf_op jit(solution)/shard_map/all_gather | solution.py:942
  104.9 20.2 %all-to-all-done.in_ref = bf16[8,64,2048]{2,1,0:T(8,128)(2,1)} async-done(((bf16[8,64,2048]{2,1,0:T(8,128)(2,1)}), bf16[8,64,2048]{2,1,0:T(8,128)(2,1)}, u32[]{:S(2)}, u32[]{:S(2)}) %all-to-all-start) | async-done | bytes 2097184 | tf_op jit(solution)/shard_map/all_to_all | solution.py:855
  137.6 15.5 %collective-permute-done.2.refs_3_ = bf16[2,256,768]{2,1,0:T(8,128)(2,1)} collective-permute-done((bf16[2,256,768]{2,1,0:T(8,128)(2,1)S(1)}, bf16[2,256,768]{2,1,0:T(8,128)(2,1)}, u32[]{:S(2)}, u32[]{:S(2)}) %collective-permute-start.2) | collective-permute-done | bytes 786464 | tf_op jit(solution)/shard_map/ppermute | solution.py:61
  158.5 18.7 %collective-permute-done.3.refs_4_ = bf16[2,256,768]{2,1,0:T(8,128)(2,1)} collective-permute-done((bf16[2,256,768]{2,1,0:T(8,128)(2,1)}, bf16[2,256,768]{2,1,0:T(8,128)(2,1)}, u32[]{:S(2)}, u32[]{:S(2)}) %collective-permute-start.3) | collective-permute-done | bytes 786464 | tf_op jit(solution)/shard_map/ppermute | solution.py:65
  200.8 10.9 %key_value.1 = (bf16[8,2,256,256]{3,2,1,0:T(8,128)(2,1)S(1)}, bf16[8,2,80,128]{3,2,1,0:T(8,128)(2,1)S(1)}, bf16[8,2,112,256]{3,2,1,0:T(8,128)(2,1)}) custom-call(s32[2]{0:T(128)S(1)} %pad_add_fusion.place_ref, bf16[512,2048]{1,0:T(8,128)(2,1)} %copy-done.23, bf16[512,128]{1,0:T(8,128)(2,1)S(1)} %convolution_convert_fusion.u_ref, ...), custom_call_target="tpu_custom_call" | custom-call | flops 2147483648 | bytes 6291456 | tf_op jit(solution)/shard_map/key_value/pallas_call | solution.py:1017
  230.5 13.4 %query.1 = (bf16[2048,512]{1,0:T(8,128)(2,1)S(1)}, bf16[4096,512]{1,0:T(8,128)(2,1)}) custom-call(s32[2]{0:T(128)S(1)} %pad_add_fusion.place_ref, bf16[512,2048]{1,0:T(8,128)(2,1)} %copy-done.23, bf16[512,128]{1,0:T(8,128)(2,1)S(1)} %convolution_convert_fusion.u_ref, bf16[4,128,512]{2,1,0:T(8,128)(2,1)S(1)} %copy-done.15, f32[32,512]{1,0:T(8,128)S(1)} %copy-done.19, ...), custom_call_target="tpu_custom_call" | custom-call | flops 4294967296 | bytes 16777216 | tf_op jit(solution)/shard_map/query/pallas_call | solution.py:1033
  251.1 19.4 %attend.1 = (bf16[512,2048]{1,0:T(8,128)(2,1)}, bf16[2048,512]{1,0:T(8,128)(2,1)}, f32[8,8,512]{2,1,0:T(8,128)}, bf16[8,2,2,160,128]{4,3,2,1,0:T(8,128)(2,1)}) custom-call(s32[1]{0:T(128)} %bitcast.prev_ref, bf16[8,2,256,256]{3,2,1,0:T(8,128)(2,1)} %copy-done.2, bf16[8,2,112,256]{3,2,1,0:T(8,128)(2,1)} %collective-permute-done.14.msg_ref, ...), custom_call_target="tpu_custom_call" | custom-call | flops 2013265920 | bytes 14680064 | tf_op jit(solution)/shard_map/attend/pallas_call | solution.py:57
  280.9 16.4 %output_projection.1 = (f32[512,2048]{1,0:T(8,128)}, bf16[512,128]{1,0:T(8,128)(2,1)}, f32[512,1]{1,0:T(8,128)}, bf16[256,2048]{1,0:T(8,128)(2,1)}, bf16[256,2048]{1,0:T(8,128)(2,1)}) custom-call(s32[2]{0:T(128)} %copy-done.21, bf16[512,2048]{1,0:T(8,128)(2,1)} %get-tuple-element.678.o_ref, bf16[2048,128]{1,0:T(8,128)(2,1)} %pad.29.ao_ref, ...), custom_call_target="tpu_custom_call" | custom-call | flops 4294967296 | bytes 20971520 | tf_op jit(solution)/shard_map/output_projection/pallas_call | solution.py:57
  298.1 8.0 %broadcast_in_dim.92 = bf16[4,8,256,768]{3,2,1,0:T(8,128)(2,1)} broadcast(bf16[8,256,768]{2,1,0:T(8,128)(2,1)} %bitcast.129), dimensions={1,2,3} | broadcast | bytes 15728640 | tf_op jit(solution)/shard_map/broadcast_in_dim | solution.py:828
  352.9 53.5 %feed_forward.4 = (bf16[1024,2048]{1,0:T(8,128)(2,1)}, bf16[1024,2048]{1,0:T(8,128)(2,1)}) custom-call(bf16[8,256,4608]{2,1,0:T(8,128)(2,1)} %bitcast.171, bf16[8,256,4608]{2,1,0:T(8,128)(2,1)} %bitcast.172, bf16[8,256,4608]{2,1,0:T(8,128)(2,1)} %bitcast.173, bf16[256,2048]{1,0:T(8,128)(2,1)} %get-tuple-element.765.refs_0_, ...), custom_call_target="tpu_custom_call" | custom-call | flops 38654705664 | bytes 62914560 | tf_op jit(solution)/shard_map/feed_forward/pallas_call | solution.py:712
  413.3 24.0 %feed_forward.5 = (bf16[2,256,1024]{2,1,0:T(8,128)(2,1)}, bf16[2,256,1024]{2,1,0:T(8,128)(2,1)}, bf16[2,256,1024]{2,1,0:T(8,128)(2,1)}, bf16[2,256,1024]{2,1,0:T...) custom-call(bf16[8,256,1536]{2,1,0:T(8,128)(2,1)} %bitcast.177, ...), custom_call_target="tpu_custom_call" | custom-call | flops 12884901888 | bytes 37748736 | tf_op jit(solution)/shard_map/feed_forward/pallas_call | solution.py:712
  441.5 52.3 %feed_forward.6 = (bf16[1024,2048]{1,0:T(8,128)(2,1)}, bf16[1024,2048]{1,0:T(8,128)(2,1)}) custom-call(bf16[8,256,4608]{2,1,0:T(8,128)(2,1)} %bitcast.174, bf16[8,256,4608]{2,1,0:T(8,128)(2,1)} %bitcast.175, bf16[8,256,4608]{2,1,0:T(8,128)(2,1)} %bitcast.176, bf16[256,2048]{1,0:T(8,128)(2,1)} %get-tuple-element.839.refs_0_, bf16[256,2048]{1,0:T(8,128)(2,1)} %copy-done.51, ...), custom_call_target="tpu_custom_call" | custom-call | flops 38654705664 | bytes 62914560 | tf_op jit(solution)/shard_map/feed_forward/pallas_call | solution.py:712
  504.1 24.1 %feed_forward.7 = (bf16[2,256,1024]{2,1,0:T(8,128)(2,1)}, bf16[2,256,1024]{2,1,0:T(8,128)(2,1)}, bf16[2,256,1024]{2,1,0:T(8,128)(2,1)}, bf16[2,256,1024]{2,1,0:T...) custom-call(bf16[8,256,1536]{2,1,0:T(8,128)(2,1)} %bitcast.180, ...), custom_call_target="tpu_custom_call" | custom-call | flops 12884901888 | bytes 37748736 | tf_op jit(solution)/shard_map/feed_forward/pallas_call | solution.py:712
  536.7 5.4 mid_back.2
  542.1 10.3 %collective-permute-done.43.from_x.refs_2_ = bf16[2,256,1024]{2,1,0:T(8,128)(2,1)S(1)} collective-permute-done((bf16[2,256,1024]{2,1,0:T(8,128)(2,1)}, bf16[2,256,1024]{2,1,0:T(8,128)(2,1)S(1)}, u32[]{:S(2)}, u32[]{:S(2)}) %collective-permute-start.43) | collective-permute-done | bytes 1048608 | tf_op jit(solution)/shard_map/ppermute | solution.py:61
  559.3 8.8 %collective-permute-done.45.refs_3_ = bf16[256,1024]{1,0:T(8,128)(2,1)S(1)} collective-permute-done((bf16[256,1024]{1,0:T(8,128)(2,1)}, bf16[256,1024]{1,0:T(8,128)(2,1)S(1)}, u32[]{:S(2)}, u32[]{:S(2)}) %collective-permute-start.45) | collective-permute-done | bytes 524320 | tf_op jit(solution)/shard_map/ppermute | solution.py:65
  580.2 10.3 %output_projection_back.1 = (bf16[2048,512]{1,0:T(8,128)(2,1)}, f32[16,2048]{1,0:T(8,128)}) custom-call(bf16[512,2048]{1,0:T(8,128)(2,1)} %get-tuple-element.946.gb_ref, bf16[4,8,256,512]{3,2,1,0:T(8,128)(2,1)} %bitcast_dynamic-update-slice_fusion.13.w_ref, bf16[2048,128]{1,0:T(8,128)(2,1)} %pad.29.ao_ref, bf16[512,128]{1,0:T(8,128)(2,1)} %get-tuple-element.948.guo_ref, ...), custom_call_target="tpu_custom_call" | custom-call | flops 4294967296 | bytes 12582912 | tf_op jit(solution)/shard_map/output_projection_back/pallas_call | solution.py:1281
  600.6 26.7 %attend_back.1 = (bf16[4,512,512]{2,1,0:T(8,128)(2,1)}, f32[8,256,64]{2,1,0:T(8,128)}, f32[8,2,256,256]{3,2,1,0:T(8,128)}, f32[8,2,2,160,128]{4,3,2,1,0:T(8,128)...) custom-call(s32[1]{0:T(128)} %bitcast.prev_ref, bf16[8,2,256,256]{3,2,1,0:T(8,128)(2,1)} %copy-done.2, ...), custom_call_target="tpu_custom_call" | custom-call | flops 6039797760 | bytes 25165824 | tf_op jit(solution)/shard_map/attend_back/pallas_call | solution.py:57
  643.6 12.4 %query_input_gradient.1 = (f32[512,2048]{1,0:T(8,128)}, f32[512,128]{1,0:T(8,128)}, f32[32,2048]{1,0:T(8,128)}) custom-call(bf16[4,512,512]{2,1,0:T(8,128)(2,1)} %get-tuple-element.1005.gq_ref, bf16[4,8,256,768]{3,2,1,0:T(8,128)(2,1)} %bitcast_dynamic-update-slice_fusion.9.wq_ref.wkv_ref, bf16[512,128]{1,0:T(8,128)(2,1)} %copy-done.13, ...), custom_call_target="tpu_custom_call" | custom-call | flops 4294967296 | bytes 16777216 | tf_op jit(solution)/shard_map/query_input_gradient/pallas_call | solution.py:57
  656.0 18.1 %collective-permute-done.53.refs_1_ = bf16[8,2,80,128]{3,2,1,0:T(8,128)(2,1)} collective-permute-done((bf16[8,2,80,128]{3,2,1,0:T(8,128)(2,1)}, bf16[8,2,80,128]{3,2,1,0:T(8,128)(2,1)}, u32[]{:S(2)}, u32[]{:S(2)}) %collective-permute-start.53) | collective-permute-done | bytes 327712 | tf_op jit(solution)/shard_map/ppermute | solution.py:847
  679.8 11.5 %key_value_back.1 = (bf16[4,512,256]{2,1,0:T(8,128)(2,1)}, f32[4,128,64]{2,1,0:T(8,128)}, bf16[512,128]{1,0:T(8,128)(2,1)}, f32[4,32,256]{2,1,0:T(8,128)}, f32[32,2048]{1,0:T(8,128)}) custom-call(f32[8,2,256,256]{3,2,1,0:T(8,128)} %get-tuple-element.1032.gn_ref, bf16[8,2,144,256]{3,2,1,0:T(8,128)(2,1)} %copy-done.42, bf16[8,2,256,256]{3,2,1,0:T(8,128)(2,1)} %copy-done.2, ...), custom_call_target="tpu_custom_call" | custom-call | flops 67108864 | bytes 8388608 | tf_op jit(solution)/shard_map/key_value_back/pallas_call | solution.py:1391
  691.4 13.4 %input_gradient.1 = (bf16[512,2048]{1,0:T(8,128)(2,1)}, f32[1,2048]{1,0:T(1,128)}) custom-call(f32[512,2048]{1,0:T(8,128)} %get-tuple-element.1031.part_ref, bf16[4,512,256]{2,1,0:T(8,128)(2,1)} %get-tuple-element.1039.gkv_ref, bf16[4,8,256,768]{3,2,1,0:T(8,128)(2,1)} %bitcast_dynamic-update-slice_fusion.9.wq_ref.wkv_ref, ...), custom_call_target="tpu_custom_call" | custom-call | flops 2147483648 | bytes 31457280 | tf_op jit(solution)/shard_map/input_gradient/pallas_call | solution.py:1395
  (402 shorter events, 305.1 us)
Async XLA Ops:
  7.2 44.9 %all-gather.10.cloned.1.call-start = ((), (), s32[]{:S(2)}) async-start(), calls=%async_computation.6 | async-start | bytes 3538944 | tf_op jit(solution)/shard_map/all_gather | solution.py:941
  9.4 90.0 %all-gather.12.cloned.1.call-start = ((), (), s32[]{:S(2)}) async-start(), calls=%async_computation.7 | async-start | bytes 2359296 | tf_op jit(solution)/shard_map/all_gather | solution.py:942
  54.8 70.3 %all-to-all-start = ((bf16[8,64,2048]{2,1,0:T(8,128)(2,1)}), bf16[8,64,2048]{2,1,0:T(8,128)(2,1)}, u32[]{:S(2)}, u32[]{:S(2)}) async-start(bf16[8,64,2048]{2,1,0:T(8,128)(2,1)} %bitcast.154), calls=%async_computation | async-start | bytes 4194304 | tf_op jit(solution)/shard_map/all_to_all | solution.py:855
  66.8 36.9 %collective-permute-start = (bf16[4,256,768]{2,1,0:T(8,128)(2,1)}, bf16[4,256,768]{2,1,0:T(8,128)(2,1)S(1)}, u32[]{:S(2)}, u32[]{:S(2)}) collective-permute-start(bf16[4,256,768]{2,1,0:T(8,128)(2,1)} %constant_dynamic-slice_fusion.3), channel_id=1, source_target_pairs={{0,1},{1,0},{2,3},{3,2},{4,5},{5,4},{6,7},{7,6},{8,9},{9,8},{10,11... | collective-permute-start | bytes 4718600 | tf_op jit(solution)/shard_map/ppermute | solution.py:61
  68.3 36.6 %collective-permute-start.1 = (bf16[4,256,768]{2,1,0:T(8,128)(2,1)}, bf16[4,256,768]{2,1,0:T(8,128)(2,1)S(1)}, u32[]{:S(2)}, u32[]{:S(2)}) collective-permute-start(bf16[4,256,768]{2,1,0:T(8,128)(2,1)} %constant_dynamic-slice_fusion.3), channel_id=1, source_target_pairs={{0,2},{1,3},{2,0},{3,1},{4,6},{5,7},{6,4},{7,5},{8,10},{9,11},{10,... | collective-permute-start | bytes 4718600 | tf_op jit(solution)/shard_map/ppermute | solution.py:65
  128.1 53.4 %all-to-all-start.1 = ((bf16[8,64,2048]{2,1,0:T(8,128)(2,1)}), bf16[8,64,2048]{2,1,0:T(8,128)(2,1)}, u32[]{:S(2)}, u32[]{:S(2)}) async-start(bf16[8,64,2048]{2,1,0:T(8,128)(2,1)} %reorder.3), calls=%async_computation.1 | async-start | bytes 4194304 | tf_op jit(solution)/shard_map/all_to_all | solution.py:876
  132.5 220.4 %all-gather.16.cloned.1.call-start = ((), (), s32[]{:S(2)}) async-start(), calls=%async_computation.9 | async-start | bytes 21233664 | tf_op jit(solution)/shard_map/all_gather | solution.py:1003
  134.1 43.1 %collective-permute-start.4 = (bf16[4,256,768]{2,1,0:T(8,128)(2,1)S(1)}, bf16[4,256,768]{2,1,0:T(8,128)(2,1)}, u32[]{:S(2)}, u32[]{:S(2)}) collective-permute-start(bf16[4,256,768]{2,1,0:T(8,128)(2,1)S(1)} %collective-permute-done.refs_1_), channel_id=1, source_target_pairs={{0,4},{4,0},{8,12},{12,8},{16,20},{20,16},{24,28},{28,24},{1,5},{5... | collective-permute-start | bytes 4718600 | tf_op jit(solution)/shard_map/ppermute | solution.py:787
  134.2 43.0 %collective-permute-start.5 = (bf16[4,256,768]{2,1,0:T(8,128)(2,1)S(1)}, bf16[4,256,768]{2,1,0:T(8,128)(2,1)}, u32[]{:S(2)}, u32[]{:S(2)}) collective-permute-start(bf16[4,256,768]{2,1,0:T(8,128)(2,1)S(1)} %collective-permute-done.1.refs_2_), channel_id=1, source_target_pairs={{0,4},{4,0},{8,12},{12,8},{16,20},{20,16},{24,28},{28,24},{1,5},{5... | collective-permute-start | bytes 4718600 | tf_op jit(solution)/shard_map/ppermute | solution.py:787
  134.6 42.6 %collective-permute-start.6 = (bf16[4,256,512]{2,1,0:T(8,128)(2,1)}, bf16[4,256,512]{2,1,0:T(8,128)(2,1)}, u32[]{:S(2)}, u32[]{:S(2)}) collective-permute-start(bf16[4,256,512]{2,1,0:T(8,128)(2,1)} %constant_dynamic-slice_fusion.2), channel_id=1, source_target_pairs={{0,1},{1,0},{2,3},{3,2},{4,5},{5,4},{6,7},{7,6},{8,9},{9,8},{10,11... | collective-permute-start | bytes 3145736 | tf_op jit(solution)/shard_map/ppermute | solution.py:61
  135.2 42.0 %collective-permute-start.7 = (bf16[4,256,512]{2,1,0:T(8,128)(2,1)}, bf16[4,256,512]{2,1,0:T(8,128)(2,1)}, u32[]{:S(2)}, u32[]{:S(2)}) collective-permute-start(bf16[4,256,512]{2,1,0:T(8,128)(2,1)} %constant_dynamic-slice_fusion.2), channel_id=1, source_target_pairs={{0,2},{1,3},{2,0},{3,1},{4,6},{5,7},{6,4},{7,5},{8,10},{9,11},{10,... | collective-permute-start | bytes 3145736 | tf_op jit(solution)/shard_map/ppermute | solution.py:65
  181.6 231.8 %all-gather.14.cloned.1.call-start = ((), (), s32[]{:S(2)}) async-start(), calls=%async_computation.8 | async-start | bytes 7077888 | tf_op jit(solution)/shard_map/all_gather | solution.py:1064
  348.9 57.6 %collective-permute-start.27 = (bf16[256,2048]{1,0:T(8,128)(2,1)}, bf16[256,2048]{1,0:T(8,128)(2,1)S(1)}, u32[]{:S(2)}, u32[]{:S(2)}) collective-permute-start(bf16[256,2048]{1,0:T(8,128)(2,1)} %get-tuple-element.839.refs_0_), channel_id=1, source_target_pairs={{0,1},{1,0},{2,3},{3,2},{4,5},{5,4},{6,7},{7,6},{8,9},{9,8},{10,11... | collective-permute-start | bytes 3145736 | tf_op jit(solution)/shard_map/ppermute | solution.py:61
  349.0 57.5 %collective-permute-start.28 = (bf16[256,2048]{1,0:T(8,128)(2,1)}, bf16[256,2048]{1,0:T(8,128)(2,1)S(1)}, u32[]{:S(2)}, u32[]{:S(2)}) collective-permute-start(bf16[256,2048]{1,0:T(8,128)(2,1)} %get-tuple-element.839.refs_0_), channel_id=1, source_target_pairs={{0,2},{1,3},{2,0},{3,1},{4,6},{5,7},{6,4},{7,5},{8,10},{9,11},{10,... | collective-permute-start | bytes 3145736 | tf_op jit(solution)/shard_map/ppermute | solution.py:65
  350.3 56.2 %collective-permute-start.29 = (bf16[256,2048]{1,0:T(8,128)(2,1)S(1)}, bf16[256,2048]{1,0:T(8,128)(2,1)}, u32[]{:S(2)}, u32[]{:S(2)}) collective-permute-start(bf16[256,2048]{1,0:T(8,128)(2,1)S(1)} %copy-done.31), channel_id=1, source_target_pairs={{0,1},{1,0},{2,3},{3,2},{4,5},{5,4},{6,7},{7,6},{8,9},{9,8},{10,11... | collective-permute-start | bytes 3145736 | tf_op jit(solution)/shard_map/ppermute | solution.py:61
  351.8 54.7 %collective-permute-start.30 = (bf16[256,2048]{1,0:T(8,128)(2,1)S(1)}, bf16[256,2048]{1,0:T(8,128)(2,1)}, u32[]{:S(2)}, u32[]{:S(2)}) collective-permute-start(bf16[256,2048]{1,0:T(8,128)(2,1)S(1)} %copy-done.31), channel_id=1, source_target_pairs={{0,2},{1,3},{2,0},{3,1},{4,6},{5,7},{6,4},{7,5},{8,10},{9,11},{10,... | collective-permute-start | bytes 3145736 | tf_op jit(solution)/shard_map/ppermute | solution.py:65
  437.4 56.4 %collective-permute-start.35 = (bf16[2,256,1024]{2,1,0:T(8,128)(2,1)}, bf16[2,256,1024]{2,1,0:T(8,128)(2,1)S(1)}, u32[]{:S(2)}, u32[]{:S(2)}) collective-permute-start(bf16[2,256,1024]{2,1,0:T(8,128)(2,1)} %get-tuple-element.823), channel_id=1, source_target_pairs={{0,1},{1,0},{2,3},{3,2},{4,5},{5,4},{6,7},{7,6},{8,9},{9,8},{10,11... | collective-permute-start | bytes 3145736 | tf_op jit(solution)/shard_map/ppermute | solution.py:61
  438.9 54.9 %collective-permute-start.36 = (bf16[2,256,1024]{2,1,0:T(8,128)(2,1)}, bf16[2,256,1024]{2,1,0:T(8,128)(2,1)S(1)}, u32[]{:S(2)}, u32[]{:S(2)}) collective-permute-start(bf16[2,256,1024]{2,1,0:T(8,128)(2,1)} %get-tuple-element.824), channel_id=1, source_target_pairs={{0,2},{1,3},{2,0},{3,1},{4,6},{5,7},{6,4},{7,5},{8,10},{9,11},{10,... | collective-permute-start | bytes 3145736 | tf_op jit(solution)/shard_map/ppermute | solution.py:65
  440.4 53.4 %collective-permute-start.37 = (bf16[2,256,1024]{2,1,0:T(8,128)(2,1)}, bf16[2,256,1024]{2,1,0:T(8,128)(2,1)S(1)}, u32[]{:S(2)}, u32[]{:S(2)}) collective-permute-start(bf16[2,256,1024]{2,1,0:T(8,128)(2,1)} %get-tuple-element.827), channel_id=1, source_target_pairs={{0,1},{1,0},{2,3},{3,2},{4,5},{5,4},{6,7},{7,6},{8,9},{9,8},{10,11... | collective-permute-start | bytes 3145736 | tf_op jit(solution)/shard_map/ppermute | solution.py:61
  440.9 52.9 %collective-permute-start.38 = (bf16[2,256,1024]{2,1,0:T(8,128)(2,1)}, bf16[2,256,1024]{2,1,0:T(8,128)(2,1)}, u32[]{:S(2)}, u32[]{:S(2)}) collective-permute-start(bf16[2,256,1024]{2,1,0:T(8,128)(2,1)} %get-tuple-element.828), channel_id=1, source_target_pairs={{0,2},{1,3},{2,0},{3,1},{4,6},{5,7},{6,4},{7,5},{8,10},{9,11},{10,... | collective-permute-start | bytes 3145736 | tf_op jit(solution)/shard_map/ppermute | solution.py:65
  591.8 35.6 %all-to-all-start.2 = ((bf16[8,32,2048]{2,1,0:T(8,128)(2,1)}), bf16[8,32,2048]{2,1,0:T(8,128)(2,1)S(1)}, u32[]{:S(2)}, u32[]{:S(2)}) async-start(bf16[8,32,2048]{2,1,0:T(8,128)(2,1)} %bitcast.39), calls=%async_computation.2 | async-start | bytes 2097152 | tf_op jit(solution)/shard_map/all_to_all | solution.py:855
  630.8 43.3 %all-to-all-start.3 = ((bf16[8,32,2048]{2,1,0:T(8,128)(2,1)}), bf16[8,32,2048]{2,1,0:T(8,128)(2,1)S(1)}, u32[]{:S(2)}, u32[]{:S(2)}) async-start(bf16[8,32,2048]{2,1,0:T(8,128)(2,1)} %reorder.4), calls=%async_computation.3 | async-start | bytes 2097152 | tf_op jit(solution)/shard_map/all_to_all | solution.py:876
  635.9 38.2 %collective-permute-start.51 = (bf16[8,2,144,256]{3,2,1,0:T(8,128)(2,1)}, bf16[8,2,144,256]{3,2,1,0:T(8,128)(2,1)S(1)}, u32[]{:S(2)}, u32[]{:S(2)}) collective-permute-start(bf16[8,2,144,256]{3,2,1,0:T(8,128)(2,1)} %get-tuple-element.1012), channel_id=1, source_target_pairs={{1,0},{2,1},{3,2},{5,4},{6,5},{7,6},{9,8},{10,9},{11,10},{13,12},{... | collective-permute-start | bytes 3538952 | tf_op jit(solution)/shard_map/ppermute | solution.py:1319
  638.4 35.6 %collective-permute-start.53 = (bf16[8,2,80,128]{3,2,1,0:T(8,128)(2,1)}, bf16[8,2,80,128]{3,2,1,0:T(8,128)(2,1)}, u32[]{:S(2)}, u32[]{:S(2)}) collective-permute-start(bf16[8,2,80,128]{3,2,1,0:T(8,128)(2,1)} %get-tuple-element.1013), channel_id=1, source_target_pairs={{3,0},{7,4},{11,8},{15,12},{19,16},{23,20},{27,24},{31,28}} | collective-permute-start | bytes 983048 | tf_op jit(solution)/shard_map/ppermute | solution.py:847
  (106 other events, 1906.6 us)
Sparse Core Ops, SparseCore 0:
  10.2 41.8 all-gather.9
  53.7 45.5 all-gather.11
  181.7 167.1 all-gather.15
  350.3 62.9 all-gather.13
